TPU v7x, 32 devices: a whole 2x2x4 slice. The times are simulated.
32 devices in a mesh: face: 4 (over y, core), blk: 8 (over z, x).
Axes of the slice: x: 2, y: 2, z: 4, core: 2. Of those that a mesh axis runs over, the one named last changes fastest.
Arguments:
- isotope_ratios: float32 [3, 32, 64, 1024], P(None, None, 'face', 'blk'), may hold values from 2 to 4
- advecting_velocity: float32 [2, 32, 64, 1024], P(None, None, 'face', 'blk'), may hold values from -1 to 1
- metric_scaling: float32 [64, 1024], P('face', 'blk'), may hold values from 0.5 to 2
- thermal_state: float32 [4, 32, 9216], P('face', None, 'blk'), may hold values from 255 to 300
- outgoing_site_order: int32 [4, 9216], P('face', 'blk'), may hold values from 0 to 1151, as said below
- daytime_indicator: int32 [4, 9216], P('face', 'blk'), may hold values from 0 to 1, as said below
Outputs:
- new_tracers: float32 [3, 32, 64, 1024], P(None, None, 'face', 'blk')
- phys_tracers: float32 [4, 3, 32, 9216], P('face', None, None, 'blk')
Inputs may be any that keep to these rules, and one draw needn't show every extreme that they name: `outgoing_site_order`: the 1152 entries that belong to one device are a permutation of 0 .. 1151; the device's entries k of its block name the local column it sends in position k, to blk peer k // 144. `daytime_indicator`: each device sends the same number of day columns to every peer along blk, and every physics batch (the 1152 columns one device receives) holds exactly 576 day columns.
All inputs are finite; a program needn't handle non-finite values.
Results may differ from a plain program's by a relative error of at most 0.0003.
Values sent between devices are 32-bit elements; how exact they have to be, the bound alone decides.
No kernel may reach another device: no remote copies, remote signals or barrier semaphores. Data moves between devices by JAX's collectives and lax.ppermute only.
A program may use at most 64 MiB of HBM per device.

v0:
```python
import math

import jax
import jax.numpy as jnp
import numpy as np
from jax import lax
from jax.sharding import PartitionSpec as P

time_step = 0.006
absorb_coef = 0.02
heat_gain = 100.0
sat_base = 3.0
clausius = 0.07
ref_temp = 280.0


def extended(x, sides, width):
    for axis, dim in sides:
        devices, length = (lax.axis_size(axis), x.shape[dim])
        up = [(i, (i + 1) % devices) for i in range(devices)]
        down = [(j, i) for i, j in up]
        last = lax.slice_in_dim(x, length - width, length, axis=dim)
        initial = lax.slice_in_dim(x, 0, width, axis=dim)
        before = lax.ppermute(last, axis, up)
        after = lax.ppermute(initial, axis, down)
        x = jnp.concatenate([before, x, after], axis=dim)
    return x


def gll_tables():
    inv_root = 1.0 / math.sqrt(5.0)
    gll_nodes = np.array([-1.0, -inv_root, inv_root, 1.0])
    legendre = (5.0 * gll_nodes**3 - 3.0 * gll_nodes) / 2.0
    deriv_matrix = np.zeros((4, 4))
    for row_index in range(4):
        for col_index in range(4):
            if row_index != col_index:
                deriv_matrix[row_index, col_index] = legendre[row_index] / (
                    legendre[col_index] * (gll_nodes[row_index] - gll_nodes[col_index])
                )
    deriv_matrix[0, 0] = -3.0
    deriv_matrix[3, 3] = 3.0
    weights = np.array([1.0, 5.0, 5.0, 1.0]) / 6.0
    return (deriv_matrix, weights)


def add_partners(padded, axis_dim):
    span_len = padded.shape[axis_dim] - 2
    centre = lax.slice_in_dim(padded, 1, span_len + 1, axis=axis_dim)
    following = lax.slice_in_dim(padded, 2, span_len + 2, axis=axis_dim)
    before = lax.slice_in_dim(padded, 0, span_len, axis=axis_dim)
    bcast_shape = [1] * padded.ndim
    bcast_shape[axis_dim] = span_len
    position = (jnp.arange(span_len) % 4).reshape(bcast_shape)
    return centre + jnp.where(position == 3, following, 0.0) + jnp.where(position == 0, before, 0.0)


def radiative_warming(vapour):
    depth = jnp.cumsum(absorb_coef * vapour, axis=0)
    return heat_gain * absorb_coef * vapour * jnp.exp(-depth)


def condense(vapour, heavy, deuter, warmed_profiles):
    saturation = sat_base * jnp.exp(clausius * (warmed_profiles - ref_temp))
    remain = jnp.minimum(vapour, saturation)
    log_ratio = jnp.log(remain / vapour)
    inverse = 1.0 / warmed_profiles
    alpha_heavy = jnp.exp(1137.0 * inverse * inverse - 0.4156 * inverse - 0.0020667)
    alpha_deut = jnp.exp(24844.0 * inverse * inverse - 76.248 * inverse + 0.052612)
    return jnp.stack(
        [remain, heavy * jnp.exp(alpha_heavy * log_ratio), deuter * jnp.exp(alpha_deut * log_ratio)]
    )


def on_device(
    isotope_ratios,
    advecting_velocity,
    metric_scaling,
    thermal_state,
    outgoing_site_order,
    daytime_indicator,
):
    deriv_np, weight_np = gll_tables()
    size_x, size_y = metric_scaling.shape
    layer_total = isotope_ratios.shape[1]
    sites_per_processor = outgoing_site_order.shape[1]
    block_width = math.gcd(size_y, 128)
    kron_first = jnp.asarray(np.kron(np.eye(size_x // 4), deriv_np), jnp.float32)
    kron_second = jnp.asarray(np.kron(np.eye(block_width // 4), deriv_np), jnp.float32)
    outer_weight = np.outer(np.tile(weight_np, size_x // 4), np.tile(weight_np, size_y // 4))
    node_mass = jnp.asarray(outer_weight, jnp.float32) * metric_scaling
    flux_x = metric_scaling * advecting_velocity[0] * isotope_ratios
    flux_y = metric_scaling * advecting_velocity[1] * isotope_ratios
    grad_x = jnp.einsum("ij,sljy->sliy", kron_first, flux_x, precision=lax.Precision.HIGHEST)
    shaped_y = flux_y.reshape(3, layer_total, size_x, size_y // block_width, block_width)
    grad_y = jnp.einsum("slxab,cb->slxac", shaped_y, kron_second, precision=lax.Precision.HIGHEST)
    tendency = -(grad_x + grad_y.reshape(3, layer_total, size_x, size_y)) / metric_scaling
    payload = jnp.concatenate(
        [(node_mass * tendency).reshape(3 * layer_total, size_x, size_y), node_mass[None]], axis=0
    )
    padded = extended(payload, (("face", 1), ("blk", 2)), 1)
    summed = add_partners(add_partners(padded, 1), 2)
    ratio = summed[: 3 * layer_total] / summed[3 * layer_total]
    new_tracers = isotope_ratios + time_step * ratio.reshape(3, layer_total, size_x, size_y)
    shaped = new_tracers.reshape(3, layer_total, size_x // 4, 4, size_y // 4, 4)[:, :, :, :3, :, :3]
    profile_list = shaped.reshape(3, layer_total, sites_per_processor)
    send_perm = outgoing_site_order[0]
    profile_warmth = thermal_state[0]
    state = jnp.concatenate(
        [profile_list.reshape(3 * layer_total, sites_per_processor), profile_warmth], axis=0
    )
    moved_state, moved_mask = (
        lax.all_to_all(state[:, send_perm], "blk", split_axis=1, concat_axis=1, tiled=True),
        lax.all_to_all(
            daytime_indicator[:, send_perm], "blk", split_axis=1, concat_axis=1, tiled=True
        ),
    )
    vapour = moved_state[0:layer_total]
    heavy = moved_state[layer_total : 2 * layer_total]
    deuter = moved_state[2 * layer_total : 3 * layer_total]
    moved_temps = moved_state[3 * layer_total :]
    warmed_profiles = moved_temps + jnp.where(
        moved_mask[0][None, :] == 1, radiative_warming(vapour), 0.0
    )
    result = condense(vapour, heavy, deuter, warmed_profiles)
    return (new_tracers, result[None])


def solution(mesh):
    placed = (
        P(None, None, "face", "blk"),
        P(None, None, "face", "blk"),
        P("face", "blk"),
        P("face", None, "blk"),
        P("face", "blk"),
        P("face", "blk"),
    )
    return jax.shard_map(
        on_device,
        mesh=mesh,
        in_specs=placed,
        out_specs=(P(None, None, "face", "blk"), P("face", None, None, "blk")),
        check_vma=False,
    )
```

profile of v0, /device:TPU:0, one launch (start us, length us, event | category | flops | bytes accessed | tf_op | source)
XLA Modules:
  0.0 65.6 jit_solution(17761344773586707527)
XLA Ops:
  0.7 1.1 %multiply_bitcast_fusion = (f32[32,16,128]{2,1,0:T(8,128)S(1)}, f32[32,16,128]{2,1,0:T(8,128)S(1)}) fusion(f32[2,32,16,128]{3,2,1,0:T(8,128)} %param.10, f32[16,128]{1,0:T(8,128)} %param.11), kind=kLoop, calls=%fused_computation.26 | loop fusion | flops 131072 | bytes 1056768 | tf_op jit(solution)/shard_map/mul | solution.py:93
  1.8 0.7 %mul.222 = f32[16,128]{1,0:T(8,128)S(1)} multiply(f32[16,128]{1,0:T(8,128)} %constant.75.clone, f32[16,128]{1,0:T(8,128)} %param.11) | non-fusion elementwise | flops 2048 | bytes 24576 | tf_op jit(solution)/shard_map/mul | solution.py:91
  2.6 1.5 %convolution_bitcast_fusion = f32[3,32,16,128]{3,2,1,0:T(8,128)S(1)} fusion(f32[16,16,1,1]{1,0,3,2:T(8,128)} %constant.79, f32[3,32,16,128]{3,2,1,0:T(8,128)S(1)} %copy-done.1, f32[32,16,128]{2,1,0:T(8,128)S(1)} %get-tuple-element.16), kind=kOutput, calls=%fused_computation.9 | convolution fusion | flops 37945344 | bytes 1836032 | tf_op jit(solution)/shard_map/ij,sljy->sliy/dot_general | solution.py:94
  4.1 0.8 %fusion.4 = f32[3,32,16,128]{3,2,1,0:T(8,128)S(1)} fusion(f32[3,32,16,128]{3,2,1,0:T(8,128)S(1)} %convolution_bitcast_fusion, f32[128,128,1,1]{1,0,3,2:T(8,128)S(1)} %copy-done.9, f32[3,32,16,128]{3,2,1,0:T(8,128)S(1)} %copy-done.1, f32[16,128]{1,0:T(8,128)S(1)} %copy-done.5, f32[32,16,128]{2,1,0:T(8,128)S(1)} %get-tuple-element.15, f32[16,128]{1,0:T(8,128)S(1)} %mul.222), kind=kOutput, calls=%fused_computation.11 | convolution fusion | flops 302972928 | bytes 2703360 | tf_op jit(solution)/shard_map/slxab,cb->slxac/dot_general | solution.py:96
  4.9 0.1 pad_maximum_fusion.4
  5.0 0.5 collective-permute-start
  5.5 2.0 %collective-permute-start.1 = (f32[97,1,128]{2,1,0:T(1,128)S(1)}, f32[97,1,128]{2,1,0:T(1,128)S(1)}, u32[]{:S(2)}, u32[]{:S(2)}) collective-permute-start(f32[97,1,128]{2,1,0:T(1,128)S(1)} %get-tuple-element.9), channel_id=1, source_target_pairs={{8,0},{16,8},{24,16},{0,24},{9,1},{17,9},{25,17},{1,25},{10,2},{18... | collective-permute-start | bytes 149000 | tf_op jit(solution)/shard_map/ppermute | solution.py:25
  7.6 6.5 %gather_fusion.1 = s32[1152]{0:T(1024)S(1)} fusion(s32[1152]{0:T(1024)S(1)} %reduce.1, s32[2048]{0:T(1024)S(1)} %pad_clamp_fusion), kind=kCustom, calls=%fused_computation.1 | custom fusion | bytes 13824 | tf_op jit(solution)/shard_map/gather | solution.py:115
  14.1 0.7 %all_to_all.14 = s32[1,8,144]{2,0,1:T(1,128)} reshape(s32[1152]{0:T(1024)S(1)} %gather_fusion.1) | data formatting | bytes 9216 | tf_op jit(solution)/shard_map/all_to_all | solution.py:114
  14.8 6.5 %all-to-all-start.1 = ((s32[1,8,144]{2,0,1:T(1,128)}), s32[1,8,144]{2,0,1:T(1,128)}, u32[]{:S(2)}, u32[]{:S(2)}) async-start(s32[1,8,144]{2,0,1:T(1,128)} %all_to_all.14), calls=%async_computation.1 | async-start | bytes 16384 | tf_op jit(solution)/shard_map/all_to_all | solution.py:114
  21.3 0.5 broadcast_compare_fusion.2
  21.9 0.2 pad_maximum_fusion.1
  22.1 0.4 fusion.28
  22.4 0.4 copy.35
  22.8 2.1 %collective-permute-start.2 = (f32[97,18,1]{0,2,1:T(1,128)S(1)}, f32[97,18,1]{0,2,1:T(1,128)S(1)}, u32[]{:S(2)}, u32[]{:S(2)}) collective-permute-start(f32[97,18,1]{0,2,1:T(1,128)S(1)} %copy.35), channel_id=1, source_target_pairs={{0,1},{1,2},{2,3},{3,4},{4,5},{5,6},{6,7},{7,0},{8,9},{9,10},{10,1... | collective-permute-start | bytes 20960 | tf_op jit(solution)/shard_map/ppermute | solution.py:24
  24.9 0.4 copy.36
  25.2 2.7 %collective-permute-start.3 = (f32[97,18,1]{0,2,1:T(1,128)S(1)}, f32[97,18,1]{0,2,1:T(1,128)S(1)}, u32[]{:S(2)}, u32[]{:S(2)}) collective-permute-start(f32[97,18,1]{0,2,1:T(1,128)S(1)} %copy.36), channel_id=1, source_target_pairs={{1,0},{2,1},{3,2},{4,3},{5,4},{6,5},{7,6},{0,7},{9,8},{10,9},{11,1... | collective-permute-start | bytes 20960 | tf_op jit(solution)/shard_map/ppermute | solution.py:25
  28.0 1.1 %copy.41 = f32[1,32,1152]{1,2,0:T(8,128)} copy(f32[1,32,1152]{2,1,0:T(8,128)S(1)} %copy-done.4) | data formatting | bytes 294912 | tf_op args[3]
  29.0 0.2 collective-permute-done.2
  29.2 0.5 copy.37
  29.7 0.5 copy.38
  30.3 1.5 %pad_maximum_fusion = f32[97,18,130]{2,1,0:T(8,128)S(1)} fusion(f32[97,18,1]{2,1,0:T(8,128)S(1)} %copy.38, f32[97,1,128]{2,1,0:T(1,128)S(1)} %collective-permute-done.1, f32[1,16,128]{2,1,0:T(8,128)S(1)} %bitcast.55, f32[96,16,128]{2,1,0:T(8,128)S(1)} %bitcast.45, f32[97,1,128]{2,1,0:T(1,128)S(1)} %collective-permute-done, f32[97,18,1]{2,1,0:T(8,128)S(1)} %copy.37), kind=kLoop, calls=%fused_computation.2 | loop fusion | flops 1134900 | bytes 1815840 | tf_op jit(solution)/shard_map/concatenate | solution.py:26
  31.8 0.5 fusion
  32.3 0.5 fusion.5
  32.8 0.1 fusion.7
  32.8 1.0 %copy-done.2 = f32[3,32,16,128]{3,2,1,0:T(8,128)S(1)} copy-done((f32[3,32,16,128]{3,2,1,0:T(8,128)S(1)}, f32[3,32,16,128]{3,2,1,0:T(8,128)}, u32[]{:S(2)}) %copy-start.2) | copy-done | bytes 786456
  33.9 1.0 %add.109 = f32[3,32,16,128]{3,2,1,0:T(8,128)} add(f32[3,32,16,128]{3,2,1,0:T(8,128)S(1)} %copy-done.2, f32[3,32,16,128]{3,2,1,0:T(8,128)S(1)} %bitcast.46) | non-fusion elementwise | flops 196608 | bytes 2359296 | tf_op jit(solution)/shard_map/add | solution.py:104
  34.8 2.0 %copy.39 = f32[3,32,16,128]{1,3,2,0:T(8,128)S(1)} copy(f32[3,32,16,128]{3,2,1,0:T(8,128)} %add.109) | data formatting | bytes 1572864 | tf_op jit(solution)/shard_map/add | solution.py:104
  36.8 0.2 slice.106
  37.1 1.2 %copy.40 = f32[3,32,4,3,32,3]{1,0,5,4,3,2:T(4,128)S(1)} copy(f32[3,32,4,3,32,3]{1,5,4,3,2,0:T(4,128)S(1)} %slice.106) | data formatting | bytes 884736 | tf_op jit(solution)/shard_map/slice | solution.py:105
  38.3 0.9 %reshape_reshape.3 = f32[96,1152]{0,1:T(8,128)S(1)} reshape(f32[3,32,4,3,32,3]{1,0,5,4,3,2:T(4,128)S(1)} %copy.40) | data formatting | bytes 884736 | tf_op jit(solution)/shard_map/reshape;reshape | solution.py:110
  39.2 0.1 copy-done.3
  39.4 0.2 pad_maximum_fusion.2
  39.6 3.1 %gather_fusion = f32[1152,128]{1,0:T(8,128)} fusion(f32[128,1152]{0,1:T(8,128)S(1)} %pad_maximum_fusion.2, s32[2048]{0:T(1024)S(1)} %pad_clamp_fusion), kind=kCustom, calls=%fused_computation | custom fusion | bytes 1184256 | tf_op jit(solution)/shard_map/gather | solution.py:113
  42.7 5.9 %all-to-all-start = ((f32[128,8,144]{0,2,1:T(8,128)}), f32[128,8,144]{0,2,1:T(8,128)S(1)}, u32[]{:S(2)}, u32[]{:S(2)}) async-start(f32[128,8,144]{0,2,1:T(8,128)} %bitcast.15), calls=%async_computation | async-start | bytes 1179648 | tf_op jit(solution)/shard_map/all_to_all | solution.py:113
  48.6 0.7 %compare_reduce_fusion = pred[8,144]{1,0:T(8,128)(4,1)S(1)} fusion(s32[1,8,144]{2,0,1:T(1,128)} %all-to-all-done.1), kind=kLoop, calls=%fused_computation.50 | loop fusion | flops 1152 | bytes 5760 | tf_op jit(solution)/shard_map/eq | solution.py:123
  49.3 0.1 eq.58
  49.4 13.4 %all-to-all-done = f32[128,8,144]{0,2,1:T(8,128)S(1)} async-done(((f32[128,8,144]{0,2,1:T(8,128)}), f32[128,8,144]{0,2,1:T(8,128)S(1)}, u32[]{:S(2)}, u32[]{:S(2)}) %all-to-all-start) | async-done | bytes 589856 | tf_op jit(solution)/shard_map/all_to_all | solution.py:113
  62.8 0.5 fusion.29
  63.4 0.2 copy.44
  63.6 0.2 copy.49
  63.8 0.2 copy.50
  64.0 0.2 copy.51
  64.2 0.2 copy.52
  64.4 0.2 reduce_window_sum.11
  64.6 0.1 multiply_minimum_fusion
  64.6 0.2 fusion.17
  64.8 0.8 %maximum_bitcast_fusion = f32[1,3,32,1152]{3,2,1,0:T(8,128)} fusion(f32[1,32,1152]{2,1,0:T(8,128)S(1)} %get-tuple-element.18, f32[1,32,1152]{2,1,0:T(8,128)S(1)} %get-tuple-element.17, f32[1,32,1152]{2,1,0:T(8,128)S(1)} %get-tuple-element.4), kind=kLoop, calls=%fused_computation.22 | loop fusion | flops 221184 | bytes 884736 | tf_op jit(solution)/shard_map/broadcast_in_dim | solution.py:126
  (27 shorter events, 0.1 us)
Async XLA Ops:
  0.6 6.9 %copy-start = (s32[1,1152]{1,0:T(1,128)S(1)}, s32[1,1152]{1,0:T(1,128)}, u32[]{:S(2)}) copy-start(s32[1,1152]{1,0:T(1,128)} %param.14) | copy-start | bytes 13828
  0.6 3.4 %copy-start.9 = (f32[128,128,1,1]{1,0,3,2:T(8,128)S(1)}, f32[128,128,1,1]{1,0,3,2:T(8,128)}, u32[]{:S(2)}) copy-start(f32[128,128,1,1]{1,0,3,2:T(8,128)} %constant.80) | copy-start | bytes 196612
  0.7 3.4 %copy-start.5 = (f32[16,128]{1,0:T(8,128)S(1)}, f32[16,128]{1,0:T(8,128)}, u32[]{:S(2)}) copy-start(f32[16,128]{1,0:T(8,128)} %param.11) | copy-start | bytes 24580
  0.7 1.9 %copy-start.1 = (f32[3,32,16,128]{3,2,1,0:T(8,128)S(1)}, f32[3,32,16,128]{3,2,1,0:T(8,128)}, u32[]{:S(2)}) copy-start(f32[3,32,16,128]{3,2,1,0:T(8,128)} %param.9) | copy-start | bytes 2359300
  4.1 3.4 %copy-start.6 = (s32[1,1152]{1,0:T(1,128)S(1)}, s32[1,1152]{1,0:T(1,128)}, u32[]{:S(2)}) copy-start(s32[1,1152]{1,0:T(1,128)} %param.13) | copy-start | bytes 13828
  5.0 16.8 %collective-permute-start = (f32[97,1,128]{2,1,0:T(1,128)S(1)}, f32[97,1,128]{2,1,0:T(1,128)S(1)}, u32[]{:S(2)}, u32[]{:S(2)}) collective-permute-start(f32[97,1,128]{2,1,0:T(1,128)S(1)} %get-tuple-element.8), channel_id=1, source_target_pairs={{0,8},{8,16},{16,24},{24,0},{1,9},{9,17},{17,25},{25,1},{2,10},{10... | collective-permute-start | bytes 149000 | tf_op jit(solution)/shard_map/ppermute | solution.py:24
  5.5 16.3 %collective-permute-start.1 = (f32[97,1,128]{2,1,0:T(1,128)S(1)}, f32[97,1,128]{2,1,0:T(1,128)S(1)}, u32[]{:S(2)}, u32[]{:S(2)}) collective-permute-start(f32[97,1,128]{2,1,0:T(1,128)S(1)} %get-tuple-element.9), channel_id=1, source_target_pairs={{8,0},{16,8},{24,16},{0,24},{9,1},{17,9},{25,17},{1,25},{10,2},{18... | collective-permute-start | bytes 149000 | tf_op jit(solution)/shard_map/ppermute | solution.py:25
  14.8 27.9 %all-to-all-start.1 = ((s32[1,8,144]{2,0,1:T(1,128)}), s32[1,8,144]{2,0,1:T(1,128)}, u32[]{:S(2)}, u32[]{:S(2)}) async-start(s32[1,8,144]{2,0,1:T(1,128)} %all_to_all.14), calls=%async_computation.1 | async-start | bytes 16384 | tf_op jit(solution)/shard_map/all_to_all | solution.py:114
  22.4 5.5 %copy-start.4 = (f32[1,32,1152]{2,1,0:T(8,128)S(1)}, f32[1,32,1152]{2,1,0:T(8,128)}, u32[]{:S(2)}) copy-start(f32[1,32,1152]{2,1,0:T(8,128)} %param.12) | copy-start | bytes 442372
  22.8 6.4 %collective-permute-start.2 = (f32[97,18,1]{0,2,1:T(1,128)S(1)}, f32[97,18,1]{0,2,1:T(1,128)S(1)}, u32[]{:S(2)}, u32[]{:S(2)}) collective-permute-start(f32[97,18,1]{0,2,1:T(1,128)S(1)} %copy.35), channel_id=1, source_target_pairs={{0,1},{1,2},{2,3},{3,4},{4,5},{5,6},{6,7},{7,0},{8,9},{9,10},{10,1... | collective-permute-start | bytes 20960 | tf_op jit(solution)/shard_map/ppermute | solution.py:24
  25.2 4.5 %collective-permute-start.3 = (f32[97,18,1]{0,2,1:T(1,128)S(1)}, f32[97,18,1]{0,2,1:T(1,128)S(1)}, u32[]{:S(2)}, u32[]{:S(2)}) collective-permute-start(f32[97,18,1]{0,2,1:T(1,128)S(1)} %copy.36), channel_id=1, source_target_pairs={{1,0},{2,1},{3,2},{4,3},{5,4},{6,5},{7,6},{0,7},{9,8},{10,9},{11,1... | collective-permute-start | bytes 20960 | tf_op jit(solution)/shard_map/ppermute | solution.py:25
  30.3 1.5 %copy-start.7 = (pred[16]{0:T(512)(128)(4,1)S(1)}, pred[16]{0:T(512)(128)(4,1)}, u32[]{:S(2)}) copy-start(pred[16]{0:T(512)(128)(4,1)} %get-tuple-element.19) | copy-start | bytes 52
  30.3 1.5 %copy-start.8 = (pred[16]{0:T(512)(128)(4,1)S(1)}, pred[16]{0:T(512)(128)(4,1)}, u32[]{:S(2)}) copy-start(pred[16]{0:T(512)(128)(4,1)} %get-tuple-element.20) | copy-start | bytes 52
  32.7 1.1 %copy-start.2 = (f32[3,32,16,128]{3,2,1,0:T(8,128)S(1)}, f32[3,32,16,128]{3,2,1,0:T(8,128)}, u32[]{:S(2)}) copy-start(f32[3,32,16,128]{3,2,1,0:T(8,128)} %param.9) | copy-start | bytes 2359300
  38.3 1.1 %copy-start.3 = (f32[1,32,1152]{1,2,0:T(8,128)S(1)}, f32[1,32,1152]{1,2,0:T(8,128)}, u32[]{:S(2)}) copy-start(f32[1,32,1152]{1,2,0:T(8,128)} %copy.41) | copy-start | bytes 442372
  42.7 20.1 %all-to-all-start = ((f32[128,8,144]{0,2,1:T(8,128)}), f32[128,8,144]{0,2,1:T(8,128)S(1)}, u32[]{:S(2)}, u32[]{:S(2)}) async-start(f32[128,8,144]{0,2,1:T(8,128)} %bitcast.15), calls=%async_computation | async-start | bytes 1179648 | tf_op jit(solution)/shard_map/all_to_all | solution.py:113
where the time goes:
time: 66.1 us; the launch traced here: 65.6 us
  local copies, waits for them, and re-layouts  20.2 us (31%)
  starting transfers between devices  19.7 us (30%)
  waiting for transfers between devices  13.6 us (21%)
  other arithmetic  8.89 us (13%)
  matrix products  2.33 us (4%)
  between operations  0.93 us (1%)
    all_to_all x1, waiting for transfers between devices, on_device(): lax.all_to_all(state[:, send_perm], 'blk', split_axis=1, concat_axis=1, t...  13.4 us
    all_to_all x1, starting transfers between devices, on_device(): lax.all_to_all(daytime_indicator[:, send_perm], 'blk', split_axis=1, conc...  6.53 us
    gather x1, local copies, waits for them, and re-layouts, on_device(): daytime_indicator[:, send_perm]  6.48 us
    all_to_all x1, starting transfers between devices, on_device(): lax.all_to_all(state[:, send_perm], 'blk', split_axis=1, concat_axis=1, t...  5.87 us
    ppermute x2, starting transfers between devices, extended(): after = lax.ppermute(initial, axis, down)  4.76 us
    gather x1, local copies, waits for them, and re-layouts, on_device(): state[:, send_perm]  3.11 us
    ppermute x2, starting transfers between devices, extended(): before = lax.ppermute(last, axis, up)  2.56 us
    unnamed x21, local copies, waits for them, and re-layouts  2.28 us
  transfers between devices with their start and end apart: 6, of which 2 were waited for; matrix products, arithmetic and copies ran while one was open for 34% of the time, Pallas kernels for 0%

commit v1 on v0

v1 whole, which is shorter than its diff:
```python
import math

import jax
import jax.numpy as jnp
import numpy as np
from jax import lax
from jax.experimental import pallas as pl
from jax.experimental.pallas import tpu as pltpu
from jax.sharding import PartitionSpec as P

time_step = 0.006
absorb_coef = 0.02
heat_gain = 100.0
sat_base = 3.0
clausius = 0.07
ref_temp = 280.0
LANES = 128


def gll_tables():
    inv_root = 1.0 / math.sqrt(5.0)
    gll_nodes = np.array([-1.0, -inv_root, inv_root, 1.0])
    legendre = (5.0 * gll_nodes**3 - 3.0 * gll_nodes) / 2.0
    deriv_matrix = np.zeros((4, 4))
    for row_index in range(4):
        for col_index in range(4):
            if row_index != col_index:
                deriv_matrix[row_index, col_index] = legendre[row_index] / (
                    legendre[col_index] * (gll_nodes[row_index] - gll_nodes[col_index])
                )
    deriv_matrix[0, 0] = -3.0
    deriv_matrix[3, 3] = 3.0
    weights = np.array([1.0, 5.0, 5.0, 1.0]) / 6.0
    return (deriv_matrix, weights)


def row_maps(size_x):
    shared, count = [], -1
    for n in range(size_x):
        if n == 0 or n % 4 != 0:
            count += 1
        shared.append(count)
    return shared, [n for n in range(size_x) if n % 4 != 3]


def second_dim_matrix(size_y):
    deriv, weight = gll_tables()
    w = np.diag(np.tile(weight, size_y // 4))
    d = np.kron(np.eye(size_y // 4), deriv)
    e = np.eye(size_y)
    for m in range(3, size_y - 1, 4):
        e[m, m + 1] = e[m + 1, m] = 1.0
    both = np.concatenate([-(e @ w @ d).T, -(e @ w).T], axis=0)
    hi = both.astype(jnp.bfloat16)
    lo = (both - hi.astype(np.float64)).astype(jnp.bfloat16)
    return np.concatenate([hi, lo], axis=1)


def split(x):
    hi = x.astype(jnp.bfloat16)
    return hi, (x - hi.astype(jnp.float32)).astype(jnp.bfloat16)


def dot(a, b):
    return jnp.dot(a, b, preferred_element_type=jnp.float32)


def lanes_of(rows):
    return lax.broadcasted_iota(jnp.int32, (rows, LANES), 1)


def transport_kernel(iso_ref, wind_ref, metric_ref, mat_ref, sums_ref, den_ref, row_ref, col_ref, hi_ref, lo_ref):
    size_x, size_y = metric_ref.shape
    levels = wind_ref.shape[0] // (2 * size_x)
    chans = 3 * levels
    deriv, weight = gll_tables()
    shared, _ = row_maps(size_x)
    n_rows = shared[-1] + 1

    def put(row, a, b):
        at = pl.ds(row * chans, chans)
        ahi, alo = split(a)
        bhi, blo = split(b)
        hi_ref[at, 0:size_y] = ahi
        hi_ref[at, size_y : 2 * size_y] = bhi
        lo_ref[at, 0:size_y] = alo
        lo_ref[at, size_y : 2 * size_y] = blo

    held = None
    for e in range(size_x // 4):
        fx, fy = [], []
        for j in range(4):
            n = 4 * e + j
            jac = metric_ref[n : n + 1, :]
            q = iso_ref[pl.ds(n, chans, stride=size_x), :]
            ju = jac * wind_ref[pl.ds(n, levels, stride=size_x), :]
            jv = (jac * float(weight[j])) * wind_ref[pl.ds(levels * size_x + n, levels, stride=size_x), :]
            fx.append(jnp.concatenate([ju, ju, ju], axis=0) * q)
            fy.append(jnp.concatenate([jv, jv, jv], axis=0) * q)
        for i in range(4):
            b = None
            for j in range(4):
                coef = float(weight[i] * deriv[i, j])
                if coef != 0.0:
                    b = coef * fx[j] if b is None else b + coef * fx[j]
            a = fy[i]
            n = 4 * e + i
            if i == 0 and held is not None:
                a, b = a + held[0], b + held[1]
            if i == 3 and n != size_x - 1:
                held = (a, b)
            else:
                put(shared[n], a, b)
    hi = hi_ref[...]
    first = dot(hi, mat_ref[...])
    total = first[:, 0:size_y] + (first[:, size_y:] + dot(lo_ref[...], mat_ref[:, 0:size_y]))
    sums_ref[...] = total

    lane = lanes_of(size_x)
    sub = lax.broadcasted_iota(jnp.int32, (size_x, LANES), 0)
    wl = jnp.where((lane % 4 == 0) | (lane % 4 == 3), float(weight[0]), float(weight[1]))
    ws = jnp.where((sub % 4 == 0) | (sub % 4 == 3), float(weight[0]), float(weight[1]))
    mass = (wl * ws) * metric_ref[...]
    after, before = pltpu.roll(mass, size_x - 1, 0), pltpu.roll(mass, 1, 0)
    mass = mass + jnp.where((sub % 4 == 3) & (sub != size_x - 1), after, 0.0) + jnp.where((sub % 4 == 0) & (sub != 0), before, 0.0)
    after, before = pltpu.roll(mass, size_y - 1, 1), pltpu.roll(mass, 1, 1)
    mass = mass + jnp.where((lane % 4 == 3) & (lane != size_y - 1), after, 0.0) + jnp.where((lane % 4 == 0) & (lane != 0), before, 0.0)
    den_ref[...] = mass

    row_ref[0:chans, :] = sums_ref[pl.ds((n_rows - 1) * chans, chans), :]
    row_ref[chans : chans + 8, :] = jnp.broadcast_to(mass[size_x - 1 : size_x, :], (8, LANES))
    wide = lanes_of(chans)
    col = jnp.zeros((chans, LANES), jnp.float32)
    for r in range(n_rows):
        moved = pltpu.roll(sums_ref[pl.ds(r * chans, chans), :], r + 1, 1)
        col = jnp.where(wide == r, moved, col)
    col_ref[0:chans, :] = col
    dcol = jnp.zeros((1, LANES), jnp.float32)
    for n in range(size_x):
        r = shared[n]
        dcol = jnp.where(lanes_of(1) == r, pltpu.roll(mass, r + 1, 1)[n : n + 1, :], dcol)
    col_ref[chans : chans + 8, :] = jnp.broadcast_to(dcol, (8, LANES))


def cumulative(x):
    rows = x.shape[0]
    sub = lax.broadcasted_iota(jnp.int32, x.shape, 0)
    step = 1
    while step < rows:
        x = x + jnp.where(sub >= step, pltpu.roll(x, step, 0), 0.0)
        step *= 2
    return x


def physics(tracers, temps, day):
    levels = temps.shape[0]
    vapour = tracers[0:levels]
    scaled = absorb_coef * vapour
    heating = heat_gain * scaled * jnp.exp(-cumulative(scaled))
    heated = temps + jnp.where(day == 1.0, heating, 0.0)
    saturation = sat_base * jnp.exp(clausius * (heated - ref_temp))
    remain = jnp.minimum(vapour, saturation)
    log_ratio = jnp.log(remain / vapour)
    inverse = 1.0 / heated
    alpha_heavy = jnp.exp(1137.0 * inverse * inverse - 0.4156 * inverse - 0.0020667)
    alpha_deut = jnp.exp(24844.0 * inverse * inverse - 76.248 * inverse + 0.052612)
    return jnp.concatenate(
        [
            remain,
            tracers[levels : 2 * levels] * jnp.exp(alpha_heavy * log_ratio),
            tracers[2 * levels :] * jnp.exp(alpha_deut * log_ratio),
        ],
        axis=0,
    )


def third(x):
    return lax.shift_right_logical(x * 43691, 17)


def spread_lanes(x):
    rows = x.shape[0]
    lane = lanes_of(rows)
    source = 3 * lax.shift_right_logical(lane, 2) + jnp.minimum(lane & 3, 2)
    padded = jnp.concatenate([x, jnp.zeros((rows, LANES - x.shape[1]), x.dtype)], axis=1)
    return jnp.take_along_axis(padded, source, axis=1)


def before_kernel(n_peers, iso_ref, sums_ref, den_ref, temps_ref, day_ref, order_ref, acc_ref, pick_ref, htemps_ref, hiso_ref, hsum_ref, lhs_ref, hot_ref):
    size_x, size_y = den_ref.shape
    levels, sites = temps_ref.shape
    chans = 3 * levels
    shared, node_rows = row_maps(size_x)
    per_row = sites // len(node_rows)
    per_peer = sites // n_peers
    full, rest = per_peer // LANES, per_peer % LANES
    k_total = (len(node_rows) - 1) * LANES

    order = order_ref[...]
    pieces = [order[:, p * per_peer + LANES * j : p * per_peer + LANES * (j + 1)] for p in range(n_peers) for j in range(full)]
    if rest:
        pieces += [order[:, p * per_peer + LANES * full : (p + 1) * per_peer] for p in range(n_peers)]
    order = jnp.concatenate(pieces, axis=1)
    row = third(lax.shift_right_logical(order, 5))
    within = order - per_row * row
    group = third(within)
    node = 4 * group + (within - 3 * group)
    main = jnp.where((row == 0) | (node == 0), -1, (row - 1) * LANES + node)
    first = jnp.where(row == 0, node, -1)
    side = jnp.where((row != 0) & (node == 0), row, -1)
    sub = lax.broadcasted_iota(jnp.int32, (LANES, LANES), 0)

    def one_hot(index):
        return jnp.where(sub == index, 1.0, 0.0).astype(jnp.bfloat16)

    for t in range(sites // LANES):
        at = slice(t * LANES, (t + 1) * LANES)
        here = main[:, at]
        for k in range(len(node_rows) - 1):
            hot_ref[k * LANES : (k + 1) * LANES, at] = one_hot(here - k * LANES)
        pick_ref[0:LANES, at] = one_hot(first[:, at])
        pick_ref[LANES : 2 * LANES, at] = one_hot(side[:, at])

    temps = temps_ref[...]
    day = day_ref[...].astype(jnp.float32)
    lane1 = lanes_of(1)
    unused = (lane1 & 3) == 3
    own = unused | (lane1 == 0)
    wide, wide_l = lanes_of(chans), lanes_of(levels)
    hiso = jnp.full((chans, LANES), 3.0, jnp.float32)
    hsum = jnp.zeros((chans, LANES), jnp.float32)
    htemp = jnp.full((levels, LANES), ref_temp, jnp.float32)
    hday = jnp.zeros((1, LANES), jnp.float32)
    inv = 1.0 / den_ref[...]
    for k, n in enumerate(node_rows):
        iso = iso_ref[pl.ds(n, chans, stride=size_x), :]
        here = sums_ref[pl.ds(k * chans, chans), :]
        t_here = temps[:, k * per_row : (k + 1) * per_row]
        t_here = jnp.where(unused, ref_temp, spread_lanes(t_here))
        d_here = spread_lanes(jnp.broadcast_to(day[:, k * per_row : (k + 1) * per_row], (8, per_row)))[0:1, :]
        if k == 0:
            htemps_ref[0:levels, :] = t_here
            htemps_ref[2 * levels : 2 * levels + 8, :] = jnp.broadcast_to(d_here, (8, LANES))
            continue
        shift = k
        hiso = jnp.where(wide == k, pltpu.roll(iso, shift, 1), hiso)
        hsum = jnp.where(wide == k, pltpu.roll(here, shift, 1), hsum)
        htemp = jnp.where(wide_l == k, pltpu.roll(t_here, shift, 1), htemp)
        hday = jnp.where(lane1 == k, pltpu.roll(jnp.broadcast_to(d_here, (8, LANES)), shift, 1)[0:1, :], hday)
        gain = jnp.where(own, 0.0, time_step * inv[n : n + 1, :])
        hi, lo = split(physics(iso + gain * here, t_here, d_here))
        lhs_ref[0:chans, (k - 1) * LANES : k * LANES] = hi
        lhs_ref[chans : 2 * chans, (k - 1) * LANES : k * LANES] = lo
    last = len(node_rows)
    hsum = jnp.where(wide == last, pltpu.roll(sums_ref[pl.ds(last * chans, chans), :], last, 1), hsum)
    htemps_ref[levels : 2 * levels, :] = htemp
    htemps_ref[2 * levels + 8 : 2 * levels + 16, :] = jnp.broadcast_to(hday, (8, LANES))
    hiso_ref[...] = hiso
    hsum_ref[0:chans, :] = hsum
    dcol = jnp.ones((1, LANES), jnp.float32)
    for n in range(size_x):
        r = shared[n]
        dcol = jnp.where(lane1 == r, pltpu.roll(den_ref[...], r, 1)[n : n + 1, :] if r else den_ref[n : n + 1, :], dcol)
    hsum_ref[chans : chans + 8, :] = jnp.broadcast_to(dcol, (8, LANES))
    both = dot(lhs_ref[...], hot_ref[...])
    acc_ref[...] = both[0:chans] + both[chans:]


def after_kernel(n_peers, iso_ref, sums_ref, den_ref, acc_ref, pick_ref, htemps_ref, hiso_ref, hsum_ref, row_ref, col_ref, corner_ref, send_ref, rows_ref, cols_ref):
    size_x = den_ref.shape[0]
    chans, sites = acc_ref.shape
    levels = chans // 3
    shared, node_rows = row_maps(size_x)
    n_rows = shared[-1] + 1
    per_peer = sites // n_peers
    full, rest = per_peer // LANES, per_peer % LANES
    wide, lane1 = lanes_of(chans), lanes_of(1)

    corner = pltpu.roll(corner_ref[...], LANES - (n_rows - 1), 1)
    extra = col_ref[...] + corner
    total = sums_ref[0:chans, :] + row_ref[0:chans, :] + jnp.where(wide == 0, extra[0:chans], 0.0)
    den = den_ref[0:1, :] + row_ref[chans : chans + 1, :] + jnp.where(lane1 == 0, extra[chans : chans + 1], 0.0)
    ratio = total / den
    rows_ref[...] = ratio
    iso = iso_ref[pl.ds(0, chans, stride=size_x), :]
    unused = (lane1 & 3) == 3
    new_row = iso + jnp.where(unused, 0.0, time_step * ratio)
    phys_row = physics(new_row, htemps_ref[0:levels, :], htemps_ref[2 * levels : 2 * levels + 1, :])

    live = lane1 < n_rows
    dcol = hsum_ref[chans : chans + 1, :] + jnp.where(live, col_ref[chans : chans + 1, :], 0.0)
    ratio_c = (hsum_ref[0:chans, :] + jnp.where(live, col_ref[0:chans, :], 0.0)) / dcol
    cols_ref[...] = jnp.where(wide == 0, ratio, ratio_c)
    in_use = (lane1 > 0) & (lane1 < len(node_rows))
    new_col = hiso_ref[...] + jnp.where(in_use, time_step * ratio_c, 0.0)
    phys_col = physics(new_col, htemps_ref[levels : 2 * levels, :], htemps_ref[2 * levels + 8 : 2 * levels + 9, :])

    rhi, rlo = split(phys_row)
    chi, clo = split(phys_col)
    lhs = jnp.concatenate([jnp.concatenate([rhi, chi], axis=1), jnp.concatenate([rlo, clo], axis=1)], axis=0)
    both = dot(lhs, pick_ref[...])
    out = acc_ref[...] + (both[0:chans] + both[chans:])
    for p in range(n_peers):
        for j in range(full):
            t = p * full + j
            send_ref[p, j * chans : (j + 1) * chans, :] = out[:, t * LANES : (t + 1) * LANES]
    if rest:
        begin = n_peers * full * LANES
        for t in range(n_peers * rest // LANES):
            block = out[:, begin + t * LANES : begin + (t + 1) * LANES]
            block = jnp.concatenate([block, jnp.zeros((LANES - chans, LANES), jnp.float32)], axis=0).T
            at = t * LANES
            while at < (t + 1) * LANES:
                p, i = at // rest, at % rest
                count = min(rest - i, (t + 1) * LANES - at)
                send_ref[p, full * chans + i : full * chans + i + count, :] = block[at - t * LANES : at - t * LANES + count, :]
                at += count


def advance_kernel(iso_ref, sums_ref, den_ref, rows_ref, cols_ref, back_row_ref, back_col_ref, new_ref):
    size_x = den_ref.shape[0]
    chans = rows_ref.shape[0]
    shared, _ = row_maps(size_x)
    wide = lanes_of(chans)
    inv = 1.0 / den_ref[...]
    for n in range(size_x):
        r = shared[n]
        if n == 0:
            ratio = rows_ref[...]
        elif n == size_x - 1:
            ratio = back_row_ref[...]
        else:
            ratio = sums_ref[pl.ds(r * chans, chans), :] * inv[n : n + 1, :]
            ratio = jnp.where(wide == 0, cols_ref[:, r : r + 1], ratio)
        if n != size_x - 1:
            ratio = jnp.where(wide == LANES - 1, back_col_ref[:, r : r + 1], ratio)
        new_ref[pl.ds(n, chans, stride=size_x), :] = iso_ref[pl.ds(n, chans, stride=size_x), :] + time_step * ratio


def gather_kernel(got_ref, out_ref):
    n_peers, rows, _ = got_ref.shape
    chans, sites = out_ref.shape
    per_peer = sites // n_peers
    full, rest = per_peer // LANES, per_peer % LANES
    lane = lanes_of(chans)
    blocks = [None] * (sites // LANES)

    def place(block, value, low, high):
        old = blocks[block]
        blocks[block] = value if old is None else jnp.where((lane >= low) & (lane < high), value, old)

    for p in range(n_peers):
        for j in range(full):
            begin = p * per_peer + j * LANES
            shift = begin % LANES
            value = got_ref[p, j * chans : (j + 1) * chans, :]
            if shift:
                value = pltpu.roll(value, shift, 1)
            place(begin // LANES, value, shift, LANES)
            if shift:
                place(begin // LANES + 1, value, 0, shift)
    if rest:
        tails = [got_ref[p, full * chans : full * chans + rest, :] for p in range(n_peers)]
        tails = jnp.concatenate(tails, axis=0)
        for t in range(n_peers * rest // LANES):
            block = tails[t * LANES : (t + 1) * LANES, :].T[0:chans, :]
            at = t * LANES
            while at < (t + 1) * LANES:
                p, i = at // rest, at % rest
                count = min(rest - i, (t + 1) * LANES - at)
                column = p * per_peer + full * LANES + i
                place(column // LANES, block, column % LANES, column % LANES + count)
                at += count
    for t, block in enumerate(blocks):
        out_ref[:, t * LANES : (t + 1) * LANES] = block


def call(kernel, outs, scratch, name, *args):
    return pl.pallas_call(
        kernel,
        out_shape=outs,
        scratch_shapes=scratch,
        name=name,
        compiler_params=pltpu.CompilerParams(vmem_limit_bytes=40 * 1024 * 1024),
    )(*args)


def on_device(
    isotope_ratios,
    advecting_velocity,
    metric_scaling,
    thermal_state,
    outgoing_site_order,
    daytime_indicator,
):
    size_x, size_y = metric_scaling.shape
    levels = isotope_ratios.shape[1]
    chans = 3 * levels
    sites = outgoing_site_order.shape[1]
    n_face, n_blk = lax.axis_size("face"), lax.axis_size("blk")
    shared, node_rows = row_maps(size_x)
    n_rows = shared[-1] + 1
    per_peer = sites // n_blk
    send_rows = chans * (per_peer // LANES) + per_peer % LANES

    def f32(*shape):
        return jax.ShapeDtypeStruct(shape, jnp.float32)

    iso = isotope_ratios.reshape(chans * size_x, size_y)
    wind = advecting_velocity.reshape(2 * levels * size_x, size_y)
    matrix = jnp.asarray(second_dim_matrix(size_y))
    sums, den, row, col = call(
        transport_kernel,
        (f32(n_rows * chans, size_y), f32(size_x, size_y), f32(chans + 8, LANES), f32(chans + 8, LANES)),
        [pltpu.VMEM((n_rows * chans, 2 * size_y), jnp.bfloat16)] * 2,
        "transport",
        iso,
        wind,
        metric_scaling,
        matrix,
    )
    face_up = [(i, (i + 1) % n_face) for i in range(n_face)]
    blk_up = [(i, (i + 1) % n_blk) for i in range(n_blk)]
    diagonal = [(i * n_blk + j, (i + 1) % n_face * n_blk + (j + 1) % n_blk) for i in range(n_face) for j in range(n_blk)]
    got_row = lax.ppermute(row, "face", face_up)
    got_col = lax.ppermute(col, "blk", blk_up)
    got_corner = lax.ppermute(col, ("face", "blk"), diagonal)

    bf16 = jnp.bfloat16
    acc, pick, htemps, hiso, hsum = call(
        lambda *refs: before_kernel(n_blk, *refs),
        (
            f32(chans, sites),
            jax.ShapeDtypeStruct((2 * LANES, sites), bf16),
            f32(2 * levels + 16, LANES),
            f32(chans, LANES),
            f32(chans + 8, LANES),
        ),
        [pltpu.VMEM((2 * chans, (len(node_rows) - 1) * LANES), bf16), pltpu.VMEM(((len(node_rows) - 1) * LANES, sites), bf16)],
        "inner_columns",
        iso,
        sums,
        den,
        thermal_state[0],
        daytime_indicator,
        outgoing_site_order,
    )
    send, rows, cols = call(
        lambda *refs: after_kernel(n_blk, *refs),
        (f32(n_blk, send_rows, LANES), f32(chans, LANES), f32(chans, LANES)),
        [],
        "edge_columns",
        iso,
        sums,
        den,
        acc,
        pick,
        htemps,
        hiso,
        hsum,
        got_row,
        got_col,
        got_corner,
    )
    got = lax.all_to_all(send, "blk", split_axis=0, concat_axis=0, tiled=True)
    back_col = lax.ppermute(cols, "blk", [(j, i) for i, j in blk_up])
    ends = jnp.where(jnp.arange(LANES)[None, :] == LANES - 1, back_col[:, 0:1], rows)
    back_row = lax.ppermute(ends, "face", [(j, i) for i, j in face_up])
    new = call(advance_kernel, f32(chans * size_x, size_y), [], "advance", iso, sums, den, rows, cols, back_row, back_col)
    phys = call(gather_kernel, f32(chans, sites), [], "assemble", got)
    return (new.reshape(isotope_ratios.shape), phys.reshape(1, 3, levels, sites))


def solution(mesh):
    placed = (
        P(None, None, "face", "blk"),
        P(None, None, "face", "blk"),
        P("face", "blk"),
        P("face", None, "blk"),
        P("face", "blk"),
        P("face", "blk"),
    )
    return jax.shard_map(
        on_device,
        mesh=mesh,
        in_specs=placed,
        out_specs=(P(None, None, "face", "blk"), P("face", None, None, "blk")),
        check_vma=False,
    )
```

time: 66.1 us -> 38.3 us (0.58)
  the two profiles are of different devices: /device:TPU:0 before, /device:TPU:11 now
where the time goes in v1:
time: 38.3 us; the launch traced here: 37.9 us
  waiting for transfers between devices  14.1 us (37%)
  starting transfers between devices  11.9 us (31%)
  Pallas kernels  7.24 us (19%)
  local copies, waits for them, and re-layouts  3.89 us (10%)
  between operations  0.72 us (2%)
    ppermute x1, waiting for transfers between devices, on_device(): back_col = lax.ppermute(cols, 'blk', [(j, i) for i, j in blk_up])  11.2 us
    pallas_call x5, Pallas kernels, call(): pl.pallas_call(kernel, out_shape=outs, scratch_shapes=scratch, name=name,...  7.24 us
    all_to_all x1, starting transfers between devices, on_device(): got = lax.all_to_all(send, 'blk', split_axis=0, concat_axis=0, tiled=True)  4.78 us
    unnamed x16, local copies, waits for them, and re-layouts  3.79 us
    ppermute x1, starting transfers between devices, on_device(): got_corner = lax.ppermute(col, ('face', 'blk'), diagonal)  3.01 us
    ppermute x1, waiting for transfers between devices, on_device(): back_row = lax.ppermute(ends, 'face', [(j, i) for i, j in face_up])  2.92 us
    ppermute x1, starting transfers between devices, on_device(): back_row = lax.ppermute(ends, 'face', [(j, i) for i, j in face_up])  2.49 us
    ppermute x1, starting transfers between devices, on_device(): got_col = lax.ppermute(col, 'blk', blk_up)  1.32 us
  transfers between devices with their start and end apart: 6, of which 2 were waited for; matrix products, arithmetic and copies ran while one was open for 0% of the time, Pallas kernels for 10%

profile of v1, /device:TPU:11, one launch (start us, length us, event | category | flops | bytes accessed | tf_op | source)
XLA Modules:
  0.0 37.9 jit_solution(5516083301824656437)
XLA Ops:
  0.6 0.0 copy-start
  0.6 1.1 %copy-done = f32[3,32,16,128]{3,2,1,0:T(8,128)S(1)} copy-done((f32[3,32,16,128]{3,2,1,0:T(8,128)S(1)}, f32[3,32,16,128]{3,2,1,0:T(8,128)}, u32[]{:S(2)}) %copy-start) | copy-done | bytes 786456
  1.8 0.0 copy-start.2
  1.8 1.0 %copy-done.2 = f32[2,32,16,128]{3,2,1,0:T(8,128)S(1)} copy-done((f32[2,32,16,128]{3,2,1,0:T(8,128)S(1)}, f32[2,32,16,128]{3,2,1,0:T(8,128)}, u32[]{:S(2)}) %copy-start.2) | copy-done | bytes 524312
  2.8 0.0 copy-start.4
  2.8 0.9 %copy-done.4 = bf16[256,256]{1,0:T(8,128)(2,1)S(1)} copy-done((bf16[256,256]{1,0:T(8,128)(2,1)S(1)}, bf16[256,256]{1,0:T(8,128)(2,1)}, u32[]{:S(2)}) %copy-start.4) | copy-done | bytes 131096
  3.7 0.0 copy-start.5
  3.7 0.7 %copy-done.5 = f32[16,128]{1,0:T(8,128)S(1)} copy-done((f32[16,128]{1,0:T(8,128)S(1)}, f32[16,128]{1,0:T(8,128)}, u32[]{:S(2)}) %copy-start.5) | copy-done | bytes 8216
  4.4 0.0 copy-start.3
  4.4 1.1 %transport.1 = (f32[1248,128]{1,0:T(8,128)S(1)}, f32[16,128]{1,0:T(8,128)S(1)}, f32[104,128]{1,0:T(8,128)S(1)}, f32[104,128]{1,0:T(8,128)S(1)}) custom-call(f32[1536,128]{1,0:T(8,128)S(1)} %bitcast.5, f32[1024,128]{1,0:T(8,128)S(1)} %bitcast.9, f32[16,128]{1,0:T(8,128)S(1)} %copy-done.5, bf16[256,256]{1,0:T(8,128)(2,1)S(1)} %copy-done.4), custom_call_target="tpu_custom_call" | custom-call | tf_op jit(solution)/shard_map/transport/pallas_call | solution.py:379
  5.5 0.0 copy-start.6
  5.5 0.0 copy-start.7
  5.6 1.3 %collective-permute-start.1 = (f32[104,128]{1,0:T(8,128)S(1)}, f32[104,128]{1,0:T(8,128)S(1)}, u32[]{:S(2)}, u32[]{:S(2)}) collective-permute-start(f32[104,128]{1,0:T(8,128)S(1)} %get-tuple-element.22), channel_id=1, source_target_pairs={{0,1},{1,2},{2,3},{3,4},{4,5},{5,6},{6,7},{7,0},{8,9},{9,10},{10,1... | collective-permute-start | bytes 159752 | tf_op jit(solution)/shard_map/ppermute | solution.py:426
  6.9 3.0 %collective-permute-start.2 = (f32[104,128]{1,0:T(8,128)S(1)}, f32[104,128]{1,0:T(8,128)S(1)}, u32[]{:S(2)}, u32[]{:S(2)}) collective-permute-start(f32[104,128]{1,0:T(8,128)S(1)} %get-tuple-element.22), channel_id=1, source_target_pairs={{0,9},{1,10},{2,11},{3,12},{4,13},{5,14},{6,15},{7,8},{8,17},{9,18... | collective-permute-start | bytes 159752 | tf_op jit(solution)/shard_map/ppermute | solution.py:427
  9.9 0.0 collective-permute-start
  9.9 0.0 copy-done.3
  9.9 0.0 copy-done.6
  9.9 0.0 copy-done.7
  9.9 2.4 %inner_columns.1 = (f32[96,1152]{1,0:T(8,128)S(1)}, bf16[256,1152]{1,0:T(8,128)(2,1)S(1)}, f32[80,128]{1,0:T(8,128)S(1)}, f32[96,128]{1,0:T(8,128)S(1)}, f32[104,128]{1,0:T(8,128)S(1)}) custom-call(f32[1536,128]{1,0:T(8,128)S(1)} %bitcast.6, f32[1248,128]{1,0:T(8,128)S(1)} %get-tuple-element.14.refs_1_.sums_ref, ...), custom_call_target="tpu_custom_call" | custom-call | tf_op jit(solution)/shard_map/inner_columns/pallas_call | solution.py:379
  12.3 0.0 collective-permute-done.1.refs_9_
  12.3 0.0 collective-permute-done.2.refs_10_
  12.3 0.0 collective-permute-done.refs_8_
  12.3 1.2 %edge_columns.1 = (f32[8,112,128]{2,1,0:T(8,128)}, f32[96,128]{1,0:T(8,128)S(1)}, f32[96,128]{1,0:T(8,128)S(1)}) custom-call(f32[1536,128]{1,0:T(8,128)S(1)} %bitcast.7, f32[1248,128]{1,0:T(8,128)S(1)} %get-tuple-element.14.refs_1_.sums_ref, f32[16,128]{1,0:T(8,128)S(1)} %get-tuple-element.15.refs_2_.den_ref, f32[96,1152]{1,0:T(8,128)S(1)} %get-tuple-element.16.refs_3_, ...), custom_call_target="tpu_custom_call" | custom-call | tf_op jit(solution)/shard_map/edge_columns/pallas_call | solution.py:379
  13.6 0.0 copy-start.1
  13.6 4.8 %all-to-all-start = ((f32[8,112,128]{2,1,0:T(8,128)}), f32[8,112,128]{2,1,0:T(8,128)S(1)}, u32[]{:S(2)}, u32[]{:S(2)}) async-start(f32[8,112,128]{2,1,0:T(8,128)} %get-tuple-element.25), calls=%async_computation | async-start | bytes 917504 | tf_op jit(solution)/shard_map/all_to_all | solution.py:465
  18.4 0.3 collective-permute-start.3
  18.7 11.2 %collective-permute-done.3.back_col_ref = f32[96,128]{1,0:T(8,128)S(1)} collective-permute-done((f32[96,128]{1,0:T(8,128)S(1)}, f32[96,128]{1,0:T(8,128)S(1)}, u32[]{:S(2)}, u32[]{:S(2)}) %collective-permute-start.3) | collective-permute-done | bytes 49184 | tf_op jit(solution)/shard_map/ppermute | solution.py:466
  29.9 0.1 slice_reduce_fusion
  30.0 0.1 broadcast_select_fusion
  30.0 2.5 %collective-permute-start.4 = (f32[96,128]{1,0:T(8,128)S(1)}, f32[96,128]{1,0:T(8,128)S(1)}, u32[]{:S(2)}, u32[]{:S(2)}) collective-permute-start(f32[96,128]{1,0:T(8,128)S(1)} %broadcast_select_fusion), channel_id=1, source_target_pairs={{8,0},{16,8},{24,16},{0,24},{9,1},{17,9},{25,17},{1,25},{10,2},{18... | collective-permute-start | bytes 147464 | tf_op jit(solution)/shard_map/ppermute | solution.py:468
  32.5 2.9 %collective-permute-done.4.back_row_ref = f32[96,128]{1,0:T(8,128)S(1)} collective-permute-done((f32[96,128]{1,0:T(8,128)S(1)}, f32[96,128]{1,0:T(8,128)S(1)}, u32[]{:S(2)}, u32[]{:S(2)}) %collective-permute-start.4) | collective-permute-done | bytes 49184 | tf_op jit(solution)/shard_map/ppermute | solution.py:468
  35.5 0.0 copy-done.1
  35.5 1.5 %advance.1 = f32[1536,128]{1,0:T(8,128)} custom-call(f32[1536,128]{1,0:T(8,128)S(1)} %bitcast.8, f32[1248,128]{1,0:T(8,128)S(1)} %get-tuple-element.14.refs_1_.sums_ref, f32[16,128]{1,0:T(8,128)S(1)} %get-tuple-element.15.refs_2_.den_ref, f32[96,128]{1,0:T(8,128)S(1)} %get-tuple-element.23.rows_ref, f32[96,128]{1,0:T(8,128)S(1)} %get-tuple-element.24.cols_ref, ...), custom_call_target="tpu_custom_call" | custom-call | tf_op jit(solution)/shard_map/advance/pallas_call | solution.py:379
  37.0 0.0 all-to-all-done.got_ref
  37.0 1.0 %assemble.1 = f32[96,1152]{1,0:T(8,128)} custom-call(f32[8,112,128]{2,1,0:T(8,128)S(1)} %all-to-all-done.got_ref), custom_call_target="tpu_custom_call" | custom-call | tf_op jit(solution)/shard_map/assemble/pallas_call | solution.py:379
  (1 shorter events, 0.0 us)
Async XLA Ops:
  0.6 1.1 %copy-start = (f32[3,32,16,128]{3,2,1,0:T(8,128)S(1)}, f32[3,32,16,128]{3,2,1,0:T(8,128)}, u32[]{:S(2)}) copy-start(f32[3,32,16,128]{3,2,1,0:T(8,128)} %param.7) | copy-start | bytes 2359300
  1.8 1.0 %copy-start.2 = (f32[2,32,16,128]{3,2,1,0:T(8,128)S(1)}, f32[2,32,16,128]{3,2,1,0:T(8,128)}, u32[]{:S(2)}) copy-start(f32[2,32,16,128]{3,2,1,0:T(8,128)} %param.8) | copy-start | bytes 1572868
  2.8 0.9 %copy-start.4 = (bf16[256,256]{1,0:T(8,128)(2,1)S(1)}, bf16[256,256]{1,0:T(8,128)(2,1)}, u32[]{:S(2)}) copy-start(bf16[256,256]{1,0:T(8,128)(2,1)} %constant.4.clone.mat_ref) | copy-start | bytes 393220
  3.7 0.7 %copy-start.5 = (f32[16,128]{1,0:T(8,128)S(1)}, f32[16,128]{1,0:T(8,128)}, u32[]{:S(2)}) copy-start(f32[16,128]{1,0:T(8,128)} %metric_ref.1) | copy-start | bytes 24580
  4.4 5.5 %copy-start.3 = (f32[1,32,1152]{2,1,0:T(8,128)S(1)}, f32[1,32,1152]{2,1,0:T(8,128)}, u32[]{:S(2)}) copy-start(f32[1,32,1152]{2,1,0:T(8,128)} %param.10) | copy-start | bytes 442372
  5.5 4.4 %copy-start.6 = (s32[1,1152]{1,0:T(1,128)S(1)}, s32[1,1152]{1,0:T(1,128)}, u32[]{:S(2)}) copy-start(s32[1,1152]{1,0:T(1,128)} %refs_4_.1) | copy-start | bytes 13828
  5.5 4.4 %copy-start.7 = (s32[1,1152]{1,0:T(1,128)S(1)}, s32[1,1152]{1,0:T(1,128)}, u32[]{:S(2)}) copy-start(s32[1,1152]{1,0:T(1,128)} %refs_5_.1) | copy-start | bytes 13828
  5.6 6.8 %collective-permute-start.1 = (f32[104,128]{1,0:T(8,128)S(1)}, f32[104,128]{1,0:T(8,128)S(1)}, u32[]{:S(2)}, u32[]{:S(2)}) collective-permute-start(f32[104,128]{1,0:T(8,128)S(1)} %get-tuple-element.22), channel_id=1, source_target_pairs={{0,1},{1,2},{2,3},{3,4},{4,5},{5,6},{6,7},{7,0},{8,9},{9,10},{10,1... | collective-permute-start | bytes 159752 | tf_op jit(solution)/shard_map/ppermute | solution.py:426
  6.9 5.4 %collective-permute-start.2 = (f32[104,128]{1,0:T(8,128)S(1)}, f32[104,128]{1,0:T(8,128)S(1)}, u32[]{:S(2)}, u32[]{:S(2)}) collective-permute-start(f32[104,128]{1,0:T(8,128)S(1)} %get-tuple-element.22), channel_id=1, source_target_pairs={{0,9},{1,10},{2,11},{3,12},{4,13},{5,14},{6,15},{7,8},{8,17},{9,18... | collective-permute-start | bytes 159752 | tf_op jit(solution)/shard_map/ppermute | solution.py:427
  9.9 2.5 %collective-permute-start = (f32[104,128]{1,0:T(8,128)S(1)}, f32[104,128]{1,0:T(8,128)S(1)}, u32[]{:S(2)}, u32[]{:S(2)}) collective-permute-start(f32[104,128]{1,0:T(8,128)S(1)} %get-tuple-element.21), channel_id=1, source_target_pairs={{0,8},{8,16},{16,24},{24,0},{1,9},{9,17},{17,25},{25,1},{2,10},{10... | collective-permute-start | bytes 159752 | tf_op jit(solution)/shard_map/ppermute | solution.py:425
  13.6 21.9 %copy-start.1 = (f32[3,32,16,128]{3,2,1,0:T(8,128)S(1)}, f32[3,32,16,128]{3,2,1,0:T(8,128)}, u32[]{:S(2)}) copy-start(f32[3,32,16,128]{3,2,1,0:T(8,128)} %param.7) | copy-start | bytes 2359300
  13.6 23.4 %all-to-all-start = ((f32[8,112,128]{2,1,0:T(8,128)}), f32[8,112,128]{2,1,0:T(8,128)S(1)}, u32[]{:S(2)}, u32[]{:S(2)}) async-start(f32[8,112,128]{2,1,0:T(8,128)} %get-tuple-element.25), calls=%async_computation | async-start | bytes 917504 | tf_op jit(solution)/shard_map/all_to_all | solution.py:465
  18.4 11.5 %collective-permute-start.3 = (f32[96,128]{1,0:T(8,128)S(1)}, f32[96,128]{1,0:T(8,128)S(1)}, u32[]{:S(2)}, u32[]{:S(2)}) collective-permute-start(f32[96,128]{1,0:T(8,128)S(1)} %get-tuple-element.24.cols_ref), channel_id=1, source_target_pairs={{1,0},{2,1},{3,2},{4,3},{5,4},{6,5},{7,6},{0,7},{9,8},{10,9},{11,1... | collective-permute-start | bytes 147464 | tf_op jit(solution)/shard_map/ppermute | solution.py:466
  30.0 5.4 %collective-permute-start.4 = (f32[96,128]{1,0:T(8,128)S(1)}, f32[96,128]{1,0:T(8,128)S(1)}, u32[]{:S(2)}, u32[]{:S(2)}) collective-permute-start(f32[96,128]{1,0:T(8,128)S(1)} %broadcast_select_fusion), channel_id=1, source_target_pairs={{8,0},{16,8},{24,16},{0,24},{9,1},{17,9},{25,17},{1,25},{10,2},{18... | collective-permute-start | bytes 147464 | tf_op jit(solution)/shard_map/ppermute | solution.py:468

commit v2 on v1

v2 whole, which is shorter than its diff:
```python
import math

import jax
import jax.numpy as jnp
import numpy as np
from jax import lax
from jax.experimental import pallas as pl
from jax.experimental.pallas import tpu as pltpu
from jax.sharding import PartitionSpec as P

time_step = 0.006
absorb_coef = 0.02
heat_gain = 100.0
sat_base = 3.0
clausius = 0.07
ref_temp = 280.0
LANES = 128


def gll_tables():
    inv_root = 1.0 / math.sqrt(5.0)
    gll_nodes = np.array([-1.0, -inv_root, inv_root, 1.0])
    legendre = (5.0 * gll_nodes**3 - 3.0 * gll_nodes) / 2.0
    deriv_matrix = np.zeros((4, 4))
    for row_index in range(4):
        for col_index in range(4):
            if row_index != col_index:
                deriv_matrix[row_index, col_index] = legendre[row_index] / (
                    legendre[col_index] * (gll_nodes[row_index] - gll_nodes[col_index])
                )
    deriv_matrix[0, 0] = -3.0
    deriv_matrix[3, 3] = 3.0
    weights = np.array([1.0, 5.0, 5.0, 1.0]) / 6.0
    return (deriv_matrix, weights)


def row_maps(size_x):
    shared, count = [], -1
    for n in range(size_x):
        if n == 0 or n % 4 != 0:
            count += 1
        shared.append(count)
    return shared, [n for n in range(size_x) if n % 4 != 3]


def second_dim_matrix(size_y):
    deriv, weight = gll_tables()
    w = np.diag(np.tile(weight, size_y // 4))
    d = np.kron(np.eye(size_y // 4), deriv)
    e = np.eye(size_y)
    for m in range(3, size_y - 1, 4):
        e[m, m + 1] = e[m + 1, m] = 1.0
    both = np.concatenate([-(e @ w @ d).T, -(e @ w).T], axis=0)
    hi = both.astype(jnp.bfloat16)
    lo = (both - hi.astype(np.float64)).astype(jnp.bfloat16)
    return np.concatenate([hi, lo], axis=1)


def split(x):
    hi = x.astype(jnp.bfloat16)
    return hi, (x - hi.astype(jnp.float32)).astype(jnp.bfloat16)


def dot(a, b):
    return jnp.dot(a, b, preferred_element_type=jnp.float32)


def lanes_of(rows):
    return lax.broadcasted_iota(jnp.int32, (rows, LANES), 1)


def put_split(hi_ref, lo_ref, at, a, b):
    size_y = a.shape[1]
    ahi, alo = split(a)
    bhi, blo = split(b)
    hi_ref[at, 0:size_y] = ahi
    hi_ref[at, size_y : 2 * size_y] = bhi
    lo_ref[at, 0:size_y] = alo
    lo_ref[at, size_y : 2 * size_y] = blo


def second_dim(hi, lo, mat):
    size_y = hi.shape[1] // 2
    first = dot(hi, mat)
    return first[:, 0:size_y] + (first[:, size_y:] + dot(lo, mat[:, 0:size_y]))


def fluxes(iso_ref, wind_ref, metric_ref, s, n, weight):
    size_x = metric_ref.shape[0]
    part = wind_ref.shape[0] // 2
    levels = part // size_x
    jac = metric_ref[n : n + 1, :]
    q = iso_ref[pl.ds(s * part + n, levels, stride=size_x), :]
    fx = (jac * wind_ref[pl.ds(n, levels, stride=size_x), :]) * q
    if weight is None:
        return fx
    return fx, ((jac * weight) * wind_ref[pl.ds(part + n, levels, stride=size_x), :]) * q


def weighted_derivative(coefs, fx):
    total = None
    for coef, f in zip(coefs, fx):
        if coef != 0.0:
            total = float(coef) * f if total is None else total + float(coef) * f
    return total


def edge_rows_kernel(
    iso_hbm,
    wind_hbm,
    metric_hbm,
    mat_hbm,
    temps_hbm,
    day_hbm,
    order_hbm,
    iso_ref,
    wind_ref,
    metric_ref,
    mat_ref,
    temps_ref,
    day_ref,
    order_ref,
    den_ref,
    low_ref,
    high_ref,
    hi_ref,
    lo_ref,
    sems,
):
    size_x, size_y = metric_ref.shape
    part = wind_ref.shape[0] // 2
    levels = part // size_x
    chans = 3 * levels
    deriv, weight = gll_tables()
    copies = [pltpu.make_async_copy(metric_hbm, metric_ref, sems.at[0])]
    for k in range(2):
        copies.append(pltpu.make_async_copy(wind_hbm.at[pl.ds(k * part, part)], wind_ref.at[pl.ds(k * part, part)], sems.at[1 + k]))
    for s in range(3):
        copies.append(pltpu.make_async_copy(iso_hbm.at[pl.ds(s * part, part)], iso_ref.at[pl.ds(s * part, part)], sems.at[3 + s]))
    copies.append(pltpu.make_async_copy(mat_hbm, mat_ref, sems.at[6]))
    for k, (src, dst) in enumerate(((temps_hbm, temps_ref), (day_hbm, day_ref), (order_hbm, order_ref))):
        copies.append(pltpu.make_async_copy(src, dst, sems.at[7 + k]))
    for c in copies:
        c.start()

    copies[0].wait()
    lane = lanes_of(size_x)
    sub = lax.broadcasted_iota(jnp.int32, (size_x, LANES), 0)
    wl = jnp.where((lane % 4 == 0) | (lane % 4 == 3), float(weight[0]), float(weight[1]))
    ws = jnp.where((sub % 4 == 0) | (sub % 4 == 3), float(weight[0]), float(weight[1]))
    mass = (wl * ws) * metric_ref[...]
    after, before = pltpu.roll(mass, size_x - 1, 0), pltpu.roll(mass, 1, 0)
    mass = mass + jnp.where((sub % 4 == 3) & (sub != size_x - 1), after, 0.0) + jnp.where((sub % 4 == 0) & (sub != 0), before, 0.0)
    after, before = pltpu.roll(mass, size_y - 1, 1), pltpu.roll(mass, 1, 1)
    mass = mass + jnp.where((lane % 4 == 3) & (lane != size_y - 1), after, 0.0) + jnp.where((lane % 4 == 0) & (lane != 0), before, 0.0)
    den_ref[...] = mass

    for c in copies[1:3]:
        c.wait()
    for s in range(3):
        copies[3 + s].wait()
        for k, (first, i) in enumerate(((0, 0), (size_x - 4, 3))):
            fx = []
            for j in range(4):
                if j == i:
                    f, fy = fluxes(iso_ref, wind_ref, metric_ref, s, first + j, float(weight[i]))
                else:
                    f = fluxes(iso_ref, wind_ref, metric_ref, s, first + j, None)
                fx.append(f)
            put_split(hi_ref, lo_ref, pl.ds(k * chans + s * levels, levels), fy, weighted_derivative(weight[i] * deriv[i], fx))
    copies[6].wait()
    total = second_dim(hi_ref[...], lo_ref[...], mat_ref[...])
    for ref, k, n in ((low_ref, 0, 0), (high_ref, 1, size_x - 1)):
        ref[0:chans, :] = total[k * chans : (k + 1) * chans, :]
        ref[chans : chans + 8, :] = jnp.broadcast_to(mass[n : n + 1, :], (8, LANES))
    for c in copies[7:]:
        c.wait()


def transport_kernel(iso_ref, wind_ref, metric_ref, mat_ref, den_ref, low_ref, high_ref, sums_ref, left_ref, right_ref, hi_ref, lo_ref):
    size_x, size_y = metric_ref.shape
    levels = wind_ref.shape[0] // (2 * size_x)
    chans = 3 * levels
    deriv, weight = gll_tables()
    shared, _ = row_maps(size_x)
    n_rows = shared[-1] + 1
    for s in range(3):
        held = None
        for e in range(size_x // 4):
            fx, fy = [], []
            for j in range(4):
                f, g = fluxes(iso_ref, wind_ref, metric_ref, s, 4 * e + j, float(weight[j]))
                fx.append(f)
                fy.append(g)
            for i in range(4):
                n = 4 * e + i
                if n == 0 or n == size_x - 1:
                    continue
                a, b = fy[i], weighted_derivative(weight[i] * deriv[i], fx)
                if i == 0:
                    a, b = a + held[0], b + held[1]
                if i == 3:
                    held = (a, b)
                else:
                    put_split(hi_ref, lo_ref, pl.ds((shared[n] - 1) * chans + s * levels, levels), a, b)
    last = (n_rows - 1) * chans
    sums_ref[0:chans, :] = low_ref[0:chans, :]
    sums_ref[chans:last, :] = second_dim(hi_ref[...], lo_ref[...], mat_ref[...])
    sums_ref[last : last + chans, :] = high_ref[0:chans, :]

    mass = den_ref[...]
    wide, lane1 = lanes_of(chans), lanes_of(1)
    first_col = jnp.zeros((chans, LANES), jnp.float32)
    last_col = first_col
    first_den = jnp.zeros((1, LANES), jnp.float32)
    last_den = first_den
    for r in range(n_rows):
        here = sums_ref[pl.ds(r * chans, chans), :]
        n = shared.index(r)
        if r:
            first_col = jnp.where(wide == r, pltpu.roll(here, r, 1), first_col)
            first_den = jnp.where(lane1 == r, pltpu.roll(mass, r, 1)[n : n + 1, :], first_den)
        else:
            first_col = jnp.where(wide == 0, here, first_col)
            first_den = jnp.where(lane1 == 0, mass[0:1, :], first_den)
        last_col = jnp.where(wide == r, pltpu.roll(here, r + 1, 1), last_col)
        last_den = jnp.where(lane1 == r, pltpu.roll(mass, r + 1, 1)[n : n + 1, :], last_den)
    left_ref[0:chans, :] = first_col
    left_ref[chans : chans + 8, :] = jnp.broadcast_to(first_den, (8, LANES))
    right_ref[0:chans, :] = last_col
    right_ref[chans : chans + 8, :] = jnp.broadcast_to(last_den, (8, LANES))


def corners_kernel(n_rows, filler_ref, left_ref, right_ref, from_low_ref, from_high_ref, new_left_ref, new_right_ref):
    del filler_ref
    low, high = from_low_ref[...], from_high_ref[...]
    lane = lanes_of(low.shape[0])
    last = n_rows - 1
    new_left_ref[...] = left_ref[...] + jnp.where(lane == 0, low, 0.0) + jnp.where(lane == last, pltpu.roll(high, last, 1), 0.0)
    new_right_ref[...] = (
        right_ref[...] + jnp.where(lane == 0, pltpu.roll(low, 1, 1), 0.0) + jnp.where(lane == last, pltpu.roll(high, last + 1, 1), 0.0)
    )


def cumulative(x):
    rows = x.shape[0]
    sub = lax.broadcasted_iota(jnp.int32, x.shape, 0)
    step = 1
    while step < rows:
        x = x + jnp.where(sub >= step, pltpu.roll(x, step, 0), 0.0)
        step *= 2
    return x


def physics(tracers, temps, day):
    levels = temps.shape[0]
    vapour = tracers[0:levels]
    scaled = absorb_coef * vapour
    heating = heat_gain * scaled * jnp.exp(-cumulative(scaled))
    heated = temps + jnp.where(day == 1.0, heating, 0.0)
    saturation = sat_base * jnp.exp(clausius * (heated - ref_temp))
    remain = jnp.minimum(vapour, saturation)
    log_ratio = jnp.log(remain / vapour)
    inverse = 1.0 / heated
    alpha_heavy = jnp.exp(1137.0 * inverse * inverse - 0.4156 * inverse - 0.0020667)
    alpha_deut = jnp.exp(24844.0 * inverse * inverse - 76.248 * inverse + 0.052612)
    return jnp.concatenate(
        [
            remain,
            tracers[levels : 2 * levels] * jnp.exp(alpha_heavy * log_ratio),
            tracers[2 * levels :] * jnp.exp(alpha_deut * log_ratio),
        ],
        axis=0,
    )


def peer_of(slot, paired):
    return lax.axis_index("blk") ^ slot if paired else slot


def third(x):
    return lax.shift_right_logical(x * 43691, 17)


def spread_lanes(x):
    rows = x.shape[0]
    lane = lanes_of(rows)
    source = 3 * lax.shift_right_logical(lane, 2) + jnp.minimum(lane & 3, 2)
    padded = jnp.concatenate([x, jnp.zeros((rows, LANES - x.shape[1]), x.dtype)], axis=1)
    return jnp.take_along_axis(padded, source, axis=1)


def send_order_kernel(n_peers, paired, temps_ref, day_ref, order_ref, hot_ref, pick_ref, ntemps_ref, nday_ref, slots_ref):
    levels, sites = temps_ref.shape
    count = ntemps_ref.shape[0] // levels - 1
    per_row = sites // count
    per_peer = sites // n_peers
    full, rest = per_peer // LANES, per_peer % LANES

    order = order_ref[...]
    for p in range(n_peers):
        mine = order[:, p * per_peer : (p + 1) * per_peer]
        pad = slots_ref.shape[1] - per_peer
        slots_ref[p : p + 1, :] = jnp.concatenate([mine, jnp.zeros((1, pad), jnp.int32)], axis=1) if pad else mine
    peers = [slots_ref[pl.ds(peer_of(k, paired), 1), :] for k in range(n_peers)]
    pieces = [mine[:, LANES * j : LANES * (j + 1)] for mine in peers for j in range(full)]
    if rest:
        pieces += [mine[:, LANES * full : per_peer] for mine in peers]
    order = jnp.concatenate(pieces, axis=1)
    row = third(lax.shift_right_logical(order, 5))
    within = order - per_row * row
    group = third(within)
    node = 4 * group + (within - 3 * group)
    main = jnp.where((row == 0) | (node == 0), -1, (row - 1) * LANES + node)
    first = jnp.where(row == 0, node, -1)
    side = jnp.where((row != 0) & (node == 0), row, -1)
    sub = lax.broadcasted_iota(jnp.int32, (LANES, LANES), 0)

    def one_hot(index):
        return jnp.where(sub == index, 1.0, 0.0).astype(jnp.bfloat16)

    for t in range(sites // LANES):
        at = slice(t * LANES, (t + 1) * LANES)
        here = main[:, at]
        for k in range(count - 1):
            hot_ref[k * LANES : (k + 1) * LANES, at] = one_hot(here - k * LANES)
        pick_ref[0:LANES, at] = one_hot(first[:, at])
        pick_ref[LANES : 2 * LANES, at] = one_hot(side[:, at])

    temps = temps_ref[...]
    day = jnp.broadcast_to(day_ref[...].astype(jnp.float32), (8, sites))
    lane1, wide_l = lanes_of(1), lanes_of(levels)
    unused = (lane1 & 3) == 3
    side_temps = jnp.full((levels, LANES), ref_temp, jnp.float32)
    side_day = jnp.zeros((8, LANES), jnp.float32)
    for k in range(count):
        t_here = jnp.where(unused, ref_temp, spread_lanes(temps[:, k * per_row : (k + 1) * per_row]))
        d_here = spread_lanes(day[:, k * per_row : (k + 1) * per_row])
        ntemps_ref[k * levels : (k + 1) * levels, :] = t_here
        nday_ref[8 * k : 8 * k + 8, :] = d_here
        if k:
            side_temps = jnp.where(wide_l == k, pltpu.roll(t_here, k, 1), side_temps)
            side_day = jnp.where(lanes_of(8) == k, pltpu.roll(d_here, k, 1), side_day)
    ntemps_ref[count * levels :, :] = side_temps
    nday_ref[8 * count :, :] = side_day


def inner_columns_kernel(after_ref, iso_ref, sums_ref, den_ref, ntemps_ref, nday_ref, hot_ref, acc_ref, hiso_ref, lhs_ref):
    del after_ref
    size_x, size_y = den_ref.shape
    chans = acc_ref.shape[0]
    levels = chans // 3
    _, node_rows = row_maps(size_x)
    lane1 = lanes_of(1)
    own = ((lane1 & 3) == 3) | (lane1 == 0)
    wide = lanes_of(chans)
    hiso = jnp.full((chans, LANES), 3.0, jnp.float32)
    inv = 1.0 / den_ref[...]
    for k, n in enumerate(node_rows):
        if k == 0:
            continue
        iso = iso_ref[pl.ds(n, chans, stride=size_x), :]
        hiso = jnp.where(wide == k, pltpu.roll(iso, k, 1), hiso)
        gain = jnp.where(own, 0.0, time_step * inv[n : n + 1, :])
        tracers = iso + gain * sums_ref[pl.ds(k * chans, chans), :]
        hi, lo = split(physics(tracers, ntemps_ref[k * levels : (k + 1) * levels, :], nday_ref[8 * k : 8 * k + 1, :]))
        lhs_ref[0:chans, (k - 1) * LANES : k * LANES] = hi
        lhs_ref[chans : 2 * chans, (k - 1) * LANES : k * LANES] = lo
    hiso_ref[...] = hiso
    both = dot(lhs_ref[...], hot_ref[...])
    acc_ref[...] = both[0:chans] + both[chans:]


def edge_columns_kernel(
    n_peers, iso_ref, sums_ref, den_ref, left_ref, acc_ref, pick_ref, ntemps_ref, nday_ref, hiso_ref, low_ref, before_ref, after_ref, *send_refs
):
    del after_ref
    chans, sites = acc_ref.shape
    levels = chans // 3
    size_x = den_ref.shape[0]
    _, node_rows = row_maps(size_x)
    count = len(node_rows)
    per_peer = sites // n_peers
    full, rest = per_peer // LANES, per_peer % LANES
    wide, lane1 = lanes_of(chans), lanes_of(1)
    unused = (lane1 & 3) == 3

    total = sums_ref[0:chans, :] + low_ref[0:chans, :] + jnp.where(wide == 0, before_ref[0:chans, :], 0.0)
    den = den_ref[0:1, :] + low_ref[chans : chans + 1, :] + jnp.where(lane1 == 0, before_ref[chans : chans + 1, :], 0.0)
    iso = iso_ref[pl.ds(0, chans, stride=size_x), :]
    new_row = iso + jnp.where(unused, 0.0, time_step / den) * total
    phys_row = physics(new_row, ntemps_ref[0:levels, :], nday_ref[0:1, :])

    in_use = (lane1 > 0) & (lane1 < count)
    dcol = jnp.where(in_use, left_ref[chans : chans + 1, :] + before_ref[chans : chans + 1, :], 1.0)
    tcol = jnp.where(in_use, left_ref[0:chans, :] + before_ref[0:chans, :], 0.0)
    new_col = hiso_ref[...] + (time_step / dcol) * tcol
    phys_col = physics(new_col, ntemps_ref[count * levels :, :], nday_ref[8 * count : 8 * count + 1, :])

    rhi, rlo = split(phys_row)
    chi, clo = split(phys_col)
    lhs = jnp.concatenate([jnp.concatenate([rhi, chi], axis=1), jnp.concatenate([rlo, clo], axis=1)], axis=0)
    both = dot(lhs, pick_ref[...])
    out = acc_ref[...] + (both[0:chans] + both[chans:])
    for p in range(n_peers):
        for j in range(full):
            t = p * full + j
            send_refs[p][0, j * chans : (j + 1) * chans, :] = out[:, t * LANES : (t + 1) * LANES]
    if rest:
        begin = n_peers * full * LANES
        for t in range(n_peers * rest // LANES):
            block = out[:, begin + t * LANES : begin + (t + 1) * LANES]
            block = jnp.concatenate([block, jnp.zeros((LANES - chans, LANES), jnp.float32)], axis=0).T
            at = t * LANES
            while at < (t + 1) * LANES:
                p, i = at // rest, at % rest
                count = min(rest - i, (t + 1) * LANES - at)
                send_refs[p][0, full * chans + i : full * chans + i + count, :] = block[at - t * LANES : at - t * LANES + count, :]
                at += count


def advance_kernel(iso_ref, sums_ref, den_ref, low_ref, high_ref, before_ref, after_ref, new_ref):
    size_x = den_ref.shape[0]
    chans = low_ref.shape[0] - 8
    shared, _ = row_maps(size_x)
    wide, lane1 = lanes_of(chans), lanes_of(1)
    for n in range(size_x):
        r = shared[n]
        total = sums_ref[pl.ds(r * chans, chans), :]
        den = den_ref[n : n + 1, :]
        for ref, at in ((low_ref, 0), (high_ref, size_x - 1)):
            if n == at:
                total = total + ref[0:chans, :]
                den = den + ref[chans : chans + 1, :]
        for ref, at in ((before_ref, 0), (after_ref, LANES - 1)):
            total = jnp.where(wide == at, total + ref[0:chans, r : r + 1], total)
            den = jnp.where(lane1 == at, den + ref[chans : chans + 1, r : r + 1], den)
        new_ref[pl.ds(n, chans, stride=size_x), :] = iso_ref[pl.ds(n, chans, stride=size_x), :] + (time_step / den) * total


def assemble_kernel(n_peers, paired, *refs):
    if paired:
        *slot_refs, out_hbm, got_ref, out_ref, sems = refs
        for k, ref in enumerate(slot_refs):
            got_ref[pl.ds(peer_of(k, paired), 1), :, :] = ref[...]
    else:
        got_ref, out_hbm, out_ref, sems = refs
    chans, sites = out_ref.shape
    per_peer = sites // n_peers
    full, rest = per_peer // LANES, per_peer % LANES
    lane = lanes_of(chans)
    blocks = [None] * (sites // LANES)

    def place(block, value, low, high):
        old = blocks[block]
        blocks[block] = value if old is None else jnp.where((lane >= low) & (lane < high), value, old)

    for p in range(n_peers):
        for j in range(full):
            begin = p * per_peer + j * LANES
            shift = begin % LANES
            value = got_ref[p, j * chans : (j + 1) * chans, :]
            if shift:
                value = pltpu.roll(value, shift, 1)
            place(begin // LANES, value, shift, LANES)
            if shift:
                place(begin // LANES + 1, value, 0, shift)
    if rest:
        tails = [got_ref[p, full * chans : full * chans + rest, :] for p in range(n_peers)]
        tails = jnp.concatenate(tails, axis=0)
        for t in range(n_peers * rest // LANES):
            block = tails[t * LANES : (t + 1) * LANES, :].T[0:chans, :]
            at = t * LANES
            while at < (t + 1) * LANES:
                p, i = at // rest, at % rest
                count = min(rest - i, (t + 1) * LANES - at)
                column = p * per_peer + full * LANES + i
                place(column // LANES, block, column % LANES, column % LANES + count)
                at += count
    copies = []
    for t, block in enumerate(blocks):
        at = pl.ds(t * LANES, LANES)
        out_ref[:, at] = block
        copies.append(pltpu.make_async_copy(out_ref.at[:, at], out_hbm.at[:, at], sems.at[t]))
        copies[-1].start()
    for c in copies:
        c.wait()


def exchange(slots, paired):
    if not paired:
        return [lax.all_to_all(jnp.concatenate(slots, axis=0), "blk", split_axis=0, concat_axis=0, tiled=True)]
    got = {}
    sent = (4, 5, 6, 7, 2, 3, 1)
    for n, k in enumerate(sent):
        block = slots[k]
        if n >= 5:
            block, got[sent[n - 5]] = lax.optimization_barrier((block, got[sent[n - 5]]))
        got[k] = lax.ppermute(block, "blk", [(j, j ^ k) for j in range(len(slots))])
    return [slots[0]] + [got[k] for k in range(1, len(slots))]


def call(kernel, outs, scratch, name, *args, **more):
    return pl.pallas_call(
        kernel,
        out_shape=outs,
        **more,
        scratch_shapes=scratch,
        name=name,
        compiler_params=pltpu.CompilerParams(vmem_limit_bytes=40 * 1024 * 1024),
    )(*args)


def on_device(
    isotope_ratios,
    advecting_velocity,
    metric_scaling,
    thermal_state,
    outgoing_site_order,
    daytime_indicator,
):
    size_x, size_y = metric_scaling.shape
    levels = isotope_ratios.shape[1]
    chans = 3 * levels
    sites = outgoing_site_order.shape[1]
    n_face, n_blk = lax.axis_size("face"), lax.axis_size("blk")
    shared, node_rows = row_maps(size_x)
    n_rows = shared[-1] + 1
    per_peer = sites // n_blk
    paired = n_blk == 8
    send_rows = chans * (per_peer // LANES) + per_peer % LANES

    def f32(*shape):
        return jax.ShapeDtypeStruct(shape, jnp.float32)

    iso = isotope_ratios.reshape(chans * size_x, size_y)
    wind = advecting_velocity.reshape(2 * levels * size_x, size_y)
    matrix = jnp.asarray(second_dim_matrix(size_y))
    edge = f32(chans + 8, LANES)
    integers = jax.ShapeDtypeStruct((1, sites), jnp.int32)
    bf16 = jnp.bfloat16
    args = (iso, wind, metric_scaling, matrix, thermal_state[0], daytime_indicator, outgoing_site_order)
    iso, wind, metric, matrix, temps, day, order, den, low, high = call(
        edge_rows_kernel,
        (*[jax.ShapeDtypeStruct(x.shape, x.dtype) for x in args], f32(size_x, size_y), edge, edge),
        [pltpu.VMEM((2 * chans, 2 * size_y), bf16)] * 2 + [pltpu.SemaphoreType.DMA((10,))],
        "edge_rows",
        *(pltpu.with_memory_space_constraint(x, pltpu.HBM) for x in args),
        in_specs=[pl.BlockSpec(memory_space=pltpu.HBM)] * len(args),
    )
    face_up = [(i, (i + 1) % n_face) for i in range(n_face)]
    blk_up = [(i, (i + 1) % n_blk) for i in range(n_blk)]
    from_low = lax.ppermute(high, "face", face_up)
    from_high = lax.ppermute(low, "face", [(j, i) for i, j in face_up])
    sums, left, right = call(
        transport_kernel,
        (f32(n_rows * chans, size_y), edge, edge),
        [pltpu.VMEM(((n_rows - 2) * chans, 2 * size_y), bf16)] * 2,
        "transport",
        iso,
        wind,
        metric,
        matrix,
        den,
        low,
        high,
    )
    count = len(node_rows)
    hot, pick, ntemps, nday = call(
        lambda *refs: send_order_kernel(n_blk, paired, *refs),
        (
            jax.ShapeDtypeStruct(((count - 1) * LANES, sites), bf16),
            jax.ShapeDtypeStruct((2 * LANES, sites), bf16),
            f32((count + 1) * levels, LANES),
            f32((count + 1) * 8, LANES),
        ),
        [pltpu.VMEM((n_blk, -(-per_peer // LANES) * LANES), jnp.int32)],
        "send_order",
        temps,
        day,
        order,
    )
    left, right = call(
        lambda *refs: corners_kernel(n_rows, *refs), (f32(chans + 8, LANES),) * 2, [], "corners", nday, left, right, from_low, from_high
    )
    before = lax.ppermute(right, "blk", blk_up)
    after = lax.ppermute(left, "blk", [(j, i) for i, j in blk_up])
    acc, hiso = call(
        inner_columns_kernel,
        (f32(chans, sites), f32(chans, LANES)),
        [pltpu.VMEM((2 * chans, (count - 1) * LANES), bf16)],
        "inner_columns",
        left,
        iso,
        sums,
        den,
        ntemps,
        nday,
        hot,
    )
    slots = call(
        lambda *refs: edge_columns_kernel(n_blk, *refs),
        (f32(1, send_rows, LANES),) * n_blk,
        [],
        "edge_columns",
        iso,
        sums,
        den,
        left,
        acc,
        pick,
        ntemps,
        nday,
        hiso,
        from_low,
        before,
        after,
    )
    got = exchange(slots, paired)
    new = call(advance_kernel, f32(chans * size_x, size_y), [], "advance", iso, sums, den, from_low, from_high, before, after)
    phys = call(
        lambda *refs: assemble_kernel(n_blk, paired, *refs),
        f32(chans, sites),
        ([pltpu.VMEM((n_blk, send_rows, LANES), jnp.float32)] if paired else [])
        + [pltpu.VMEM((chans, sites), jnp.float32), pltpu.SemaphoreType.DMA((sites // LANES,))],
        "assemble",
        *got,
        out_specs=pl.BlockSpec(memory_space=pltpu.HBM),
    )
    return (new.reshape(isotope_ratios.shape), phys.reshape(1, 3, levels, sites))


def solution(mesh):
    placed = (
        P(None, None, "face", "blk"),
        P(None, None, "face", "blk"),
        P("face", "blk"),
        P("face", None, "blk"),
        P("face", "blk"),
        P("face", "blk"),
    )
    return jax.shard_map(
        on_device,
        mesh=mesh,
        in_specs=placed,
        out_specs=(P(None, None, "face", "blk"), P("face", None, None, "blk")),
        check_vma=False,
    )
```

time: 38.3 us -> 32.8 us (0.86)
  the two profiles are of different devices: /device:TPU:11 before, /device:TPU:0 now
where the time goes in v2:
time: 32.8 us; the launch traced here: 32.6 us
  starting transfers between devices  17.9 us (55%)
  Pallas kernels  9.42 us (29%)
  waiting for transfers between devices  4.65 us (14%)
  between operations  0.68 us (2%)
    ppermute x7, starting transfers between devices, exchange(): got[k] = lax.ppermute(block, 'blk', [(j, j ^ k) for j in range(len(slots))])  10.6 us
    pallas_call x8, Pallas kernels, call(): pl.pallas_call(kernel, out_shape=outs, **more, scratch_shapes=scratch, na...  9.42 us
    ppermute x1, starting transfers between devices, on_device(): after = lax.ppermute(left, 'blk', [(j, i) for i, j in blk_up])  3.23 us
    ppermute x7, waiting for transfers between devices, exchange(): got[k] = lax.ppermute(block, 'blk', [(j, j ^ k) for j in range(len(slots))])  3.21 us
    ppermute x1, starting transfers between devices, on_device(): from_high = lax.ppermute(low, 'face', [(j, i) for i, j in face_up])  2.46 us
    ppermute x1, starting transfers between devices, on_device(): before = lax.ppermute(right, 'blk', blk_up)  1.54 us
    ppermute x1, waiting for transfers between devices, on_device(): before = lax.ppermute(right, 'blk', blk_up)  0.82 us
  transfers between devices with their start and end apart: 11, of which 4 were waited for; matrix products, arithmetic and copies ran while one was open for 0% of the time, Pallas kernels for 19%

profile of v2, /device:TPU:0, one launch (start us, length us, event | category | flops | bytes accessed | tf_op | source)
XLA Modules:
  0.0 32.6 jit_solution(17979278526200582214)
XLA Ops:
  0.6 1.8 %edge_rows.1 = (f32[1536,128]{1,0:T(8,128)S(1)}, f32[1024,128]{1,0:T(8,128)S(1)}, f32[16,128]{1,0:T(8,128)S(1)}, bf16[256,256]{1,0:T(8,128)(2,1)S(1)}, f32[32,11...) custom-call(f32[1536,128]{1,0:T(8,128)} %bitcast.5, ...), custom_call_target="tpu_custom_call" | custom-call | tf_op jit(solution)/shard_map/edge_rows/pallas_call | solution.py:504
  2.4 2.5 %collective-permute-start.1 = (f32[104,128]{1,0:T(8,128)S(1)}, f32[104,128]{1,0:T(8,128)S(1)}, u32[]{:S(2)}, u32[]{:S(2)}) collective-permute-start(f32[104,128]{1,0:T(8,128)S(1)} %get-tuple-element.40.low_ref), channel_id=1, source_target_pairs={{8,0},{16,8},{24,16},{0,24},{9,1},{17,9},{25,17},{1,25},{10,2},{18... | collective-permute-start | bytes 159752 | tf_op jit(solution)/shard_map/ppermute | solution.py:554
  4.9 0.0 collective-permute-start
  4.9 1.6 %send_order.1 = (bf16[1408,1152]{1,0:T(8,128)(2,1)S(1)}, bf16[256,1152]{1,0:T(8,128)(2,1)S(1)}, f32[416,128]{1,0:T(8,128)S(1)}, f32[104,128]{1,0:T(8,128)S(1)}) custom-call(f32[32,1152]{1,0:T(8,128)S(1)} %get-tuple-element.43.refs_0_, s32[1,1152]{1,0:T(1,128)S(1)} %get-tuple-element.44.refs_1_, s32[1,1152]{1,0:T(1,128)S(1)} %get-tuple-element.45.refs_2_), custom_call_target="tpu_custom_call" | custom-call | tf_op jit(solution)/shard_map/send_order/pallas_call | solution.py:504
  6.5 1.3 %transport.1 = (f32[1248,128]{1,0:T(8,128)S(1)}, f32[104,128]{1,0:T(8,128)S(1)}, f32[104,128]{1,0:T(8,128)S(1)}) custom-call(f32[1536,128]{1,0:T(8,128)S(1)} %get-tuple-element.35.iso_ref.refs_0_, f32[1024,128]{1,0:T(8,128)S(1)} %get-tuple-element.36.wind_ref, f32[16,128]{1,0:T(8,128)S(1)} %get-tuple-element.37.metric_ref, ...), custom_call_target="tpu_custom_call" | custom-call | tf_op jit(solution)/shard_map/transport/pallas_call | solution.py:504
  7.8 0.0 collective-permute-done.1.refs_4_.high_ref
  7.8 0.6 %collective-permute-done.refs_3_.low_ref.refs_9_ = f32[104,128]{1,0:T(8,128)S(1)} collective-permute-done((f32[104,128]{1,0:T(8,128)S(1)}, f32[104,128]{1,0:T(8,128)S(1)}, u32[]{:S(2)}, u32[]{:S(2)}) %collective-permute-start) | collective-permute-done | bytes 53280 | tf_op jit(solution)/shard_map/ppermute | solution.py:553
  8.4 0.1 corners.1
  8.5 1.5 %collective-permute-start.2 = (f32[104,128]{1,0:T(8,128)S(1)}, f32[104,128]{1,0:T(8,128)S(1)}, u32[]{:S(2)}, u32[]{:S(2)}) collective-permute-start(f32[104,128]{1,0:T(8,128)S(1)} %get-tuple-element.49), channel_id=1, source_target_pairs={{0,1},{1,2},{2,3},{3,4},{4,5},{5,6},{6,7},{7,0},{8,9},{9,10},{10,1... | collective-permute-start | bytes 159752 | tf_op jit(solution)/shard_map/ppermute | solution.py:586
  10.1 3.2 %collective-permute-start.3 = (f32[104,128]{1,0:T(8,128)S(1)}, f32[104,128]{1,0:T(8,128)S(1)}, u32[]{:S(2)}, u32[]{:S(2)}) collective-permute-start(f32[104,128]{1,0:T(8,128)S(1)} %get-tuple-element.50.after_ref.refs_3_), channel_id=1, source_target_pairs={{1,0},{2,1},{3,2},{4,3},{5,4},{6,5},{7,6},{0,7},{9,8},{10,9},{11,1... | collective-permute-start | bytes 159752 | tf_op jit(solution)/shard_map/ppermute | solution.py:587
  13.3 1.3 %inner_columns.1 = (f32[96,1152]{1,0:T(8,128)S(1)}, f32[96,128]{1,0:T(8,128)S(1)}) custom-call(f32[104,128]{1,0:T(8,128)S(1)} %get-tuple-element.50.after_ref.refs_3_, f32[1536,128]{1,0:T(8,128)S(1)} %get-tuple-element.35.iso_ref.refs_0_, f32[1248,128]{1,0:T(8,128)S(1)} %get-tuple-element.42.sums_ref.refs_1_, ...), custom_call_target="tpu_custom_call" | custom-call | tf_op jit(solution)/shard_map/inner_columns/pallas_call | solution.py:504
  14.6 0.8 %collective-permute-done.2.before_ref.refs_10_ = f32[104,128]{1,0:T(8,128)S(1)} collective-permute-done((f32[104,128]{1,0:T(8,128)S(1)}, f32[104,128]{1,0:T(8,128)S(1)}, u32[]{:S(2)}, u32[]{:S(2)}) %collective-permute-start.2) | collective-permute-done | bytes 53280 | tf_op jit(solution)/shard_map/ppermute | solution.py:586
  15.4 0.0 collective-permute-done.3.after_ref.refs_11_
  15.4 0.5 %edge_columns.1 = (f32[1,112,128]{2,1,0:T(8,128)S(1)}, f32[1,112,128]{2,1,0:T(8,128)S(1)}, f32[1,112,128]{2,1,0:T(8,128)S(1)}, f32[1,112,128]{2,1,0:T(8,128)S(1)...) custom-call(f32[1536,128]{1,0:T(8,128)S(1)} %get-tuple-element.35.is, ...), custom_call_target="tpu_custom_call" | custom-call | tf_op jit(solution)/shard_map/edge_columns/pallas_call | solution.py:504
  15.9 3.3 %collective-permute-start.4 = (f32[1,112,128]{2,1,0:T(8,128)S(1)}, f32[1,112,128]{2,1,0:T(8,128)S(1)}, u32[]{:S(2)}, u32[]{:S(2)}) collective-permute-start(f32[1,112,128]{2,1,0:T(8,128)S(1)} %get-tuple-element.58), channel_id=1, source_target_pairs={{0,5},{1,4},{2,7},{3,6},{4,1},{5,0},{6,3},{7,2},{8,13},{9,12},{10,... | collective-permute-start | bytes 172040 | tf_op jit(solution)/shard_map/ppermute | solution.py:499
  19.2 0.3 %collective-permute-start.7 = (f32[1,112,128]{2,1,0:T(8,128)S(1)}, f32[1,112,128]{2,1,0:T(8,128)S(1)}, u32[]{:S(2)}, u32[]{:S(2)}) collective-permute-start(f32[1,112,128]{2,1,0:T(8,128)S(1)} %get-tuple-element.62), channel_id=1, source_target_pairs={{0,4},{1,5},{2,6},{3,7},{4,0},{5,1},{6,2},{7,3},{8,12},{9,13},{10,... | collective-permute-start | bytes 172040 | tf_op jit(solution)/shard_map/ppermute | solution.py:499
  19.5 1.7 %collective-permute-start.6 = (f32[1,112,128]{2,1,0:T(8,128)S(1)}, f32[1,112,128]{2,1,0:T(8,128)S(1)}, u32[]{:S(2)}, u32[]{:S(2)}) collective-permute-start(f32[1,112,128]{2,1,0:T(8,128)S(1)} %get-tuple-element.60), channel_id=1, source_target_pairs={{0,2},{1,3},{2,0},{3,1},{4,6},{5,7},{6,4},{7,5},{8,10},{9,11},{10,... | collective-permute-start | bytes 172040 | tf_op jit(solution)/shard_map/ppermute | solution.py:499
  21.2 2.4 %collective-permute-start.9 = (f32[1,112,128]{2,1,0:T(8,128)S(1)}, f32[1,112,128]{2,1,0:T(8,128)S(1)}, u32[]{:S(2)}, u32[]{:S(2)}) collective-permute-start(f32[1,112,128]{2,1,0:T(8,128)S(1)} %get-tuple-element.66), channel_id=1, source_target_pairs={{0,6},{1,7},{2,4},{3,5},{4,2},{5,3},{6,0},{7,1},{8,14},{9,15},{10,... | collective-permute-start | bytes 172040 | tf_op jit(solution)/shard_map/ppermute | solution.py:499
  23.6 1.5 %collective-permute-start.10 = (f32[1,112,128]{2,1,0:T(8,128)S(1)}, f32[1,112,128]{2,1,0:T(8,128)S(1)}, u32[]{:S(2)}, u32[]{:S(2)}) collective-permute-start(f32[1,112,128]{2,1,0:T(8,128)S(1)} %get-tuple-element.67), channel_id=1, source_target_pairs={{0,7},{1,6},{2,5},{3,4},{4,3},{5,2},{6,1},{7,0},{8,15},{9,14},{10,... | collective-permute-start | bytes 172040 | tf_op jit(solution)/shard_map/ppermute | solution.py:499
  25.1 0.0 collective-permute-done.4.refs_5_
  25.1 1.4 %collective-permute-start.5 = (f32[1,112,128]{2,1,0:T(8,128)S(1)}, f32[1,112,128]{2,1,0:T(8,128)S(1)}, u32[]{:S(2)}, u32[]{:S(2)}) collective-permute-start(f32[1,112,128]{2,1,0:T(8,128)S(1)} %get-tuple-element.59), channel_id=1, source_target_pairs={{0,1},{1,0},{2,3},{3,2},{4,5},{5,4},{6,7},{7,6},{8,9},{9,8},{10,11... | collective-permute-start | bytes 172040 | tf_op jit(solution)/shard_map/ppermute | solution.py:499
  26.5 0.0 collective-permute-done.7.refs_4_
  26.5 0.0 collective-permute-start.8
  26.5 1.9 %advance.1 = f32[1536,128]{1,0:T(8,128)} custom-call(f32[1536,128]{1,0:T(8,128)S(1)} %get-tuple-element.35.iso_ref.refs_0_, f32[1248,128]{1,0:T(8,128)S(1)} %get-tuple-element.42.sums_ref.refs_1_, f32[16,128]{1,0:T(8,128)S(1)} %get-tuple-element.39.den_ref.refs_2_, f32[104,128]{1,0:T(8,128)S(1)} %collective-permute-done.refs_3_.low_ref.refs_9_, ...), custom_call_target="tpu_custom_call" | custom-call | tf_op jit(solution)/shard_map/advance/pallas_call | solution.py:504
  28.4 0.0 collective-permute-done.6.refs_2_
  28.4 0.0 collective-permute-done.9.refs_6_
  28.4 2.1 %collective-permute-done.10.refs_7_ = f32[1,112,128]{2,1,0:T(8,128)S(1)} collective-permute-done((f32[1,112,128]{2,1,0:T(8,128)S(1)}, f32[1,112,128]{2,1,0:T(8,128)S(1)}, u32[]{:S(2)}, u32[]{:S(2)}) %collective-permute-start.10) | collective-permute-done | bytes 57376 | tf_op jit(solution)/shard_map/ppermute | solution.py:499
  30.5 0.0 collective-permute-done.5.refs_1_
  30.5 1.1 %collective-permute-done.8.refs_3_ = f32[1,112,128]{2,1,0:T(8,128)S(1)} collective-permute-done((f32[1,112,128]{2,1,0:T(8,128)S(1)}, f32[1,112,128]{2,1,0:T(8,128)S(1)}, u32[]{:S(2)}, u32[]{:S(2)}) %collective-permute-start.8) | collective-permute-done | bytes 57376 | tf_op jit(solution)/shard_map/ppermute | solution.py:499
  31.6 1.0 %assemble.1 = f32[96,1152]{1,0:T(8,128)} custom-call(f32[1,112,128]{2,1,0:T(8,128)S(1)} %get-tuple-element.56.refs_0_, f32[1,112,128]{2,1,0:T(8,128)S(1)} %collective-permute-done.5.refs_1_, f32[1,112,128]{2,1,0:T(8,128)S(1)} %collective-permute-done.6.refs_2_, f32[1,112,128]{2,1,0:T(8,128)S(1)} %collective-permute-done.8.refs_3_, ...), custom_call_target="tpu_custom_call" | custom-call | tf_op jit(solution)/shard_map/assemble/pallas_call | solution.py:504
Async XLA Ops:
  2.4 5.4 %collective-permute-start.1 = (f32[104,128]{1,0:T(8,128)S(1)}, f32[104,128]{1,0:T(8,128)S(1)}, u32[]{:S(2)}, u32[]{:S(2)}) collective-permute-start(f32[104,128]{1,0:T(8,128)S(1)} %get-tuple-element.40.low_ref), channel_id=1, source_target_pairs={{8,0},{16,8},{24,16},{0,24},{9,1},{17,9},{25,17},{1,25},{10,2},{18... | collective-permute-start | bytes 159752 | tf_op jit(solution)/shard_map/ppermute | solution.py:554
  4.9 3.6 %collective-permute-start = (f32[104,128]{1,0:T(8,128)S(1)}, f32[104,128]{1,0:T(8,128)S(1)}, u32[]{:S(2)}, u32[]{:S(2)}) collective-permute-start(f32[104,128]{1,0:T(8,128)S(1)} %get-tuple-element.41.high_ref), channel_id=1, source_target_pairs={{0,8},{8,16},{16,24},{24,0},{1,9},{9,17},{17,25},{25,1},{2,10},{10... | collective-permute-start | bytes 159752 | tf_op jit(solution)/shard_map/ppermute | solution.py:553
  8.5 6.9 %collective-permute-start.2 = (f32[104,128]{1,0:T(8,128)S(1)}, f32[104,128]{1,0:T(8,128)S(1)}, u32[]{:S(2)}, u32[]{:S(2)}) collective-permute-start(f32[104,128]{1,0:T(8,128)S(1)} %get-tuple-element.49), channel_id=1, source_target_pairs={{0,1},{1,2},{2,3},{3,4},{4,5},{5,6},{6,7},{7,0},{8,9},{9,10},{10,1... | collective-permute-start | bytes 159752 | tf_op jit(solution)/shard_map/ppermute | solution.py:586
  10.1 5.3 %collective-permute-start.3 = (f32[104,128]{1,0:T(8,128)S(1)}, f32[104,128]{1,0:T(8,128)S(1)}, u32[]{:S(2)}, u32[]{:S(2)}) collective-permute-start(f32[104,128]{1,0:T(8,128)S(1)} %get-tuple-element.50.after_ref.refs_3_), channel_id=1, source_target_pairs={{1,0},{2,1},{3,2},{4,3},{5,4},{6,5},{7,6},{0,7},{9,8},{10,9},{11,1... | collective-permute-start | bytes 159752 | tf_op jit(solution)/shard_map/ppermute | solution.py:587
  15.9 9.2 %collective-permute-start.4 = (f32[1,112,128]{2,1,0:T(8,128)S(1)}, f32[1,112,128]{2,1,0:T(8,128)S(1)}, u32[]{:S(2)}, u32[]{:S(2)}) collective-permute-start(f32[1,112,128]{2,1,0:T(8,128)S(1)} %get-tuple-element.58), channel_id=1, source_target_pairs={{0,5},{1,4},{2,7},{3,6},{4,1},{5,0},{6,3},{7,2},{8,13},{9,12},{10,... | collective-permute-start | bytes 172040 | tf_op jit(solution)/shard_map/ppermute | solution.py:499
  19.2 7.3 %collective-permute-start.7 = (f32[1,112,128]{2,1,0:T(8,128)S(1)}, f32[1,112,128]{2,1,0:T(8,128)S(1)}, u32[]{:S(2)}, u32[]{:S(2)}) collective-permute-start(f32[1,112,128]{2,1,0:T(8,128)S(1)} %get-tuple-element.62), channel_id=1, source_target_pairs={{0,4},{1,5},{2,6},{3,7},{4,0},{5,1},{6,2},{7,3},{8,12},{9,13},{10,... | collective-permute-start | bytes 172040 | tf_op jit(solution)/shard_map/ppermute | solution.py:499
  19.5 8.8 %collective-permute-start.6 = (f32[1,112,128]{2,1,0:T(8,128)S(1)}, f32[1,112,128]{2,1,0:T(8,128)S(1)}, u32[]{:S(2)}, u32[]{:S(2)}) collective-permute-start(f32[1,112,128]{2,1,0:T(8,128)S(1)} %get-tuple-element.60), channel_id=1, source_target_pairs={{0,2},{1,3},{2,0},{3,1},{4,6},{5,7},{6,4},{7,5},{8,10},{9,11},{10,... | collective-permute-start | bytes 172040 | tf_op jit(solution)/shard_map/ppermute | solution.py:499
  21.2 7.2 %collective-permute-start.9 = (f32[1,112,128]{2,1,0:T(8,128)S(1)}, f32[1,112,128]{2,1,0:T(8,128)S(1)}, u32[]{:S(2)}, u32[]{:S(2)}) collective-permute-start(f32[1,112,128]{2,1,0:T(8,128)S(1)} %get-tuple-element.66), channel_id=1, source_target_pairs={{0,6},{1,7},{2,4},{3,5},{4,2},{5,3},{6,0},{7,1},{8,14},{9,15},{10,... | collective-permute-start | bytes 172040 | tf_op jit(solution)/shard_map/ppermute | solution.py:499
  23.6 6.9 %collective-permute-start.10 = (f32[1,112,128]{2,1,0:T(8,128)S(1)}, f32[1,112,128]{2,1,0:T(8,128)S(1)}, u32[]{:S(2)}, u32[]{:S(2)}) collective-permute-start(f32[1,112,128]{2,1,0:T(8,128)S(1)} %get-tuple-element.67), channel_id=1, source_target_pairs={{0,7},{1,6},{2,5},{3,4},{4,3},{5,2},{6,1},{7,0},{8,15},{9,14},{10,... | collective-permute-start | bytes 172040 | tf_op jit(solution)/shard_map/ppermute | solution.py:499
  25.1 5.3 %collective-permute-start.5 = (f32[1,112,128]{2,1,0:T(8,128)S(1)}, f32[1,112,128]{2,1,0:T(8,128)S(1)}, u32[]{:S(2)}, u32[]{:S(2)}) collective-permute-start(f32[1,112,128]{2,1,0:T(8,128)S(1)} %get-tuple-element.59), channel_id=1, source_target_pairs={{0,1},{1,0},{2,3},{3,2},{4,5},{5,4},{6,7},{7,6},{8,9},{9,8},{10,11... | collective-permute-start | bytes 172040 | tf_op jit(solution)/shard_map/ppermute | solution.py:499
  26.5 5.1 %collective-permute-start.8 = (f32[1,112,128]{2,1,0:T(8,128)S(1)}, f32[1,112,128]{2,1,0:T(8,128)S(1)}, u32[]{:S(2)}, u32[]{:S(2)}) collective-permute-start(f32[1,112,128]{2,1,0:T(8,128)S(1)} %get-tuple-element.63), channel_id=1, source_target_pairs={{0,3},{1,2},{2,1},{3,0},{4,7},{5,6},{6,5},{7,4},{8,11},{9,10},{10,... | collective-permute-start | bytes 172040 | tf_op jit(solution)/shard_map/ppermute | solution.py:499

commit v3 on v2

--- a/solution.py
+++ b/solution.py
@@ -15,6 +15,7 @@
 clausius = 0.07
 ref_temp = 280.0
 LANES = 128
+SENT = (4, 7, 5, 3, 1, 6, 2)
 
 
 def gll_tables():
@@ -278,6 +279,10 @@
     return lax.axis_index("blk") ^ slot if paired else slot
 
 
+def carriers(n_peers):
+    return sorted({j ^ ((j - 1) % n_peers) for j in range(n_peers)})
+
+
 def third(x):
     return lax.shift_right_logical(x * 43691, 17)
 
@@ -372,9 +377,8 @@
 
 
 def edge_columns_kernel(
-    n_peers, iso_ref, sums_ref, den_ref, left_ref, acc_ref, pick_ref, ntemps_ref, nday_ref, hiso_ref, low_ref, before_ref, after_ref, *send_refs
+    n_peers, paired, iso_ref, sums_ref, den_ref, left_ref, acc_ref, pick_ref, ntemps_ref, nday_ref, hiso_ref, low_ref, before_ref, *send_refs
 ):
-    del after_ref
     chans, sites = acc_ref.shape
     levels = chans // 3
     size_x = den_ref.shape[0]
@@ -419,30 +423,67 @@
                 at += count
 
 
-def advance_kernel(iso_ref, sums_ref, den_ref, low_ref, high_ref, before_ref, after_ref, new_ref):
+    if paired:
+        pad = jnp.zeros((LANES - left_ref.shape[0], LANES), jnp.float32)
+        turned = jnp.concatenate([left_ref[...], pad], axis=0).T
+        for k in carriers(n_peers):
+            rows = send_refs[k].shape[1] - send_refs[0].shape[1]
+            send_refs[k][0, send_refs[0].shape[1] :, :] = turned[0:rows, :]
+
+
+def advance_kernel(n_peers, paired, carried, iso_ref, sums_ref, den_ref, low_ref, high_ref, before_ref, *rest):
+    *after_refs, new_hbm, after_ref, new_ref, sems = rest
     size_x = den_ref.shape[0]
     chans = low_ref.shape[0] - 8
     shared, _ = row_maps(size_x)
-    wide, lane1 = lanes_of(chans), lanes_of(1)
+    lane1 = lanes_of(1)
+    if paired:
+        me = lax.axis_index("blk")
+        mine = me ^ lax.rem(me + 1, n_peers)
+        turned = jnp.zeros((carried, LANES), jnp.float32)
+        for k, ref in zip(carriers(n_peers), after_refs):
+            turned = jnp.where(mine == k, ref[0, ref.shape[1] - carried :, :], turned)
+        pad = jnp.zeros((LANES - carried, LANES), jnp.float32)
+        after_ref[...] = jnp.concatenate([turned, pad], axis=0).T[0 : chans + 8, :]
+    else:
+        after_ref[...] = after_refs[0][...]
+    gains = []
     for n in range(size_x):
-        r = shared[n]
-        total = sums_ref[pl.ds(r * chans, chans), :]
         den = den_ref[n : n + 1, :]
         for ref, at in ((low_ref, 0), (high_ref, size_x - 1)):
             if n == at:
-                total = total + ref[0:chans, :]
                 den = den + ref[chans : chans + 1, :]
         for ref, at in ((before_ref, 0), (after_ref, LANES - 1)):
-            total = jnp.where(wide == at, total + ref[0:chans, r : r + 1], total)
-            den = jnp.where(lane1 == at, den + ref[chans : chans + 1, r : r + 1], den)
-        new_ref[pl.ds(n, chans, stride=size_x), :] = iso_ref[pl.ds(n, chans, stride=size_x), :] + (time_step / den) * total
+            den = jnp.where(lane1 == at, den + ref[chans : chans + 1, shared[n] : shared[n] + 1], den)
+        gains.append(time_step / den)
+    levels = chans // 3
+    part = levels * size_x
+    wide = lanes_of(levels)
+    copies = []
+    for s in range(3):
+        for n in range(size_x):
+            r = shared[n]
+            total = sums_ref[pl.ds(r * chans + s * levels, levels), :]
+            at_s = pl.ds(s * levels, levels)
+            for ref, at in ((low_ref, 0), (high_ref, size_x - 1)):
+                if n == at:
+                    total = total + ref[at_s, :]
+            for ref, at in ((before_ref, 0), (after_ref, LANES - 1)):
+                total = jnp.where(wide == at, total + ref[at_s, r : r + 1], total)
+            here = pl.ds(s * part + n, levels, stride=size_x)
+            new_ref[here, :] = iso_ref[here, :] + gains[n] * total
+        done = pl.ds(s * part, part)
+        copies.append(pltpu.make_async_copy(new_ref.at[done], new_hbm.at[done], sems.at[s]))
+        copies[-1].start()
+    for c in copies:
+        c.wait()
 
 
 def assemble_kernel(n_peers, paired, *refs):
     if paired:
         *slot_refs, out_hbm, got_ref, out_ref, sems = refs
         for k, ref in enumerate(slot_refs):
-            got_ref[pl.ds(peer_of(k, paired), 1), :, :] = ref[...]
+            got_ref[pl.ds(peer_of(k, paired), 1), :, :] = ref[:, 0 : got_ref.shape[1], :]
     else:
         got_ref, out_hbm, out_ref, sems = refs
     chans, sites = out_ref.shape
@@ -487,17 +528,20 @@
         c.wait()
 
 
-def exchange(slots, paired):
+def exchange(slots, left, paired):
+    n_peers = lax.axis_size("blk")
     if not paired:
-        return [lax.all_to_all(jnp.concatenate(slots, axis=0), "blk", split_axis=0, concat_axis=0, tiled=True)]
-    got = {}
-    sent = (4, 5, 6, 7, 2, 3, 1)
+        got = lax.all_to_all(jnp.concatenate(slots, axis=0), "blk", split_axis=0, concat_axis=0, tiled=True)
+        return [got], [lax.ppermute(left, "blk", [((j + 1) % n_peers, j) for j in range(n_peers)])]
+    got = []
+    sent = SENT
     for n, k in enumerate(sent):
         block = slots[k]
         if n >= 5:
-            block, got[sent[n - 5]] = lax.optimization_barrier((block, got[sent[n - 5]]))
-        got[k] = lax.ppermute(block, "blk", [(j, j ^ k) for j in range(len(slots))])
-    return [slots[0]] + [got[k] for k in range(1, len(slots))]
+            block, got[n - 5] = lax.optimization_barrier((block, got[n - 5]))
+        got.append(lax.ppermute(block, "blk", [(j, j ^ k) for j in range(n_peers)]))
+    got = [slots[0]] + [got[sent.index(k)] for k in range(1, n_peers)]
+    return got, [got[k] for k in carriers(n_peers)]
 
 
 def call(kernel, outs, scratch, name, *args, **more):
@@ -528,6 +572,7 @@
     n_rows = shared[-1] + 1
     per_peer = sites // n_blk
     paired = n_blk == 8
+    carried = -(-n_rows // 8) * 8
     send_rows = chans * (per_peer // LANES) + per_peer % LANES
 
     def f32(*shape):
@@ -584,7 +629,6 @@
         lambda *refs: corners_kernel(n_rows, *refs), (f32(chans + 8, LANES),) * 2, [], "corners", nday, left, right, from_low, from_high
     )
     before = lax.ppermute(right, "blk", blk_up)
-    after = lax.ppermute(left, "blk", [(j, i) for i, j in blk_up])
     acc, hiso = call(
         inner_columns_kernel,
         (f32(chans, sites), f32(chans, LANES)),
@@ -599,8 +643,8 @@
         hot,
     )
     slots = call(
-        lambda *refs: edge_columns_kernel(n_blk, *refs),
-        (f32(1, send_rows, LANES),) * n_blk,
+        lambda *refs: edge_columns_kernel(n_blk, paired, *refs),
+        [f32(1, send_rows + (carried if paired and k in carriers(n_blk) else 0), LANES) for k in range(n_blk)],
         [],
         "edge_columns",
         iso,
@@ -614,10 +658,22 @@
         hiso,
         from_low,
         before,
-        after,
-    )
-    got = exchange(slots, paired)
-    new = call(advance_kernel, f32(chans * size_x, size_y), [], "advance", iso, sums, den, from_low, from_high, before, after)
+    )
+    got, after = exchange(slots, left, paired)
+    new = call(
+        lambda *refs: advance_kernel(n_blk, paired, carried, *refs),
+        f32(chans * size_x, size_y),
+        [pltpu.VMEM((chans + 8, LANES), jnp.float32), pltpu.VMEM((chans * size_x, size_y), jnp.float32), pltpu.SemaphoreType.DMA((3,))],
+        "advance",
+        iso,
+        sums,
+        den,
+        from_low,
+        from_high,
+        before,
+        *after,
+        out_specs=pl.BlockSpec(memory_space=pltpu.HBM),
+    )
     phys = call(
         lambda *refs: assemble_kernel(n_blk, paired, *refs),
         f32(chans, sites),

time: 32.8 us -> 30.9 us (0.942)
  starting transfers between devices: 17.9 us -> 14.1 us
  waiting for transfers between devices: 4.65 us -> 6.52 us
    ppermute x8 -> x7, starting transfers between devices: 13.9 us -> 10.1 us  [exchange(): got.append(lax.ppermute(block, 'blk', [(j, j ^ k) for j in range(n_peers)]))]
    ppermute x1, waiting for transfers between devices: 0.82 us -> 4.05 us  [on_device(): before = lax.ppermute(right, 'blk', blk_up)]
    ppermute x8 -> x7, waiting for transfers between devices: 3.22 us -> 1.85 us  [exchange(): got.append(lax.ppermute(block, 'blk', [(j, j ^ k) for j in range(n_peers)]))]
  transfers between devices with their start and end apart: 11 -> 10, of which waited for: 4 -> 6; matrix products, arithmetic and copies ran while one was open for 0% -> 0% of each run, Pallas kernels for 19% -> 19%
where the time goes in v3:
time: 30.9 us; the launch traced here: 30.6 us
  starting transfers between devices  14.1 us (46%)
  Pallas kernels  9.21 us (30%)
  waiting for transfers between devices  6.52 us (21%)
  between operations  0.69 us (2%)
    ppermute x7, starting transfers between devices, exchange(): got.append(lax.ppermute(block, 'blk', [(j, j ^ k) for j in range(n_peers)]))  10.1 us
    pallas_call x8, Pallas kernels, call(): pl.pallas_call(kernel, out_shape=outs, **more, scratch_shapes=scratch, na...  9.21 us
    ppermute x1, waiting for transfers between devices, on_device(): before = lax.ppermute(right, 'blk', blk_up)  4.05 us
    ppermute x1, starting transfers between devices, on_device(): from_high = lax.ppermute(low, 'face', [(j, i) for i, j in face_up])  2.46 us
    ppermute x7, waiting for transfers between devices, exchange(): got.append(lax.ppermute(block, 'blk', [(j, j ^ k) for j in range(n_peers)]))  1.85 us
    ppermute x1, starting transfers between devices, on_device(): before = lax.ppermute(right, 'blk', blk_up)  1.54 us
  transfers between devices with their start and end apart: 10, of which 6 were waited for; matrix products, arithmetic and copies ran while one was open for 0% of the time, Pallas kernels for 19%

profile of v3, /device:TPU:0, one launch (start us, length us, event | category | flops | bytes accessed | tf_op | source)
XLA Modules:
  0.0 30.6 jit_solution(6601057371388046192)
XLA Ops:
  0.6 1.8 %edge_rows.1 = (f32[1536,128]{1,0:T(8,128)S(1)}, f32[1024,128]{1,0:T(8,128)S(1)}, f32[16,128]{1,0:T(8,128)S(1)}, bf16[256,256]{1,0:T(8,128)(2,1)S(1)}, f32[32,11...) custom-call(f32[1536,128]{1,0:T(8,128)} %bitcast.5, ...), custom_call_target="tpu_custom_call" | custom-call | tf_op jit(solution)/shard_map/edge_rows/pallas_call | solution.py:548
  2.4 2.5 %collective-permute-start.1 = (f32[104,128]{1,0:T(8,128)S(1)}, f32[104,128]{1,0:T(8,128)S(1)}, u32[]{:S(2)}, u32[]{:S(2)}) collective-permute-start(f32[104,128]{1,0:T(8,128)S(1)} %get-tuple-element.40.low_ref), channel_id=1, source_target_pairs={{8,0},{16,8},{24,16},{0,24},{9,1},{17,9},{25,17},{1,25},{10,2},{18... | collective-permute-start | bytes 159752 | tf_op jit(solution)/shard_map/ppermute | solution.py:599
  4.9 0.0 collective-permute-start
  4.9 1.6 %send_order.1 = (bf16[1408,1152]{1,0:T(8,128)(2,1)S(1)}, bf16[256,1152]{1,0:T(8,128)(2,1)S(1)}, f32[416,128]{1,0:T(8,128)S(1)}, f32[104,128]{1,0:T(8,128)S(1)}) custom-call(f32[32,1152]{1,0:T(8,128)S(1)} %get-tuple-element.43.refs_0_, s32[1,1152]{1,0:T(1,128)S(1)} %get-tuple-element.44.refs_1_, s32[1,1152]{1,0:T(1,128)S(1)} %get-tuple-element.45.refs_2_), custom_call_target="tpu_custom_call" | custom-call | tf_op jit(solution)/shard_map/send_order/pallas_call | solution.py:548
  6.5 1.3 %transport.1 = (f32[1248,128]{1,0:T(8,128)S(1)}, f32[104,128]{1,0:T(8,128)S(1)}, f32[104,128]{1,0:T(8,128)S(1)}) custom-call(f32[1536,128]{1,0:T(8,128)S(1)} %get-tuple-element.35.iso_ref.refs_0_, f32[1024,128]{1,0:T(8,128)S(1)} %get-tuple-element.36.wind_ref, f32[16,128]{1,0:T(8,128)S(1)} %get-tuple-element.37.metric_ref, ...), custom_call_target="tpu_custom_call" | custom-call | tf_op jit(solution)/shard_map/transport/pallas_call | solution.py:548
  7.8 0.0 collective-permute-done.1.refs_4_
  7.8 0.6 %collective-permute-done.refs_3_.refs_9_ = f32[104,128]{1,0:T(8,128)S(1)} collective-permute-done((f32[104,128]{1,0:T(8,128)S(1)}, f32[104,128]{1,0:T(8,128)S(1)}, u32[]{:S(2)}, u32[]{:S(2)}) %collective-permute-start) | collective-permute-done | bytes 53280 | tf_op jit(solution)/shard_map/ppermute | solution.py:598
  8.4 0.1 corners.1
  8.5 1.5 %collective-permute-start.2 = (f32[104,128]{1,0:T(8,128)S(1)}, f32[104,128]{1,0:T(8,128)S(1)}, u32[]{:S(2)}, u32[]{:S(2)}) collective-permute-start(f32[104,128]{1,0:T(8,128)S(1)} %get-tuple-element.49), channel_id=1, source_target_pairs={{0,1},{1,2},{2,3},{3,4},{4,5},{5,6},{6,7},{7,0},{8,9},{9,10},{10,1... | collective-permute-start | bytes 159752 | tf_op jit(solution)/shard_map/ppermute | solution.py:631
  10.1 1.3 %inner_columns.1 = (f32[96,1152]{1,0:T(8,128)S(1)}, f32[96,128]{1,0:T(8,128)S(1)}) custom-call(f32[104,128]{1,0:T(8,128)S(1)} %get-tuple-element.50.after_ref.refs_3_, f32[1536,128]{1,0:T(8,128)S(1)} %get-tuple-element.35.iso_ref.refs_0_, f32[1248,128]{1,0:T(8,128)S(1)} %get-tuple-element.42.sums_ref.refs_1_, ...), custom_call_target="tpu_custom_call" | custom-call | tf_op jit(solution)/shard_map/inner_columns/pallas_call | solution.py:548
  11.4 4.1 %collective-permute-done.2.refs_10_.refs_5_ = f32[104,128]{1,0:T(8,128)S(1)} collective-permute-done((f32[104,128]{1,0:T(8,128)S(1)}, f32[104,128]{1,0:T(8,128)S(1)}, u32[]{:S(2)}, u32[]{:S(2)}) %collective-permute-start.2) | collective-permute-done | bytes 53280 | tf_op jit(solution)/shard_map/ppermute | solution.py:631
  15.4 0.4 %edge_columns.1 = (f32[1,112,128]{2,1,0:T(8,128)S(1)}, f32[1,128,128]{2,1,0:T(8,128)S(1)}, f32[1,112,128]{2,1,0:T(8,128)S(1)}, f32[1,128,128]{2,1,0:T(8,128)S(1)...) custom-call(f32[1536,128]{1,0:T(8,128)S(1)} %get-tuple-element.35.is, ...), custom_call_target="tpu_custom_call" | custom-call | tf_op jit(solution)/shard_map/edge_columns/pallas_call | solution.py:548
  15.9 1.9 %collective-permute-start.5 = (f32[1,128,128]{2,1,0:T(8,128)S(1)}, f32[1,128,128]{2,1,0:T(8,128)S(1)}, u32[]{:S(2)}, u32[]{:S(2)}) collective-permute-start(f32[1,128,128]{2,1,0:T(8,128)S(1)} %get-tuple-element.59), channel_id=1, source_target_pairs={{0,7},{1,6},{2,5},{3,4},{4,3},{5,2},{6,1},{7,0},{8,15},{9,14},{10,... | collective-permute-start | bytes 196616 | tf_op jit(solution)/shard_map/ppermute | solution.py:542
  17.8 0.0 collective-permute-start.7
  17.8 1.4 %collective-permute-start.3 = (f32[1,128,128]{2,1,0:T(8,128)S(1)}, f32[1,128,128]{2,1,0:T(8,128)S(1)}, u32[]{:S(2)}, u32[]{:S(2)}) collective-permute-start(f32[1,128,128]{2,1,0:T(8,128)S(1)} %get-tuple-element.56), channel_id=1, source_target_pairs={{0,1},{1,0},{2,3},{3,2},{4,5},{5,4},{6,7},{7,6},{8,9},{9,8},{10,11... | collective-permute-start | bytes 196616 | tf_op jit(solution)/shard_map/ppermute | solution.py:542
  19.2 2.0 %collective-permute-start.4 = (f32[1,128,128]{2,1,0:T(8,128)S(1)}, f32[1,128,128]{2,1,0:T(8,128)S(1)}, u32[]{:S(2)}, u32[]{:S(2)}) collective-permute-start(f32[1,128,128]{2,1,0:T(8,128)S(1)} %get-tuple-element.57), channel_id=1, source_target_pairs={{0,3},{1,2},{2,1},{3,0},{4,7},{5,6},{6,5},{7,4},{8,11},{9,10},{10,... | collective-permute-start | bytes 196616 | tf_op jit(solution)/shard_map/ppermute | solution.py:542
  21.2 1.5 %collective-permute-start.8 = (f32[1,112,128]{2,1,0:T(8,128)S(1)}, f32[1,112,128]{2,1,0:T(8,128)S(1)}, u32[]{:S(2)}, u32[]{:S(2)}) collective-permute-start(f32[1,112,128]{2,1,0:T(8,128)S(1)} %get-tuple-element.66), channel_id=1, source_target_pairs={{0,5},{1,4},{2,7},{3,6},{4,1},{5,0},{6,3},{7,2},{8,13},{9,12},{10,... | collective-permute-start | bytes 172040 | tf_op jit(solution)/shard_map/ppermute | solution.py:542
  22.7 0.2 collective-permute-done.7.refs_4_
  22.8 2.2 %collective-permute-start.9 = (f32[1,112,128]{2,1,0:T(8,128)S(1)}, f32[1,112,128]{2,1,0:T(8,128)S(1)}, u32[]{:S(2)}, u32[]{:S(2)}) collective-permute-start(f32[1,112,128]{2,1,0:T(8,128)S(1)} %get-tuple-element.67), channel_id=1, source_target_pairs={{0,6},{1,7},{2,4},{3,5},{4,2},{5,3},{6,0},{7,1},{8,14},{9,15},{10,... | collective-permute-start | bytes 172040 | tf_op jit(solution)/shard_map/ppermute | solution.py:542
  25.1 0.0 collective-permute-done.5.refs_8_.refs_7_
  25.1 1.1 %collective-permute-start.6 = (f32[1,112,128]{2,1,0:T(8,128)S(1)}, f32[1,112,128]{2,1,0:T(8,128)S(1)}, u32[]{:S(2)}, u32[]{:S(2)}) collective-permute-start(f32[1,112,128]{2,1,0:T(8,128)S(1)} %get-tuple-element.62), channel_id=1, source_target_pairs={{0,2},{1,3},{2,0},{3,1},{4,6},{5,7},{6,4},{7,5},{8,10},{9,11},{10,... | collective-permute-start | bytes 172040 | tf_op jit(solution)/shard_map/ppermute | solution.py:542
  26.2 0.0 collective-permute-done.3.refs_6_.refs_1_
  26.2 0.0 collective-permute-done.4.refs_7_.refs_3_
  26.2 1.7 %advance.1 = f32[1536,128]{1,0:T(8,128)} custom-call(f32[1536,128]{1,0:T(8,128)S(1)} %get-tuple-element.35.iso_ref.refs_0_, f32[1248,128]{1,0:T(8,128)S(1)} %get-tuple-element.42.sums_ref.refs_1_, f32[16,128]{1,0:T(8,128)S(1)} %get-tuple-element.39.den_ref.refs_2_, f32[104,128]{1,0:T(8,128)S(1)} %collective-permute-done.refs_3_.refs_9_, ...), custom_call_target="tpu_custom_call" | custom-call | tf_op jit(solution)/shard_map/advance/pallas_call | solution.py:548
  27.9 0.6 %collective-permute-done.8.refs_5_ = f32[1,112,128]{2,1,0:T(8,128)S(1)} collective-permute-done((f32[1,112,128]{2,1,0:T(8,128)S(1)}, f32[1,112,128]{2,1,0:T(8,128)S(1)}, u32[]{:S(2)}, u32[]{:S(2)}) %collective-permute-start.8) | collective-permute-done | bytes 57376 | tf_op jit(solution)/shard_map/ppermute | solution.py:542
  28.5 0.5 %collective-permute-done.9.refs_6_ = f32[1,112,128]{2,1,0:T(8,128)S(1)} collective-permute-done((f32[1,112,128]{2,1,0:T(8,128)S(1)}, f32[1,112,128]{2,1,0:T(8,128)S(1)}, u32[]{:S(2)}, u32[]{:S(2)}) %collective-permute-start.9) | collective-permute-done | bytes 57376 | tf_op jit(solution)/shard_map/ppermute | solution.py:542
  28.9 0.6 %collective-permute-done.6.refs_2_ = f32[1,112,128]{2,1,0:T(8,128)S(1)} collective-permute-done((f32[1,112,128]{2,1,0:T(8,128)S(1)}, f32[1,112,128]{2,1,0:T(8,128)S(1)}, u32[]{:S(2)}, u32[]{:S(2)}) %collective-permute-start.6) | collective-permute-done | bytes 57376 | tf_op jit(solution)/shard_map/ppermute | solution.py:542
  29.5 1.0 %assemble.1 = f32[96,1152]{1,0:T(8,128)} custom-call(f32[1,112,128]{2,1,0:T(8,128)S(1)} %get-tuple-element.61.refs_0_, f32[1,128,128]{2,1,0:T(8,128)S(1)} %collective-permute-done.3.refs_6_.refs_1_, f32[1,112,128]{2,1,0:T(8,128)S(1)} %collective-permute-done.6.refs_2_, f32[1,128,128]{2,1,0:T(8,128)S(1)} %collective-permute-done.4.refs_7_.refs_3_, ...), custom_call_target="tpu_custom_call" | custom-call | tf_op jit(solution)/shard_map/assemble/pallas_call | solution.py:548
Async XLA Ops:
  2.4 5.4 %collective-permute-start.1 = (f32[104,128]{1,0:T(8,128)S(1)}, f32[104,128]{1,0:T(8,128)S(1)}, u32[]{:S(2)}, u32[]{:S(2)}) collective-permute-start(f32[104,128]{1,0:T(8,128)S(1)} %get-tuple-element.40.low_ref), channel_id=1, source_target_pairs={{8,0},{16,8},{24,16},{0,24},{9,1},{17,9},{25,17},{1,25},{10,2},{18... | collective-permute-start | bytes 159752 | tf_op jit(solution)/shard_map/ppermute | solution.py:599
  4.9 3.6 %collective-permute-start = (f32[104,128]{1,0:T(8,128)S(1)}, f32[104,128]{1,0:T(8,128)S(1)}, u32[]{:S(2)}, u32[]{:S(2)}) collective-permute-start(f32[104,128]{1,0:T(8,128)S(1)} %get-tuple-element.41.high_ref), channel_id=1, source_target_pairs={{0,8},{8,16},{16,24},{24,0},{1,9},{9,17},{17,25},{25,1},{2,10},{10... | collective-permute-start | bytes 159752 | tf_op jit(solution)/shard_map/ppermute | solution.py:598
  8.5 6.9 %collective-permute-start.2 = (f32[104,128]{1,0:T(8,128)S(1)}, f32[104,128]{1,0:T(8,128)S(1)}, u32[]{:S(2)}, u32[]{:S(2)}) collective-permute-start(f32[104,128]{1,0:T(8,128)S(1)} %get-tuple-element.49), channel_id=1, source_target_pairs={{0,1},{1,2},{2,3},{3,4},{4,5},{5,6},{6,7},{7,0},{8,9},{9,10},{10,1... | collective-permute-start | bytes 159752 | tf_op jit(solution)/shard_map/ppermute | solution.py:631
  15.9 9.2 %collective-permute-start.5 = (f32[1,128,128]{2,1,0:T(8,128)S(1)}, f32[1,128,128]{2,1,0:T(8,128)S(1)}, u32[]{:S(2)}, u32[]{:S(2)}) collective-permute-start(f32[1,128,128]{2,1,0:T(8,128)S(1)} %get-tuple-element.59), channel_id=1, source_target_pairs={{0,7},{1,6},{2,5},{3,4},{4,3},{5,2},{6,1},{7,0},{8,15},{9,14},{10,... | collective-permute-start | bytes 196616 | tf_op jit(solution)/shard_map/ppermute | solution.py:542
  17.8 5.1 %collective-permute-start.7 = (f32[1,112,128]{2,1,0:T(8,128)S(1)}, f32[1,112,128]{2,1,0:T(8,128)S(1)}, u32[]{:S(2)}, u32[]{:S(2)}) collective-permute-start(f32[1,112,128]{2,1,0:T(8,128)S(1)} %get-tuple-element.64), channel_id=1, source_target_pairs={{0,4},{1,5},{2,6},{3,7},{4,0},{5,1},{6,2},{7,3},{8,12},{9,13},{10,... | collective-permute-start | bytes 172040 | tf_op jit(solution)/shard_map/ppermute | solution.py:542
  17.8 8.4 %collective-permute-start.3 = (f32[1,128,128]{2,1,0:T(8,128)S(1)}, f32[1,128,128]{2,1,0:T(8,128)S(1)}, u32[]{:S(2)}, u32[]{:S(2)}) collective-permute-start(f32[1,128,128]{2,1,0:T(8,128)S(1)} %get-tuple-element.56), channel_id=1, source_target_pairs={{0,1},{1,0},{2,3},{3,2},{4,5},{5,4},{6,7},{7,6},{8,9},{9,8},{10,11... | collective-permute-start | bytes 196616 | tf_op jit(solution)/shard_map/ppermute | solution.py:542
  19.2 7.0 %collective-permute-start.4 = (f32[1,128,128]{2,1,0:T(8,128)S(1)}, f32[1,128,128]{2,1,0:T(8,128)S(1)}, u32[]{:S(2)}, u32[]{:S(2)}) collective-permute-start(f32[1,128,128]{2,1,0:T(8,128)S(1)} %get-tuple-element.57), channel_id=1, source_target_pairs={{0,3},{1,2},{2,1},{3,0},{4,7},{5,6},{6,5},{7,4},{8,11},{9,10},{10,... | collective-permute-start | bytes 196616 | tf_op jit(solution)/shard_map/ppermute | solution.py:542
  21.2 7.2 %collective-permute-start.8 = (f32[1,112,128]{2,1,0:T(8,128)S(1)}, f32[1,112,128]{2,1,0:T(8,128)S(1)}, u32[]{:S(2)}, u32[]{:S(2)}) collective-permute-start(f32[1,112,128]{2,1,0:T(8,128)S(1)} %get-tuple-element.66), channel_id=1, source_target_pairs={{0,5},{1,4},{2,7},{3,6},{4,1},{5,0},{6,3},{7,2},{8,13},{9,12},{10,... | collective-permute-start | bytes 172040 | tf_op jit(solution)/shard_map/ppermute | solution.py:542
  22.8 6.1 %collective-permute-start.9 = (f32[1,112,128]{2,1,0:T(8,128)S(1)}, f32[1,112,128]{2,1,0:T(8,128)S(1)}, u32[]{:S(2)}, u32[]{:S(2)}) collective-permute-start(f32[1,112,128]{2,1,0:T(8,128)S(1)} %get-tuple-element.67), channel_id=1, source_target_pairs={{0,6},{1,7},{2,4},{3,5},{4,2},{5,3},{6,0},{7,1},{8,14},{9,15},{10,... | collective-permute-start | bytes 172040 | tf_op jit(solution)/shard_map/ppermute | solution.py:542
  25.1 4.4 %collective-permute-start.6 = (f32[1,112,128]{2,1,0:T(8,128)S(1)}, f32[1,112,128]{2,1,0:T(8,128)S(1)}, u32[]{:S(2)}, u32[]{:S(2)}) collective-permute-start(f32[1,112,128]{2,1,0:T(8,128)S(1)} %get-tuple-element.62), channel_id=1, source_target_pairs={{0,2},{1,3},{2,0},{3,1},{4,6},{5,7},{6,4},{7,5},{8,10},{9,11},{10,... | collective-permute-start | bytes 172040 | tf_op jit(solution)/shard_map/ppermute | solution.py:542

commit v4 on v3

--- a/solution.py
+++ b/solution.py
@@ -15,7 +15,8 @@
 clausius = 0.07
 ref_temp = 280.0
 LANES = 128
-SENT = (4, 7, 5, 3, 1, 6, 2)
+SENT = (7, 4, 5, 1, 3, 6, 2)
+AFTER = {6: (1,), 2: (7,)}
 
 
 def gll_tables():
@@ -106,7 +107,7 @@
     return total
 
 
-def edge_rows_kernel(
+def transport_kernel(
     iso_hbm,
     wind_hbm,
     metric_hbm,
@@ -115,15 +116,17 @@
     day_hbm,
     order_hbm,
     iso_ref,
+    temps_ref,
+    day_ref,
+    order_ref,
+    sums_ref,
+    den_ref,
+    low_ref,
+    high_ref,
+    right_ref,
     wind_ref,
     metric_ref,
     mat_ref,
-    temps_ref,
-    day_ref,
-    order_ref,
-    den_ref,
-    low_ref,
-    high_ref,
     hi_ref,
     lo_ref,
     sems,
@@ -133,6 +136,8 @@
     levels = part // size_x
     chans = 3 * levels
     deriv, weight = gll_tables()
+    shared, _ = row_maps(size_x)
+    n_rows = shared[-1] + 1
     copies = [pltpu.make_async_copy(metric_hbm, metric_ref, sems.at[0])]
     for k in range(2):
         copies.append(pltpu.make_async_copy(wind_hbm.at[pl.ds(k * part, part)], wind_ref.at[pl.ds(k * part, part)], sems.at[1 + k]))
@@ -160,32 +165,6 @@
         c.wait()
     for s in range(3):
         copies[3 + s].wait()
-        for k, (first, i) in enumerate(((0, 0), (size_x - 4, 3))):
-            fx = []
-            for j in range(4):
-                if j == i:
-                    f, fy = fluxes(iso_ref, wind_ref, metric_ref, s, first + j, float(weight[i]))
-                else:
-                    f = fluxes(iso_ref, wind_ref, metric_ref, s, first + j, None)
-                fx.append(f)
-            put_split(hi_ref, lo_ref, pl.ds(k * chans + s * levels, levels), fy, weighted_derivative(weight[i] * deriv[i], fx))
-    copies[6].wait()
-    total = second_dim(hi_ref[...], lo_ref[...], mat_ref[...])
-    for ref, k, n in ((low_ref, 0, 0), (high_ref, 1, size_x - 1)):
-        ref[0:chans, :] = total[k * chans : (k + 1) * chans, :]
-        ref[chans : chans + 8, :] = jnp.broadcast_to(mass[n : n + 1, :], (8, LANES))
-    for c in copies[7:]:
-        c.wait()
-
-
-def transport_kernel(iso_ref, wind_ref, metric_ref, mat_ref, den_ref, low_ref, high_ref, sums_ref, left_ref, right_ref, hi_ref, lo_ref):
-    size_x, size_y = metric_ref.shape
-    levels = wind_ref.shape[0] // (2 * size_x)
-    chans = 3 * levels
-    deriv, weight = gll_tables()
-    shared, _ = row_maps(size_x)
-    n_rows = shared[-1] + 1
-    for s in range(3):
         held = None
         for e in range(size_x // 4):
             fx, fy = [], []
@@ -195,52 +174,36 @@
                 fy.append(g)
             for i in range(4):
                 n = 4 * e + i
-                if n == 0 or n == size_x - 1:
-                    continue
                 a, b = fy[i], weighted_derivative(weight[i] * deriv[i], fx)
-                if i == 0:
+                if i == 0 and held is not None:
                     a, b = a + held[0], b + held[1]
-                if i == 3:
+                if i == 3 and n != size_x - 1:
                     held = (a, b)
                 else:
-                    put_split(hi_ref, lo_ref, pl.ds((shared[n] - 1) * chans + s * levels, levels), a, b)
-    last = (n_rows - 1) * chans
-    sums_ref[0:chans, :] = low_ref[0:chans, :]
-    sums_ref[chans:last, :] = second_dim(hi_ref[...], lo_ref[...], mat_ref[...])
-    sums_ref[last : last + chans, :] = high_ref[0:chans, :]
-
-    mass = den_ref[...]
+                    put_split(hi_ref, lo_ref, pl.ds(shared[n] * chans + s * levels, levels), a, b)
+    copies[6].wait()
+    sums_ref[...] = second_dim(hi_ref[...], lo_ref[...], mat_ref[...])
+    for ref, r, n in ((low_ref, 0, 0), (high_ref, n_rows - 1, size_x - 1)):
+        ref[0:chans, :] = sums_ref[pl.ds(r * chans, chans), :]
+        ref[chans : chans + 8, :] = jnp.broadcast_to(mass[n : n + 1, :], (8, LANES))
+    gather_column(size_y - 1, sums_ref, mass, right_ref)
+    for c in copies[7:]:
+        c.wait()
+
+
+def gather_column(lane, sums_ref, mass, out_ref):
+    chans = out_ref.shape[0] - 8
+    shared, _ = row_maps(mass.shape[0])
     wide, lane1 = lanes_of(chans), lanes_of(1)
-    first_col = jnp.zeros((chans, LANES), jnp.float32)
-    last_col = first_col
-    first_den = jnp.zeros((1, LANES), jnp.float32)
-    last_den = first_den
-    for r in range(n_rows):
-        here = sums_ref[pl.ds(r * chans, chans), :]
-        n = shared.index(r)
-        if r:
-            first_col = jnp.where(wide == r, pltpu.roll(here, r, 1), first_col)
-            first_den = jnp.where(lane1 == r, pltpu.roll(mass, r, 1)[n : n + 1, :], first_den)
-        else:
-            first_col = jnp.where(wide == 0, here, first_col)
-            first_den = jnp.where(lane1 == 0, mass[0:1, :], first_den)
-        last_col = jnp.where(wide == r, pltpu.roll(here, r + 1, 1), last_col)
-        last_den = jnp.where(lane1 == r, pltpu.roll(mass, r + 1, 1)[n : n + 1, :], last_den)
-    left_ref[0:chans, :] = first_col
-    left_ref[chans : chans + 8, :] = jnp.broadcast_to(first_den, (8, LANES))
-    right_ref[0:chans, :] = last_col
-    right_ref[chans : chans + 8, :] = jnp.broadcast_to(last_den, (8, LANES))
-
-
-def corners_kernel(n_rows, filler_ref, left_ref, right_ref, from_low_ref, from_high_ref, new_left_ref, new_right_ref):
-    del filler_ref
-    low, high = from_low_ref[...], from_high_ref[...]
-    lane = lanes_of(low.shape[0])
-    last = n_rows - 1
-    new_left_ref[...] = left_ref[...] + jnp.where(lane == 0, low, 0.0) + jnp.where(lane == last, pltpu.roll(high, last, 1), 0.0)
-    new_right_ref[...] = (
-        right_ref[...] + jnp.where(lane == 0, pltpu.roll(low, 1, 1), 0.0) + jnp.where(lane == last, pltpu.roll(high, last + 1, 1), 0.0)
-    )
+    col = jnp.zeros((chans, LANES), jnp.float32)
+    den = jnp.zeros((1, LANES), jnp.float32)
+    for r in range(shared[-1] + 1):
+        shift = (r - lane) % LANES
+        here, n = sums_ref[pl.ds(r * chans, chans), :], shared.index(r)
+        col = jnp.where(wide == r, pltpu.roll(here, shift, 1) if shift else here, col)
+        den = jnp.where(lane1 == r, (pltpu.roll(mass, shift, 1) if shift else mass)[n : n + 1, :], den)
+    out_ref[0:chans, :] = col
+    out_ref[chans : chans + 8, :] = jnp.broadcast_to(den, (8, LANES))
 
 
 def cumulative(x):
@@ -295,7 +258,8 @@
     return jnp.take_along_axis(padded, source, axis=1)
 
 
-def send_order_kernel(n_peers, paired, temps_ref, day_ref, order_ref, hot_ref, pick_ref, ntemps_ref, nday_ref, slots_ref):
+def send_order_kernel(n_peers, paired, after_ref, temps_ref, day_ref, order_ref, hot_ref, pick_ref, ntemps_ref, nday_ref, slots_ref):
+    del after_ref
     levels, sites = temps_ref.shape
     count = ntemps_ref.shape[0] // levels - 1
     per_row = sites // count
@@ -319,10 +283,13 @@
     main = jnp.where((row == 0) | (node == 0), -1, (row - 1) * LANES + node)
     first = jnp.where(row == 0, node, -1)
     side = jnp.where((row != 0) & (node == 0), row, -1)
-    sub = lax.broadcasted_iota(jnp.int32, (LANES, LANES), 0)
+    bf16 = jnp.bfloat16
+    sub = lax.broadcasted_iota(jnp.int32, (LANES, LANES), 0).astype(bf16)
 
     def one_hot(index):
-        return jnp.where(sub == index, 1.0, 0.0).astype(jnp.bfloat16)
+        index = jnp.broadcast_to(jnp.clip(index, -1, LANES).astype(jnp.float32), (16, LANES)).astype(bf16)
+        index = jnp.concatenate([index] * (LANES // 16), axis=0)
+        return jnp.where(sub == index, jnp.ones((), bf16), jnp.zeros((), bf16))
 
     for t in range(sites // LANES):
         at = slice(t * LANES, (t + 1) * LANES)
@@ -350,8 +317,7 @@
     nday_ref[8 * count :, :] = side_day
 
 
-def inner_columns_kernel(after_ref, iso_ref, sums_ref, den_ref, ntemps_ref, nday_ref, hot_ref, acc_ref, hiso_ref, lhs_ref):
-    del after_ref
+def inner_columns_kernel(iso_ref, sums_ref, den_ref, ntemps_ref, nday_ref, hot_ref, acc_ref, hiso_ref, left_ref, lhs_ref):
     size_x, size_y = den_ref.shape
     chans = acc_ref.shape[0]
     levels = chans // 3
@@ -372,12 +338,13 @@
         lhs_ref[0:chans, (k - 1) * LANES : k * LANES] = hi
         lhs_ref[chans : 2 * chans, (k - 1) * LANES : k * LANES] = lo
     hiso_ref[...] = hiso
+    gather_column(0, sums_ref, den_ref[...], left_ref)
     both = dot(lhs_ref[...], hot_ref[...])
     acc_ref[...] = both[0:chans] + both[chans:]
 
 
 def edge_columns_kernel(
-    n_peers, paired, iso_ref, sums_ref, den_ref, left_ref, acc_ref, pick_ref, ntemps_ref, nday_ref, hiso_ref, low_ref, before_ref, *send_refs
+    n_peers, paired, iso_ref, sums_ref, den_ref, left_ref, acc_ref, pick_ref, ntemps_ref, nday_ref, hiso_ref, corner_ref, before_ref, low_ref, high_ref, *send_refs
 ):
     chans, sites = acc_ref.shape
     levels = chans // 3
@@ -389,8 +356,10 @@
     wide, lane1 = lanes_of(chans), lanes_of(1)
     unused = (lane1 & 3) == 3
 
-    total = sums_ref[0:chans, :] + low_ref[0:chans, :] + jnp.where(wide == 0, before_ref[0:chans, :], 0.0)
-    den = den_ref[0:1, :] + low_ref[chans : chans + 1, :] + jnp.where(lane1 == 0, before_ref[chans : chans + 1, :], 0.0)
+    last = row_maps(size_x)[0][-1]
+    extra = before_ref[...] + pltpu.roll(corner_ref[...], LANES - last, 1)
+    total = sums_ref[0:chans, :] + low_ref[0:chans, :] + jnp.where(wide == 0, extra[0:chans, :], 0.0)
+    den = den_ref[0:1, :] + low_ref[chans : chans + 1, :] + jnp.where(lane1 == 0, extra[chans : chans + 1, :], 0.0)
     iso = iso_ref[pl.ds(0, chans, stride=size_x), :]
     new_row = iso + jnp.where(unused, 0.0, time_step / den) * total
     phys_row = physics(new_row, ntemps_ref[0:levels, :], nday_ref[0:1, :])
@@ -423,30 +392,43 @@
                 at += count
 
 
-    if paired:
-        pad = jnp.zeros((LANES - left_ref.shape[0], LANES), jnp.float32)
-        turned = jnp.concatenate([left_ref[...], pad], axis=0).T
+    lane, high = lanes_of(chans + 8), high_ref[...]
+    edge = left_ref[...] + jnp.where(lane == 0, low_ref[...], 0.0) + jnp.where(lane == last, pltpu.roll(high, last, 1), 0.0)
+    edge = jnp.where(lane == last + 1, pltpu.roll(high, last + 2, 1), edge)
+    if not paired:
+        send_refs[n_peers][...] = edge
+    else:
+        turned = jnp.concatenate([edge, jnp.zeros((LANES - edge.shape[0], LANES), jnp.float32)], axis=0).T
         for k in carriers(n_peers):
             rows = send_refs[k].shape[1] - send_refs[0].shape[1]
             send_refs[k][0, send_refs[0].shape[1] :, :] = turned[0:rows, :]
 
 
-def advance_kernel(n_peers, paired, carried, iso_ref, sums_ref, den_ref, low_ref, high_ref, before_ref, *rest):
-    *after_refs, new_hbm, after_ref, new_ref, sems = rest
+def advance_kernel(n_peers, paired, carried, iso_ref, sums_ref, den_ref, corner_ref, near_ref, low_ref, high_ref, *rest):
+    *edge_refs, new_hbm, before_ref, after_ref, new_ref, sems = rest
     size_x = den_ref.shape[0]
     chans = low_ref.shape[0] - 8
     shared, _ = row_maps(size_x)
+    last = shared[-1]
     lane1 = lanes_of(1)
     if paired:
         me = lax.axis_index("blk")
-        mine = me ^ lax.rem(me + 1, n_peers)
-        turned = jnp.zeros((carried, LANES), jnp.float32)
-        for k, ref in zip(carriers(n_peers), after_refs):
-            turned = jnp.where(mine == k, ref[0, ref.shape[1] - carried :, :], turned)
-        pad = jnp.zeros((LANES - carried, LANES), jnp.float32)
-        after_ref[...] = jnp.concatenate([turned, pad], axis=0).T[0 : chans + 8, :]
+        turned = []
+        for other in (lax.rem(me + 1, n_peers), lax.rem(me + n_peers - 1, n_peers)):
+            mine = jnp.zeros((carried, LANES), jnp.float32)
+            for k, ref in zip(carriers(n_peers), edge_refs):
+                mine = jnp.where((me ^ other) == k, ref[0, ref.shape[1] - carried :, :], mine)
+            turned.append(mine)
+        pad = jnp.zeros((LANES - 2 * carried, LANES), jnp.float32)
+        both = jnp.concatenate(turned + [pad], axis=0).T[0 : chans + 8, :]
+        after_ref[...] = both
+        beside = pltpu.roll(both, LANES - carried - 1, 1)
     else:
-        after_ref[...] = after_refs[0][...]
+        after_ref[...] = edge_refs[0][...]
+        beside = pltpu.roll(edge_refs[1][...], LANES - 1, 1)
+    lane = lanes_of(chans + 8)
+    near = near_ref[...] + jnp.where(lane == 0, pltpu.roll(corner_ref[...], LANES - last, 1), 0.0)
+    before_ref[...] = near + jnp.where(lane == last, beside, 0.0)
     gains = []
     for n in range(size_x):
         den = den_ref[n : n + 1, :]
@@ -528,19 +510,19 @@
         c.wait()
 
 
-def exchange(slots, left, paired):
+def exchange(slots, edge, paired):
     n_peers = lax.axis_size("blk")
     if not paired:
         got = lax.all_to_all(jnp.concatenate(slots, axis=0), "blk", split_axis=0, concat_axis=0, tiled=True)
-        return [got], [lax.ppermute(left, "blk", [((j + 1) % n_peers, j) for j in range(n_peers)])]
-    got = []
-    sent = SENT
-    for n, k in enumerate(sent):
+        up = [(j, (j + 1) % n_peers) for j in range(n_peers)]
+        return [got], [lax.ppermute(edge[0], "blk", [(j, i) for i, j in up]), lax.ppermute(edge[0], "blk", up)]
+    got = {0: slots[0]}
+    for k in SENT:
         block = slots[k]
-        if n >= 5:
-            block, got[n - 5] = lax.optimization_barrier((block, got[n - 5]))
-        got.append(lax.ppermute(block, "blk", [(j, j ^ k) for j in range(n_peers)]))
-    got = [slots[0]] + [got[sent.index(k)] for k in range(1, n_peers)]
+        for w in AFTER.get(k, ()):
+            block, got[w] = lax.optimization_barrier((block, got[w]))
+        got[k] = lax.ppermute(block, "blk", [(j, j ^ k) for j in range(n_peers)])
+    got = [got[k] for k in range(n_peers)]
     return got, [got[k] for k in carriers(n_peers)]
 
 
@@ -572,7 +554,7 @@
     n_rows = shared[-1] + 1
     per_peer = sites // n_blk
     paired = n_blk == 8
-    carried = -(-n_rows // 8) * 8
+    carried = -(-(n_rows + 1) // 8) * 8
     send_rows = chans * (per_peer // LANES) + per_peer % LANES
 
     def f32(*shape):
@@ -585,31 +567,35 @@
     integers = jax.ShapeDtypeStruct((1, sites), jnp.int32)
     bf16 = jnp.bfloat16
     args = (iso, wind, metric_scaling, matrix, thermal_state[0], daytime_indicator, outgoing_site_order)
-    iso, wind, metric, matrix, temps, day, order, den, low, high = call(
-        edge_rows_kernel,
-        (*[jax.ShapeDtypeStruct(x.shape, x.dtype) for x in args], f32(size_x, size_y), edge, edge),
-        [pltpu.VMEM((2 * chans, 2 * size_y), bf16)] * 2 + [pltpu.SemaphoreType.DMA((10,))],
-        "edge_rows",
+    iso, temps, day, order, sums, den, low, high, right = call(
+        transport_kernel,
+        (
+            f32(*iso.shape),
+            f32(levels, sites),
+            integers,
+            integers,
+            f32(n_rows * chans, size_y),
+            f32(size_x, size_y),
+            *[edge] * 3,
+        ),
+        [
+            pltpu.VMEM(wind.shape, jnp.float32),
+            pltpu.VMEM((size_x, size_y), jnp.float32),
+            pltpu.VMEM(matrix.shape, bf16),
+        ]
+        + [pltpu.VMEM((n_rows * chans, 2 * size_y), bf16)] * 2 + [pltpu.SemaphoreType.DMA((10,))],
+        "transport",
         *(pltpu.with_memory_space_constraint(x, pltpu.HBM) for x in args),
         in_specs=[pl.BlockSpec(memory_space=pltpu.HBM)] * len(args),
     )
     face_up = [(i, (i + 1) % n_face) for i in range(n_face)]
     blk_up = [(i, (i + 1) % n_blk) for i in range(n_blk)]
+    corner = lax.ppermute(
+        right, ("face", "blk"), [(i * n_blk + j, i_up * n_blk + j_up) for i, i_up in face_up for j, j_up in blk_up]
+    )
+    before = lax.ppermute(right, "blk", blk_up)
     from_low = lax.ppermute(high, "face", face_up)
     from_high = lax.ppermute(low, "face", [(j, i) for i, j in face_up])
-    sums, left, right = call(
-        transport_kernel,
-        (f32(n_rows * chans, size_y), edge, edge),
-        [pltpu.VMEM(((n_rows - 2) * chans, 2 * size_y), bf16)] * 2,
-        "transport",
-        iso,
-        wind,
-        metric,
-        matrix,
-        den,
-        low,
-        high,
-    )
     count = len(node_rows)
     hot, pick, ntemps, nday = call(
         lambda *refs: send_order_kernel(n_blk, paired, *refs),
@@ -621,20 +607,16 @@
         ),
         [pltpu.VMEM((n_blk, -(-per_peer // LANES) * LANES), jnp.int32)],
         "send_order",
+        den,
         temps,
         day,
         order,
     )
-    left, right = call(
-        lambda *refs: corners_kernel(n_rows, *refs), (f32(chans + 8, LANES),) * 2, [], "corners", nday, left, right, from_low, from_high
-    )
-    before = lax.ppermute(right, "blk", blk_up)
-    acc, hiso = call(
+    acc, hiso, left = call(
         inner_columns_kernel,
-        (f32(chans, sites), f32(chans, LANES)),
+        (f32(chans, sites), f32(chans, LANES), edge),
         [pltpu.VMEM((2 * chans, (count - 1) * LANES), bf16)],
         "inner_columns",
-        left,
         iso,
         sums,
         den,
@@ -644,7 +626,7 @@
     )
     slots = call(
         lambda *refs: edge_columns_kernel(n_blk, paired, *refs),
-        [f32(1, send_rows + (carried if paired and k in carriers(n_blk) else 0), LANES) for k in range(n_blk)],
+        [f32(1, send_rows + (carried if paired and k in carriers(n_blk) else 0), LANES) for k in range(n_blk)] + [edge] * (not paired),
         [],
         "edge_columns",
         iso,
@@ -656,22 +638,30 @@
         ntemps,
         nday,
         hiso,
+        corner,
+        before,
         from_low,
-        before,
-    )
-    got, after = exchange(slots, left, paired)
+        from_high,
+    )
+    got, edges = exchange(slots[0:n_blk], slots[n_blk:], paired)
     new = call(
         lambda *refs: advance_kernel(n_blk, paired, carried, *refs),
         f32(chans * size_x, size_y),
-        [pltpu.VMEM((chans + 8, LANES), jnp.float32), pltpu.VMEM((chans * size_x, size_y), jnp.float32), pltpu.SemaphoreType.DMA((3,))],
+        [
+            pltpu.VMEM((chans + 8, LANES), jnp.float32),
+            pltpu.VMEM((chans + 8, LANES), jnp.float32),
+            pltpu.VMEM((chans * size_x, size_y), jnp.float32),
+            pltpu.SemaphoreType.DMA((3,)),
+        ],
         "advance",
         iso,
         sums,
         den,
+        corner,
+        before,
         from_low,
         from_high,
-        before,
-        *after,
+        *edges,
         out_specs=pl.BlockSpec(memory_space=pltpu.HBM),
     )
     phys = call(

time: 30.9 us -> 30.1 us (0.974)
  waiting for transfers between devices: 6.52 us -> 4.09 us
  starting transfers between devices: 14.1 us -> 16.3 us
  Pallas kernels: 9.21 us -> 8.74 us
    ppermute x1, waiting for transfers between devices: 4.05 us -> 0.93 us  [on_device(): before = lax.ppermute(right, 'blk', blk_up)]
    ppermute x7 -> x8, starting transfers between devices: 10.1 us -> 13 us  [the longest x7 10.6 us: exchange(): got[k] = lax.ppermute(block, 'blk', [(j, j ^ k) for j in range(n_peers)])]
    ppermute x1, starting transfers between devices: 2.46 us -> 0.4 us  [on_device(): from_high = lax.ppermute(low, 'face', [(j, i) for i, j in face_up])]
    ppermute x1, starting transfers between devices: 0.01 us -> 1.35 us  [on_device(): from_low = lax.ppermute(high, 'face', face_up)]
    ppermute x7 -> x8, waiting for transfers between devices: 1.85 us -> 3.16 us  [the longest x7 3.15 us: exchange(): got[k] = lax.ppermute(block, 'blk', [(j, j ^ k) for j in range(n_peers)])]
    ppermute x1, waiting for transfers between devices: 0.61 us -> 0.01 us  [on_device(): from_low = lax.ppermute(high, 'face', face_up)]
    pallas_call x8 -> x6, Pallas kernels: 9.21 us -> 8.74 us  [call(): pl.pallas_call(kernel, out_shape=outs, **more, scratch_shapes=scratch, na...]
  transfers between devices with their start and end apart: 10 -> 11, of which waited for: 6 -> 5; matrix products, arithmetic and copies ran while one was open for 0% -> 0% of each run, Pallas kernels for 19% -> 15%
where the time goes in v4:
time: 30.1 us; the launch traced here: 29.9 us
  starting transfers between devices  16.3 us (54%)
  Pallas kernels  8.74 us (29%)
  waiting for transfers between devices  4.09 us (14%)
  between operations  0.68 us (2%)
    ppermute x7, starting transfers between devices, exchange(): got[k] = lax.ppermute(block, 'blk', [(j, j ^ k) for j in range(n_peers)])  10.6 us
    pallas_call x6, Pallas kernels, call(): pl.pallas_call(kernel, out_shape=outs, **more, scratch_shapes=scratch, na...  8.74 us
    ppermute x7, waiting for transfers between devices, exchange(): got[k] = lax.ppermute(block, 'blk', [(j, j ^ k) for j in range(n_peers)])  3.15 us
    ppermute x1, starting transfers between devices, on_device(): lax.ppermute(right, ('face', 'blk'), [(i * n_blk + j, i_up * n_blk + j_up...  2.43 us
    ppermute x1, starting transfers between devices, on_device(): before = lax.ppermute(right, 'blk', blk_up)  1.55 us
    ppermute x1, starting transfers between devices, on_device(): from_low = lax.ppermute(high, 'face', face_up)  1.35 us
    ppermute x1, waiting for transfers between devices, on_device(): before = lax.ppermute(right, 'blk', blk_up)  0.93 us
  transfers between devices with their start and end apart: 11, of which 5 were waited for; matrix products, arithmetic and copies ran while one was open for 0% of the time, Pallas kernels for 15%

profile of v4, /device:TPU:0, one launch (start us, length us, event | category | flops | bytes accessed | tf_op | source)
XLA Modules:
  0.0 29.9 jit_solution(17735820868646999400)
XLA Ops:
  0.6 2.8 %transport.1 = (f32[1536,128]{1,0:T(8,128)S(1)}, f32[32,1152]{1,0:T(8,128)S(1)}, s32[1,1152]{1,0:T(1,128)S(1)}, s32[1,1152]{1,0:T(1,128)S(1)}, f32[1248,128]{1,0...) custom-call(f32[1536,128]{1,0:T(8,128)} %bitcast.5, ...), custom_call_target="tpu_custom_call" | custom-call | tf_op jit(solution)/shard_map/transport/pallas_call | solution.py:530
  3.4 2.4 %collective-permute-start = (f32[104,128]{1,0:T(8,128)S(1)}, f32[104,128]{1,0:T(8,128)S(1)}, u32[]{:S(2)}, u32[]{:S(2)}) collective-permute-start(f32[104,128]{1,0:T(8,128)S(1)} %get-tuple-element.33), channel_id=1, source_target_pairs={{0,9},{1,10},{2,11},{3,12},{4,13},{5,14},{6,15},{7,8},{8,17},{9,18... | collective-permute-start | bytes 159752 | tf_op jit(solution)/shard_map/ppermute | solution.py:593
  5.8 1.6 %collective-permute-start.1 = (f32[104,128]{1,0:T(8,128)S(1)}, f32[104,128]{1,0:T(8,128)S(1)}, u32[]{:S(2)}, u32[]{:S(2)}) collective-permute-start(f32[104,128]{1,0:T(8,128)S(1)} %get-tuple-element.33), channel_id=1, source_target_pairs={{0,1},{1,2},{2,3},{3,4},{4,5},{5,6},{6,7},{7,0},{8,9},{9,10},{10,1... | collective-permute-start | bytes 159752 | tf_op jit(solution)/shard_map/ppermute | solution.py:596
  7.4 1.3 %collective-permute-start.2 = (f32[104,128]{1,0:T(8,128)S(1)}, f32[104,128]{1,0:T(8,128)S(1)}, u32[]{:S(2)}, u32[]{:S(2)}) collective-permute-start(f32[104,128]{1,0:T(8,128)S(1)} %get-tuple-element.34), channel_id=1, source_target_pairs={{0,8},{8,16},{16,24},{24,0},{1,9},{9,17},{17,25},{25,1},{2,10},{10... | collective-permute-start | bytes 159752 | tf_op jit(solution)/shard_map/ppermute | solution.py:597
  8.7 0.4 %collective-permute-start.3 = (f32[104,128]{1,0:T(8,128)S(1)}, f32[104,128]{1,0:T(8,128)S(1)}, u32[]{:S(2)}, u32[]{:S(2)}) collective-permute-start(f32[104,128]{1,0:T(8,128)S(1)} %get-tuple-element.35), channel_id=1, source_target_pairs={{8,0},{16,8},{24,16},{0,24},{9,1},{17,9},{25,17},{1,25},{10,2},{18... | collective-permute-start | bytes 159752 | tf_op jit(solution)/shard_map/ppermute | solution.py:598
  9.1 1.3 %send_order.1 = (bf16[1408,1152]{1,0:T(8,128)(2,1)S(1)}, bf16[256,1152]{1,0:T(8,128)(2,1)S(1)}, f32[416,128]{1,0:T(8,128)S(1)}, f32[104,128]{1,0:T(8,128)S(1)}) custom-call(f32[16,128]{1,0:T(8,128)S(1)} %get-tuple-element.32.refs_0_.den_ref.refs_2_, f32[32,1152]{1,0:T(8,128)S(1)} %get-tuple-element.36.refs_1_, s32[1,1152]{1,0:T(1,128)S(1)} %get-tuple-element.37.refs_2_, ...), custom_call_target="tpu_custom_call" | custom-call | tf_op jit(solution)/shard_map/send_order/pallas_call | solution.py:530
  10.5 1.3 %inner_columns.1 = (f32[96,1152]{1,0:T(8,128)S(1)}, f32[96,128]{1,0:T(8,128)S(1)}, f32[104,128]{1,0:T(8,128)S(1)}) custom-call(f32[1536,128]{1,0:T(8,128)S(1)} %get-tuple-element.30.iso_ref.refs_0_, f32[1248,128]{1,0:T(8,128)S(1)} %get-tuple-element.31.sums_ref.refs_1_, f32[16,128]{1,0:T(8,128)S(1)} %get-tuple-element.32.refs_0_.den_ref.refs_2_, ...), custom_call_target="tpu_custom_call" | custom-call | tf_op jit(solution)/shard_map/inner_columns/pallas_call | solution.py:530
  11.8 0.0 collective-permute-done.refs_9_.refs_3_
  11.8 0.9 %collective-permute-done.1.refs_10_.refs_4_ = f32[104,128]{1,0:T(8,128)S(1)} collective-permute-done((f32[104,128]{1,0:T(8,128)S(1)}, f32[104,128]{1,0:T(8,128)S(1)}, u32[]{:S(2)}, u32[]{:S(2)}) %collective-permute-start.1) | collective-permute-done | bytes 53280 | tf_op jit(solution)/shard_map/ppermute | solution.py:596
  12.7 0.0 collective-permute-done.2.refs_11_.refs_5_
  12.7 0.0 collective-permute-done.3.refs_12_.refs_6_
  12.7 0.5 %edge_columns.1 = (f32[1,112,128]{2,1,0:T(8,128)S(1)}, f32[1,128,128]{2,1,0:T(8,128)S(1)}, f32[1,112,128]{2,1,0:T(8,128)S(1)}, f32[1,128,128]{2,1,0:T(8,128)S(1)...) custom-call(f32[1536,128]{1,0:T(8,128)S(1)} %get-tuple-element.30.is, ...), custom_call_target="tpu_custom_call" | custom-call | tf_op jit(solution)/shard_map/edge_columns/pallas_call | solution.py:530
  13.3 2.3 %collective-permute-start.6 = (f32[1,128,128]{2,1,0:T(8,128)S(1)}, f32[1,128,128]{2,1,0:T(8,128)S(1)}, u32[]{:S(2)}, u32[]{:S(2)}) collective-permute-start(f32[1,128,128]{2,1,0:T(8,128)S(1)} %get-tuple-element.51), channel_id=1, source_target_pairs={{0,7},{1,6},{2,5},{3,4},{4,3},{5,2},{6,1},{7,0},{8,15},{9,14},{10,... | collective-permute-start | bytes 196616 | tf_op jit(solution)/shard_map/ppermute | solution.py:524
  15.5 1.0 %collective-permute-start.4 = (f32[1,128,128]{2,1,0:T(8,128)S(1)}, f32[1,128,128]{2,1,0:T(8,128)S(1)}, u32[]{:S(2)}, u32[]{:S(2)}) collective-permute-start(f32[1,128,128]{2,1,0:T(8,128)S(1)} %get-tuple-element.47), channel_id=1, source_target_pairs={{0,1},{1,0},{2,3},{3,2},{4,5},{5,4},{6,7},{7,6},{8,9},{9,8},{10,11... | collective-permute-start | bytes 196616 | tf_op jit(solution)/shard_map/ppermute | solution.py:524
  16.5 1.4 %collective-permute-start.5 = (f32[1,128,128]{2,1,0:T(8,128)S(1)}, f32[1,128,128]{2,1,0:T(8,128)S(1)}, u32[]{:S(2)}, u32[]{:S(2)}) collective-permute-start(f32[1,128,128]{2,1,0:T(8,128)S(1)} %get-tuple-element.49), channel_id=1, source_target_pairs={{0,3},{1,2},{2,1},{3,0},{4,7},{5,6},{6,5},{7,4},{8,11},{9,10},{10,... | collective-permute-start | bytes 196616 | tf_op jit(solution)/shard_map/ppermute | solution.py:524
  17.9 1.2 %collective-permute-start.8 = (f32[1,112,128]{2,1,0:T(8,128)S(1)}, f32[1,112,128]{2,1,0:T(8,128)S(1)}, u32[]{:S(2)}, u32[]{:S(2)}) collective-permute-start(f32[1,112,128]{2,1,0:T(8,128)S(1)} %get-tuple-element.55), channel_id=1, source_target_pairs={{0,4},{1,5},{2,6},{3,7},{4,0},{5,1},{6,2},{7,3},{8,12},{9,13},{10,... | collective-permute-start | bytes 172040 | tf_op jit(solution)/shard_map/ppermute | solution.py:524
  19.1 1.7 %collective-permute-start.9 = (f32[1,112,128]{2,1,0:T(8,128)S(1)}, f32[1,112,128]{2,1,0:T(8,128)S(1)}, u32[]{:S(2)}, u32[]{:S(2)}) collective-permute-start(f32[1,112,128]{2,1,0:T(8,128)S(1)} %get-tuple-element.56), channel_id=1, source_target_pairs={{0,5},{1,4},{2,7},{3,6},{4,1},{5,0},{6,3},{7,2},{8,13},{9,12},{10,... | collective-permute-start | bytes 172040 | tf_op jit(solution)/shard_map/ppermute | solution.py:524
  20.8 0.1 collective-permute-done.6.refs_9_.refs_7_
  20.9 1.5 %collective-permute-start.7 = (f32[1,112,128]{2,1,0:T(8,128)S(1)}, f32[1,112,128]{2,1,0:T(8,128)S(1)}, u32[]{:S(2)}, u32[]{:S(2)}) collective-permute-start(f32[1,112,128]{2,1,0:T(8,128)S(1)} %get-tuple-element.54), channel_id=1, source_target_pairs={{0,2},{1,3},{2,0},{3,1},{4,6},{5,7},{6,4},{7,5},{8,10},{9,11},{10,... | collective-permute-start | bytes 172040 | tf_op jit(solution)/shard_map/ppermute | solution.py:524
  22.4 0.5 %collective-permute-done.4.refs_7_.refs_1_ = f32[1,128,128]{2,1,0:T(8,128)S(1)} collective-permute-done((f32[1,128,128]{2,1,0:T(8,128)S(1)}, f32[1,128,128]{2,1,0:T(8,128)S(1)}, u32[]{:S(2)}, u32[]{:S(2)}) %collective-permute-start.4) | collective-permute-done | bytes 65568 | tf_op jit(solution)/shard_map/ppermute | solution.py:524
  22.9 1.6 %collective-permute-start.10 = (f32[1,112,128]{2,1,0:T(8,128)S(1)}, f32[1,112,128]{2,1,0:T(8,128)S(1)}, u32[]{:S(2)}, u32[]{:S(2)}) collective-permute-start(f32[1,112,128]{2,1,0:T(8,128)S(1)} %get-tuple-element.57), channel_id=1, source_target_pairs={{0,6},{1,7},{2,4},{3,5},{4,2},{5,3},{6,0},{7,1},{8,14},{9,15},{10,... | collective-permute-start | bytes 172040 | tf_op jit(solution)/shard_map/ppermute | solution.py:524
  24.4 0.0 collective-permute-done.5.refs_8_.refs_3_
  24.4 1.8 %advance.1 = f32[1536,128]{1,0:T(8,128)} custom-call(f32[1536,128]{1,0:T(8,128)S(1)} %get-tuple-element.30.iso_ref.refs_0_, f32[1248,128]{1,0:T(8,128)S(1)} %get-tuple-element.31.sums_ref.refs_1_, f32[16,128]{1,0:T(8,128)S(1)} %get-tuple-element.32.refs_0_.den_ref.refs_2_, f32[104,128]{1,0:T(8,128)S(1)} %collective-permute-done.refs_9_.refs_3_, ...), custom_call_target="tpu_custom_call" | custom-call | tf_op jit(solution)/shard_map/advance/pallas_call | solution.py:530
  26.2 0.0 collective-permute-done.8.refs_4_
  26.2 0.7 %collective-permute-done.9.refs_5_ = f32[1,112,128]{2,1,0:T(8,128)S(1)} collective-permute-done((f32[1,112,128]{2,1,0:T(8,128)S(1)}, f32[1,112,128]{2,1,0:T(8,128)S(1)}, u32[]{:S(2)}, u32[]{:S(2)}) %collective-permute-start.9) | collective-permute-done | bytes 57376 | tf_op jit(solution)/shard_map/ppermute | solution.py:524
  26.9 0.0 collective-permute-done.7.refs_2_
  26.9 1.9 %collective-permute-done.10.refs_6_ = f32[1,112,128]{2,1,0:T(8,128)S(1)} collective-permute-done((f32[1,112,128]{2,1,0:T(8,128)S(1)}, f32[1,112,128]{2,1,0:T(8,128)S(1)}, u32[]{:S(2)}, u32[]{:S(2)}) %collective-permute-start.10) | collective-permute-done | bytes 57376 | tf_op jit(solution)/shard_map/ppermute | solution.py:524
  28.8 1.0 %assemble.1 = f32[96,1152]{1,0:T(8,128)} custom-call(f32[1,112,128]{2,1,0:T(8,128)S(1)} %get-tuple-element.53.refs_0_, f32[1,128,128]{2,1,0:T(8,128)S(1)} %collective-permute-done.4.refs_7_.refs_1_, f32[1,112,128]{2,1,0:T(8,128)S(1)} %collective-permute-done.7.refs_2_, f32[1,128,128]{2,1,0:T(8,128)S(1)} %collective-permute-done.5.refs_8_.refs_3_, ...), custom_call_target="tpu_custom_call" | custom-call | tf_op jit(solution)/shard_map/assemble/pallas_call | solution.py:530
Async XLA Ops:
  3.4 8.3 %collective-permute-start = (f32[104,128]{1,0:T(8,128)S(1)}, f32[104,128]{1,0:T(8,128)S(1)}, u32[]{:S(2)}, u32[]{:S(2)}) collective-permute-start(f32[104,128]{1,0:T(8,128)S(1)} %get-tuple-element.33), channel_id=1, source_target_pairs={{0,9},{1,10},{2,11},{3,12},{4,13},{5,14},{6,15},{7,8},{8,17},{9,18... | collective-permute-start | bytes 159752 | tf_op jit(solution)/shard_map/ppermute | solution.py:593
  5.8 6.9 %collective-permute-start.1 = (f32[104,128]{1,0:T(8,128)S(1)}, f32[104,128]{1,0:T(8,128)S(1)}, u32[]{:S(2)}, u32[]{:S(2)}) collective-permute-start(f32[104,128]{1,0:T(8,128)S(1)} %get-tuple-element.33), channel_id=1, source_target_pairs={{0,1},{1,2},{2,3},{3,4},{4,5},{5,6},{6,7},{7,0},{8,9},{9,10},{10,1... | collective-permute-start | bytes 159752 | tf_op jit(solution)/shard_map/ppermute | solution.py:596
  7.4 5.3 %collective-permute-start.2 = (f32[104,128]{1,0:T(8,128)S(1)}, f32[104,128]{1,0:T(8,128)S(1)}, u32[]{:S(2)}, u32[]{:S(2)}) collective-permute-start(f32[104,128]{1,0:T(8,128)S(1)} %get-tuple-element.34), channel_id=1, source_target_pairs={{0,8},{8,16},{16,24},{24,0},{1,9},{9,17},{17,25},{25,1},{2,10},{10... | collective-permute-start | bytes 159752 | tf_op jit(solution)/shard_map/ppermute | solution.py:597
  8.7 4.0 %collective-permute-start.3 = (f32[104,128]{1,0:T(8,128)S(1)}, f32[104,128]{1,0:T(8,128)S(1)}, u32[]{:S(2)}, u32[]{:S(2)}) collective-permute-start(f32[104,128]{1,0:T(8,128)S(1)} %get-tuple-element.35), channel_id=1, source_target_pairs={{8,0},{16,8},{24,16},{0,24},{9,1},{17,9},{25,17},{1,25},{10,2},{18... | collective-permute-start | bytes 159752 | tf_op jit(solution)/shard_map/ppermute | solution.py:598
  13.3 7.6 %collective-permute-start.6 = (f32[1,128,128]{2,1,0:T(8,128)S(1)}, f32[1,128,128]{2,1,0:T(8,128)S(1)}, u32[]{:S(2)}, u32[]{:S(2)}) collective-permute-start(f32[1,128,128]{2,1,0:T(8,128)S(1)} %get-tuple-element.51), channel_id=1, source_target_pairs={{0,7},{1,6},{2,5},{3,4},{4,3},{5,2},{6,1},{7,0},{8,15},{9,14},{10,... | collective-permute-start | bytes 196616 | tf_op jit(solution)/shard_map/ppermute | solution.py:524
  15.5 7.3 %collective-permute-start.4 = (f32[1,128,128]{2,1,0:T(8,128)S(1)}, f32[1,128,128]{2,1,0:T(8,128)S(1)}, u32[]{:S(2)}, u32[]{:S(2)}) collective-permute-start(f32[1,128,128]{2,1,0:T(8,128)S(1)} %get-tuple-element.47), channel_id=1, source_target_pairs={{0,1},{1,0},{2,3},{3,2},{4,5},{5,4},{6,7},{7,6},{8,9},{9,8},{10,11... | collective-permute-start | bytes 196616 | tf_op jit(solution)/shard_map/ppermute | solution.py:524
  16.5 7.9 %collective-permute-start.5 = (f32[1,128,128]{2,1,0:T(8,128)S(1)}, f32[1,128,128]{2,1,0:T(8,128)S(1)}, u32[]{:S(2)}, u32[]{:S(2)}) collective-permute-start(f32[1,128,128]{2,1,0:T(8,128)S(1)} %get-tuple-element.49), channel_id=1, source_target_pairs={{0,3},{1,2},{2,1},{3,0},{4,7},{5,6},{6,5},{7,4},{8,11},{9,10},{10,... | collective-permute-start | bytes 196616 | tf_op jit(solution)/shard_map/ppermute | solution.py:524
  17.9 8.3 %collective-permute-start.8 = (f32[1,112,128]{2,1,0:T(8,128)S(1)}, f32[1,112,128]{2,1,0:T(8,128)S(1)}, u32[]{:S(2)}, u32[]{:S(2)}) collective-permute-start(f32[1,112,128]{2,1,0:T(8,128)S(1)} %get-tuple-element.55), channel_id=1, source_target_pairs={{0,4},{1,5},{2,6},{3,7},{4,0},{5,1},{6,2},{7,3},{8,12},{9,13},{10,... | collective-permute-start | bytes 172040 | tf_op jit(solution)/shard_map/ppermute | solution.py:524
  19.1 7.8 %collective-permute-start.9 = (f32[1,112,128]{2,1,0:T(8,128)S(1)}, f32[1,112,128]{2,1,0:T(8,128)S(1)}, u32[]{:S(2)}, u32[]{:S(2)}) collective-permute-start(f32[1,112,128]{2,1,0:T(8,128)S(1)} %get-tuple-element.56), channel_id=1, source_target_pairs={{0,5},{1,4},{2,7},{3,6},{4,1},{5,0},{6,3},{7,2},{8,13},{9,12},{10,... | collective-permute-start | bytes 172040 | tf_op jit(solution)/shard_map/ppermute | solution.py:524
  20.9 6.1 %collective-permute-start.7 = (f32[1,112,128]{2,1,0:T(8,128)S(1)}, f32[1,112,128]{2,1,0:T(8,128)S(1)}, u32[]{:S(2)}, u32[]{:S(2)}) collective-permute-start(f32[1,112,128]{2,1,0:T(8,128)S(1)} %get-tuple-element.54), channel_id=1, source_target_pairs={{0,2},{1,3},{2,0},{3,1},{4,6},{5,7},{6,4},{7,5},{8,10},{9,11},{10,... | collective-permute-start | bytes 172040 | tf_op jit(solution)/shard_map/ppermute | solution.py:524
  22.9 6.0 %collective-permute-start.10 = (f32[1,112,128]{2,1,0:T(8,128)S(1)}, f32[1,112,128]{2,1,0:T(8,128)S(1)}, u32[]{:S(2)}, u32[]{:S(2)}) collective-permute-start(f32[1,112,128]{2,1,0:T(8,128)S(1)} %get-tuple-element.57), channel_id=1, source_target_pairs={{0,6},{1,7},{2,4},{3,5},{4,2},{5,3},{6,0},{7,1},{8,14},{9,15},{10,... | collective-permute-start | bytes 172040 | tf_op jit(solution)/shard_map/ppermute | solution.py:524

commit v5 on v4

--- a/solution.py
+++ b/solution.py
@@ -15,6 +15,7 @@
 clausius = 0.07
 ref_temp = 280.0
 LANES = 128
+PAD_ROWS = 8
 SENT = (7, 4, 5, 1, 3, 6, 2)
 AFTER = {6: (1,), 2: (7,)}
 
@@ -88,15 +89,15 @@
 
 
 def fluxes(iso_ref, wind_ref, metric_ref, s, n, weight):
-    size_x = metric_ref.shape[0]
+    pitch = metric_ref.shape[0] + PAD_ROWS
     part = wind_ref.shape[0] // 2
-    levels = part // size_x
+    levels = part // pitch
     jac = metric_ref[n : n + 1, :]
-    q = iso_ref[pl.ds(s * part + n, levels, stride=size_x), :]
-    fx = (jac * wind_ref[pl.ds(n, levels, stride=size_x), :]) * q
+    q = iso_ref[pl.ds(s * part + n, levels, stride=pitch), :]
+    fx = (jac * wind_ref[pl.ds(n, levels, stride=pitch), :]) * q
     if weight is None:
         return fx
-    return fx, ((jac * weight) * wind_ref[pl.ds(part + n, levels, stride=size_x), :]) * q
+    return fx, ((jac * weight) * wind_ref[pl.ds(part + n, levels, stride=pitch), :]) * q
 
 
 def weighted_derivative(coefs, fx):
@@ -133,16 +134,20 @@
 ):
     size_x, size_y = metric_ref.shape
     part = wind_ref.shape[0] // 2
-    levels = part // size_x
+    pitch = size_x + PAD_ROWS
+    levels = part // pitch
     chans = 3 * levels
     deriv, weight = gll_tables()
     shared, _ = row_maps(size_x)
     n_rows = shared[-1] + 1
     copies = [pltpu.make_async_copy(metric_hbm, metric_ref, sems.at[0])]
+    wind_in, wind = (ref.reshape(2, levels, -1, size_y) for ref in (wind_hbm, wind_ref))
+    iso_in, iso = (ref.reshape(3, levels, -1, size_y) for ref in (iso_hbm, iso_ref))
+    rows = pl.ds(0, size_x)
     for k in range(2):
-        copies.append(pltpu.make_async_copy(wind_hbm.at[pl.ds(k * part, part)], wind_ref.at[pl.ds(k * part, part)], sems.at[1 + k]))
+        copies.append(pltpu.make_async_copy(wind_in.at[k], wind.at[k, :, rows], sems.at[1 + k]))
     for s in range(3):
-        copies.append(pltpu.make_async_copy(iso_hbm.at[pl.ds(s * part, part)], iso_ref.at[pl.ds(s * part, part)], sems.at[3 + s]))
+        copies.append(pltpu.make_async_copy(iso_in.at[s], iso.at[s, :, rows], sems.at[3 + s]))
     copies.append(pltpu.make_async_copy(mat_hbm, mat_ref, sems.at[6]))
     for k, (src, dst) in enumerate(((temps_hbm, temps_ref), (day_hbm, day_ref), (order_hbm, order_ref))):
         copies.append(pltpu.make_async_copy(src, dst, sems.at[7 + k]))
@@ -258,10 +263,10 @@
     return jnp.take_along_axis(padded, source, axis=1)
 
 
-def send_order_kernel(n_peers, paired, after_ref, temps_ref, day_ref, order_ref, hot_ref, pick_ref, ntemps_ref, nday_ref, slots_ref):
+def send_order_kernel(n_peers, paired, after_ref, order_ref, hot_ref, pick_ref, slots_ref):
     del after_ref
-    levels, sites = temps_ref.shape
-    count = ntemps_ref.shape[0] // levels - 1
+    sites = order_ref.shape[1]
+    count = hot_ref.shape[0] // LANES + 1
     per_row = sites // count
     per_peer = sites // n_peers
     full, rest = per_peer // LANES, per_peer % LANES
@@ -299,6 +304,11 @@
         pick_ref[0:LANES, at] = one_hot(first[:, at])
         pick_ref[LANES : 2 * LANES, at] = one_hot(side[:, at])
 
+
+def spread_columns(temps_ref, day_ref, ntemps_ref, nday_ref):
+    levels, sites = temps_ref.shape
+    count = ntemps_ref.shape[0] // levels - 1
+    per_row = sites // count
     temps = temps_ref[...]
     day = jnp.broadcast_to(day_ref[...].astype(jnp.float32), (8, sites))
     lane1, wide_l = lanes_of(1), lanes_of(levels)
@@ -317,7 +327,8 @@
     nday_ref[8 * count :, :] = side_day
 
 
-def inner_columns_kernel(iso_ref, sums_ref, den_ref, ntemps_ref, nday_ref, hot_ref, acc_ref, hiso_ref, left_ref, lhs_ref):
+def inner_columns_kernel(iso_ref, sums_ref, den_ref, temps_ref, day_ref, hot_ref, acc_ref, hiso_ref, left_ref, ntemps_ref, nday_ref, lhs_ref):
+    spread_columns(temps_ref, day_ref, ntemps_ref, nday_ref)
     size_x, size_y = den_ref.shape
     chans = acc_ref.shape[0]
     levels = chans // 3
@@ -330,7 +341,7 @@
     for k, n in enumerate(node_rows):
         if k == 0:
             continue
-        iso = iso_ref[pl.ds(n, chans, stride=size_x), :]
+        iso = iso_ref[pl.ds(n, chans, stride=size_x + PAD_ROWS), :]
         hiso = jnp.where(wide == k, pltpu.roll(iso, k, 1), hiso)
         gain = jnp.where(own, 0.0, time_step * inv[n : n + 1, :])
         tracers = iso + gain * sums_ref[pl.ds(k * chans, chans), :]
@@ -360,7 +371,7 @@
     extra = before_ref[...] + pltpu.roll(corner_ref[...], LANES - last, 1)
     total = sums_ref[0:chans, :] + low_ref[0:chans, :] + jnp.where(wide == 0, extra[0:chans, :], 0.0)
     den = den_ref[0:1, :] + low_ref[chans : chans + 1, :] + jnp.where(lane1 == 0, extra[chans : chans + 1, :], 0.0)
-    iso = iso_ref[pl.ds(0, chans, stride=size_x), :]
+    iso = iso_ref[pl.ds(0, chans, stride=size_x + PAD_ROWS), :]
     new_row = iso + jnp.where(unused, 0.0, time_step / den) * total
     phys_row = physics(new_row, ntemps_ref[0:levels, :], nday_ref[0:1, :])
 
@@ -439,7 +450,6 @@
             den = jnp.where(lane1 == at, den + ref[chans : chans + 1, shared[n] : shared[n] + 1], den)
         gains.append(time_step / den)
     levels = chans // 3
-    part = levels * size_x
     wide = lanes_of(levels)
     copies = []
     for s in range(3):
@@ -452,10 +462,10 @@
                     total = total + ref[at_s, :]
             for ref, at in ((before_ref, 0), (after_ref, LANES - 1)):
                 total = jnp.where(wide == at, total + ref[at_s, r : r + 1], total)
-            here = pl.ds(s * part + n, levels, stride=size_x)
+            here = pl.ds(s * levels * (size_x + PAD_ROWS) + n, levels, stride=size_x + PAD_ROWS)
             new_ref[here, :] = iso_ref[here, :] + gains[n] * total
-        done = pl.ds(s * part, part)
-        copies.append(pltpu.make_async_copy(new_ref.at[done], new_hbm.at[done], sems.at[s]))
+        made, out = (ref.reshape(3, levels, -1, LANES) for ref in (new_ref, new_hbm))
+        copies.append(pltpu.make_async_copy(made.at[s, :, pl.ds(0, size_x)], out.at[s], sems.at[s]))
         copies[-1].start()
     for c in copies:
         c.wait()
@@ -570,7 +580,7 @@
     iso, temps, day, order, sums, den, low, high, right = call(
         transport_kernel,
         (
-            f32(*iso.shape),
+            f32(chans * (size_x + PAD_ROWS), size_y),
             f32(levels, sites),
             integers,
             integers,
@@ -579,7 +589,7 @@
             *[edge] * 3,
         ),
         [
-            pltpu.VMEM(wind.shape, jnp.float32),
+            pltpu.VMEM((2 * levels * (size_x + PAD_ROWS), size_y), jnp.float32),
             pltpu.VMEM((size_x, size_y), jnp.float32),
             pltpu.VMEM(matrix.shape, bf16),
         ]
@@ -597,31 +607,24 @@
     from_low = lax.ppermute(high, "face", face_up)
     from_high = lax.ppermute(low, "face", [(j, i) for i, j in face_up])
     count = len(node_rows)
-    hot, pick, ntemps, nday = call(
+    hot, pick = call(
         lambda *refs: send_order_kernel(n_blk, paired, *refs),
-        (
-            jax.ShapeDtypeStruct(((count - 1) * LANES, sites), bf16),
-            jax.ShapeDtypeStruct((2 * LANES, sites), bf16),
-            f32((count + 1) * levels, LANES),
-            f32((count + 1) * 8, LANES),
-        ),
+        (jax.ShapeDtypeStruct(((count - 1) * LANES, sites), bf16), jax.ShapeDtypeStruct((2 * LANES, sites), bf16)),
         [pltpu.VMEM((n_blk, -(-per_peer // LANES) * LANES), jnp.int32)],
         "send_order",
         den,
-        temps,
-        day,
         order,
     )
-    acc, hiso, left = call(
+    acc, hiso, left, ntemps, nday = call(
         inner_columns_kernel,
-        (f32(chans, sites), f32(chans, LANES), edge),
+        (f32(chans, sites), f32(chans, LANES), edge, f32((count + 1) * levels, LANES), f32((count + 1) * 8, LANES)),
         [pltpu.VMEM((2 * chans, (count - 1) * LANES), bf16)],
         "inner_columns",
         iso,
         sums,
         den,
-        ntemps,
-        nday,
+        temps,
+        day,
         hot,
     )
     slots = call(
@@ -650,7 +653,7 @@
         [
             pltpu.VMEM((chans + 8, LANES), jnp.float32),
             pltpu.VMEM((chans + 8, LANES), jnp.float32),
-            pltpu.VMEM((chans * size_x, size_y), jnp.float32),
+            pltpu.VMEM((chans * (size_x + PAD_ROWS), size_y), jnp.float32),
             pltpu.SemaphoreType.DMA((3,)),
         ],
         "advance",

time: 30.1 us -> 29.3 us (0.973)
  Pallas kernels: 8.74 us -> 7.94 us
    pallas_call x6, Pallas kernels: 8.74 us -> 7.94 us  [call(): pl.pallas_call(kernel, out_shape=outs, **more, scratch_shapes=scratch, na...]
    ppermute x7, waiting for transfers between devices: 3.15 us -> 2.75 us  [exchange(): got[k] = lax.ppermute(block, 'blk', [(j, j ^ k) for j in range(n_peers)])]
  transfers between devices with their start and end apart: 11 -> 11, of which waited for: 5 -> 6; matrix products, arithmetic and copies ran while one was open for 0% -> 0% of each run, Pallas kernels for 15% -> 13%
where the time goes in v5:
time: 29.3 us; the launch traced here: 29.1 us
  starting transfers between devices  16.4 us (56%)
  Pallas kernels  7.94 us (27%)
  waiting for transfers between devices  4.05 us (14%)
  between operations  0.68 us (2%)
    ppermute x7, starting transfers between devices, exchange(): got[k] = lax.ppermute(block, 'blk', [(j, j ^ k) for j in range(n_peers)])  10.7 us
    pallas_call x6, Pallas kernels, call(): pl.pallas_call(kernel, out_shape=outs, **more, scratch_shapes=scratch, na...  7.94 us
    ppermute x7, waiting for transfers between devices, exchange(): got[k] = lax.ppermute(block, 'blk', [(j, j ^ k) for j in range(n_peers)])  2.75 us
    ppermute x1, starting transfers between devices, on_device(): lax.ppermute(right, ('face', 'blk'), [(i * n_blk + j, i_up * n_blk + j_up...  2.43 us
    ppermute x1, starting transfers between devices, on_device(): before = lax.ppermute(right, 'blk', blk_up)  1.54 us
    ppermute x1, starting transfers between devices, on_device(): from_low = lax.ppermute(high, 'face', face_up)  1.35 us
    ppermute x1, waiting for transfers between devices, on_device(): before = lax.ppermute(right, 'blk', blk_up)  1.04 us
  transfers between devices with their start and end apart: 11, of which 6 were waited for; matrix products, arithmetic and copies ran while one was open for 0% of the time, Pallas kernels for 13%

profile of v5, /device:TPU:0, one launch (start us, length us, event | category | flops | bytes accessed | tf_op | source)
XLA Modules:
  0.0 29.1 jit_solution(3347481685640884995)
XLA Ops:
  0.6 2.5 %transport.1 = (f32[2304,128]{1,0:T(8,128)S(1)}, f32[32,1152]{1,0:T(8,128)S(1)}, s32[1,1152]{1,0:T(1,128)S(1)}, s32[1,1152]{1,0:T(1,128)S(1)}, f32[1248,128]{1,0...) custom-call(f32[1536,128]{1,0:T(8,128)} %bitcast.5, ...), custom_call_target="tpu_custom_call" | custom-call | tf_op jit(solution)/shard_map/transport/pallas_call | solution.py:540
  3.1 2.4 %collective-permute-start = (f32[104,128]{1,0:T(8,128)S(1)}, f32[104,128]{1,0:T(8,128)S(1)}, u32[]{:S(2)}, u32[]{:S(2)}) collective-permute-start(f32[104,128]{1,0:T(8,128)S(1)} %get-tuple-element.33), channel_id=1, source_target_pairs={{0,9},{1,10},{2,11},{3,12},{4,13},{5,14},{6,15},{7,8},{8,17},{9,18... | collective-permute-start | bytes 159752 | tf_op jit(solution)/shard_map/ppermute | solution.py:603
  5.5 1.5 %collective-permute-start.1 = (f32[104,128]{1,0:T(8,128)S(1)}, f32[104,128]{1,0:T(8,128)S(1)}, u32[]{:S(2)}, u32[]{:S(2)}) collective-permute-start(f32[104,128]{1,0:T(8,128)S(1)} %get-tuple-element.33), channel_id=1, source_target_pairs={{0,1},{1,2},{2,3},{3,4},{4,5},{5,6},{6,7},{7,0},{8,9},{9,10},{10,1... | collective-permute-start | bytes 159752 | tf_op jit(solution)/shard_map/ppermute | solution.py:606
  7.1 1.4 %collective-permute-start.2 = (f32[104,128]{1,0:T(8,128)S(1)}, f32[104,128]{1,0:T(8,128)S(1)}, u32[]{:S(2)}, u32[]{:S(2)}) collective-permute-start(f32[104,128]{1,0:T(8,128)S(1)} %get-tuple-element.34), channel_id=1, source_target_pairs={{0,8},{8,16},{16,24},{24,0},{1,9},{9,17},{17,25},{25,1},{2,10},{10... | collective-permute-start | bytes 159752 | tf_op jit(solution)/shard_map/ppermute | solution.py:607
  8.4 0.4 %collective-permute-start.3 = (f32[104,128]{1,0:T(8,128)S(1)}, f32[104,128]{1,0:T(8,128)S(1)}, u32[]{:S(2)}, u32[]{:S(2)}) collective-permute-start(f32[104,128]{1,0:T(8,128)S(1)} %get-tuple-element.35), channel_id=1, source_target_pairs={{8,0},{16,8},{24,16},{0,24},{9,1},{17,9},{25,17},{1,25},{10,2},{18... | collective-permute-start | bytes 159752 | tf_op jit(solution)/shard_map/ppermute | solution.py:608
  8.8 0.8 %send_order.1 = (bf16[1408,1152]{1,0:T(8,128)(2,1)S(1)}, bf16[256,1152]{1,0:T(8,128)(2,1)S(1)}) custom-call(f32[16,128]{1,0:T(8,128)S(1)} %get-tuple-element.32.refs_0_.den_ref.refs_2_, s32[1,1152]{1,0:T(1,128)S(1)} %get-tuple-element.38.refs_1_), custom_call_target="tpu_custom_call" | custom-call | tf_op jit(solution)/shard_map/send_order/pallas_call | solution.py:540
  9.6 1.5 %inner_columns.1 = (f32[96,1152]{1,0:T(8,128)S(1)}, f32[96,128]{1,0:T(8,128)S(1)}, f32[104,128]{1,0:T(8,128)S(1)}, f32[416,128]{1,0:T(8,128)S(1)}, f32[104,128]{1,0:T(8,128)S(1)}) custom-call(f32[2304,128]{1,0:T(8,128)S(1)} %get-tuple-element.30.iso_ref.refs_0_, f32[1248,128]{1,0:T(8,128)S(1)} %get-tuple-element.31.sums_ref.refs_1_, ...), custom_call_target="tpu_custom_call" | custom-call | tf_op jit(solution)/shard_map/inner_columns/pallas_call | solution.py:540
  11.1 0.2 collective-permute-done.refs_9_.refs_3_
  11.3 1.0 %collective-permute-done.1.refs_10_.refs_4_ = f32[104,128]{1,0:T(8,128)S(1)} collective-permute-done((f32[104,128]{1,0:T(8,128)S(1)}, f32[104,128]{1,0:T(8,128)S(1)}, u32[]{:S(2)}, u32[]{:S(2)}) %collective-permute-start.1) | collective-permute-done | bytes 53280 | tf_op jit(solution)/shard_map/ppermute | solution.py:606
  12.4 0.0 collective-permute-done.2.refs_11_.refs_5_
  12.4 0.0 collective-permute-done.3.refs_12_.refs_6_
  12.4 0.5 %edge_columns.1 = (f32[1,112,128]{2,1,0:T(8,128)S(1)}, f32[1,128,128]{2,1,0:T(8,128)S(1)}, f32[1,112,128]{2,1,0:T(8,128)S(1)}, f32[1,128,128]{2,1,0:T(8,128)S(1)...) custom-call(f32[2304,128]{1,0:T(8,128)S(1)} %get-tuple-element.30.is, ...), custom_call_target="tpu_custom_call" | custom-call | tf_op jit(solution)/shard_map/edge_columns/pallas_call | solution.py:540
  12.9 2.0 %collective-permute-start.6 = (f32[1,128,128]{2,1,0:T(8,128)S(1)}, f32[1,128,128]{2,1,0:T(8,128)S(1)}, u32[]{:S(2)}, u32[]{:S(2)}) collective-permute-start(f32[1,128,128]{2,1,0:T(8,128)S(1)} %get-tuple-element.51), channel_id=1, source_target_pairs={{0,7},{1,6},{2,5},{3,4},{4,3},{5,2},{6,1},{7,0},{8,15},{9,14},{10,... | collective-permute-start | bytes 196616 | tf_op jit(solution)/shard_map/ppermute | solution.py:534
  14.9 1.3 %collective-permute-start.4 = (f32[1,128,128]{2,1,0:T(8,128)S(1)}, f32[1,128,128]{2,1,0:T(8,128)S(1)}, u32[]{:S(2)}, u32[]{:S(2)}) collective-permute-start(f32[1,128,128]{2,1,0:T(8,128)S(1)} %get-tuple-element.47), channel_id=1, source_target_pairs={{0,1},{1,0},{2,3},{3,2},{4,5},{5,4},{6,7},{7,6},{8,9},{9,8},{10,11... | collective-permute-start | bytes 196616 | tf_op jit(solution)/shard_map/ppermute | solution.py:534
  16.2 1.0 %collective-permute-start.5 = (f32[1,128,128]{2,1,0:T(8,128)S(1)}, f32[1,128,128]{2,1,0:T(8,128)S(1)}, u32[]{:S(2)}, u32[]{:S(2)}) collective-permute-start(f32[1,128,128]{2,1,0:T(8,128)S(1)} %get-tuple-element.49), channel_id=1, source_target_pairs={{0,3},{1,2},{2,1},{3,0},{4,7},{5,6},{6,5},{7,4},{8,11},{9,10},{10,... | collective-permute-start | bytes 196616 | tf_op jit(solution)/shard_map/ppermute | solution.py:534
  17.2 1.2 %collective-permute-start.8 = (f32[1,112,128]{2,1,0:T(8,128)S(1)}, f32[1,112,128]{2,1,0:T(8,128)S(1)}, u32[]{:S(2)}, u32[]{:S(2)}) collective-permute-start(f32[1,112,128]{2,1,0:T(8,128)S(1)} %get-tuple-element.55), channel_id=1, source_target_pairs={{0,4},{1,5},{2,6},{3,7},{4,0},{5,1},{6,2},{7,3},{8,12},{9,13},{10,... | collective-permute-start | bytes 172040 | tf_op jit(solution)/shard_map/ppermute | solution.py:534
  18.5 1.7 %collective-permute-start.9 = (f32[1,112,128]{2,1,0:T(8,128)S(1)}, f32[1,112,128]{2,1,0:T(8,128)S(1)}, u32[]{:S(2)}, u32[]{:S(2)}) collective-permute-start(f32[1,112,128]{2,1,0:T(8,128)S(1)} %get-tuple-element.56), channel_id=1, source_target_pairs={{0,5},{1,4},{2,7},{3,6},{4,1},{5,0},{6,3},{7,2},{8,13},{9,12},{10,... | collective-permute-start | bytes 172040 | tf_op jit(solution)/shard_map/ppermute | solution.py:534
  20.1 0.4 %collective-permute-done.6.refs_9_.refs_7_ = f32[1,128,128]{2,1,0:T(8,128)S(1)} collective-permute-done((f32[1,128,128]{2,1,0:T(8,128)S(1)}, f32[1,128,128]{2,1,0:T(8,128)S(1)}, u32[]{:S(2)}, u32[]{:S(2)}) %collective-permute-start.6) | collective-permute-done | bytes 65568 | tf_op jit(solution)/shard_map/ppermute | solution.py:534
  20.6 1.5 %collective-permute-start.7 = (f32[1,112,128]{2,1,0:T(8,128)S(1)}, f32[1,112,128]{2,1,0:T(8,128)S(1)}, u32[]{:S(2)}, u32[]{:S(2)}) collective-permute-start(f32[1,112,128]{2,1,0:T(8,128)S(1)} %get-tuple-element.54), channel_id=1, source_target_pairs={{0,2},{1,3},{2,0},{3,1},{4,6},{5,7},{6,4},{7,5},{8,10},{9,11},{10,... | collective-permute-start | bytes 172040 | tf_op jit(solution)/shard_map/ppermute | solution.py:534
  22.1 0.0 collective-permute-done.4.refs_7_.refs_1_
  22.1 2.0 %collective-permute-start.10 = (f32[1,112,128]{2,1,0:T(8,128)S(1)}, f32[1,112,128]{2,1,0:T(8,128)S(1)}, u32[]{:S(2)}, u32[]{:S(2)}) collective-permute-start(f32[1,112,128]{2,1,0:T(8,128)S(1)} %get-tuple-element.57), channel_id=1, source_target_pairs={{0,6},{1,7},{2,4},{3,5},{4,2},{5,3},{6,0},{7,1},{8,14},{9,15},{10,... | collective-permute-start | bytes 172040 | tf_op jit(solution)/shard_map/ppermute | solution.py:534
  24.1 0.0 collective-permute-done.5.refs_8_.refs_3_
  24.1 1.7 %advance.1 = f32[1536,128]{1,0:T(8,128)} custom-call(f32[2304,128]{1,0:T(8,128)S(1)} %get-tuple-element.30.iso_ref.refs_0_, f32[1248,128]{1,0:T(8,128)S(1)} %get-tuple-element.31.sums_ref.refs_1_, f32[16,128]{1,0:T(8,128)S(1)} %get-tuple-element.32.refs_0_.den_ref.refs_2_, f32[104,128]{1,0:T(8,128)S(1)} %collective-permute-done.refs_9_.refs_3_, ...), custom_call_target="tpu_custom_call" | custom-call | tf_op jit(solution)/shard_map/advance/pallas_call | solution.py:540
  25.8 0.0 collective-permute-done.8.refs_4_
  25.8 0.3 %collective-permute-done.9.refs_5_ = f32[1,112,128]{2,1,0:T(8,128)S(1)} collective-permute-done((f32[1,112,128]{2,1,0:T(8,128)S(1)}, f32[1,112,128]{2,1,0:T(8,128)S(1)}, u32[]{:S(2)}, u32[]{:S(2)}) %collective-permute-start.9) | collective-permute-done | bytes 57376 | tf_op jit(solution)/shard_map/ppermute | solution.py:534
  26.1 0.2 collective-permute-done.7.refs_2_
  26.3 1.8 %collective-permute-done.10.refs_6_ = f32[1,112,128]{2,1,0:T(8,128)S(1)} collective-permute-done((f32[1,112,128]{2,1,0:T(8,128)S(1)}, f32[1,112,128]{2,1,0:T(8,128)S(1)}, u32[]{:S(2)}, u32[]{:S(2)}) %collective-permute-start.10) | collective-permute-done | bytes 57376 | tf_op jit(solution)/shard_map/ppermute | solution.py:534
  28.1 1.0 %assemble.1 = f32[96,1152]{1,0:T(8,128)} custom-call(f32[1,112,128]{2,1,0:T(8,128)S(1)} %get-tuple-element.53.refs_0_, f32[1,128,128]{2,1,0:T(8,128)S(1)} %collective-permute-done.4.refs_7_.refs_1_, f32[1,112,128]{2,1,0:T(8,128)S(1)} %collective-permute-done.7.refs_2_, f32[1,128,128]{2,1,0:T(8,128)S(1)} %collective-permute-done.5.refs_8_.refs_3_, ...), custom_call_target="tpu_custom_call" | custom-call | tf_op jit(solution)/shard_map/assemble/pallas_call | solution.py:540
Async XLA Ops:
  3.1 8.2 %collective-permute-start = (f32[104,128]{1,0:T(8,128)S(1)}, f32[104,128]{1,0:T(8,128)S(1)}, u32[]{:S(2)}, u32[]{:S(2)}) collective-permute-start(f32[104,128]{1,0:T(8,128)S(1)} %get-tuple-element.33), channel_id=1, source_target_pairs={{0,9},{1,10},{2,11},{3,12},{4,13},{5,14},{6,15},{7,8},{8,17},{9,18... | collective-permute-start | bytes 159752 | tf_op jit(solution)/shard_map/ppermute | solution.py:603
  5.5 6.9 %collective-permute-start.1 = (f32[104,128]{1,0:T(8,128)S(1)}, f32[104,128]{1,0:T(8,128)S(1)}, u32[]{:S(2)}, u32[]{:S(2)}) collective-permute-start(f32[104,128]{1,0:T(8,128)S(1)} %get-tuple-element.33), channel_id=1, source_target_pairs={{0,1},{1,2},{2,3},{3,4},{4,5},{5,6},{6,7},{7,0},{8,9},{9,10},{10,1... | collective-permute-start | bytes 159752 | tf_op jit(solution)/shard_map/ppermute | solution.py:606
  7.1 5.3 %collective-permute-start.2 = (f32[104,128]{1,0:T(8,128)S(1)}, f32[104,128]{1,0:T(8,128)S(1)}, u32[]{:S(2)}, u32[]{:S(2)}) collective-permute-start(f32[104,128]{1,0:T(8,128)S(1)} %get-tuple-element.34), channel_id=1, source_target_pairs={{0,8},{8,16},{16,24},{24,0},{1,9},{9,17},{17,25},{25,1},{2,10},{10... | collective-permute-start | bytes 159752 | tf_op jit(solution)/shard_map/ppermute | solution.py:607
  8.4 4.0 %collective-permute-start.3 = (f32[104,128]{1,0:T(8,128)S(1)}, f32[104,128]{1,0:T(8,128)S(1)}, u32[]{:S(2)}, u32[]{:S(2)}) collective-permute-start(f32[104,128]{1,0:T(8,128)S(1)} %get-tuple-element.35), channel_id=1, source_target_pairs={{8,0},{16,8},{24,16},{0,24},{9,1},{17,9},{25,17},{1,25},{10,2},{18... | collective-permute-start | bytes 159752 | tf_op jit(solution)/shard_map/ppermute | solution.py:608
  12.9 7.6 %collective-permute-start.6 = (f32[1,128,128]{2,1,0:T(8,128)S(1)}, f32[1,128,128]{2,1,0:T(8,128)S(1)}, u32[]{:S(2)}, u32[]{:S(2)}) collective-permute-start(f32[1,128,128]{2,1,0:T(8,128)S(1)} %get-tuple-element.51), channel_id=1, source_target_pairs={{0,7},{1,6},{2,5},{3,4},{4,3},{5,2},{6,1},{7,0},{8,15},{9,14},{10,... | collective-permute-start | bytes 196616 | tf_op jit(solution)/shard_map/ppermute | solution.py:534
  14.9 7.2 %collective-permute-start.4 = (f32[1,128,128]{2,1,0:T(8,128)S(1)}, f32[1,128,128]{2,1,0:T(8,128)S(1)}, u32[]{:S(2)}, u32[]{:S(2)}) collective-permute-start(f32[1,128,128]{2,1,0:T(8,128)S(1)} %get-tuple-element.47), channel_id=1, source_target_pairs={{0,1},{1,0},{2,3},{3,2},{4,5},{5,4},{6,7},{7,6},{8,9},{9,8},{10,11... | collective-permute-start | bytes 196616 | tf_op jit(solution)/shard_map/ppermute | solution.py:534
  16.2 7.9 %collective-permute-start.5 = (f32[1,128,128]{2,1,0:T(8,128)S(1)}, f32[1,128,128]{2,1,0:T(8,128)S(1)}, u32[]{:S(2)}, u32[]{:S(2)}) collective-permute-start(f32[1,128,128]{2,1,0:T(8,128)S(1)} %get-tuple-element.49), channel_id=1, source_target_pairs={{0,3},{1,2},{2,1},{3,0},{4,7},{5,6},{6,5},{7,4},{8,11},{9,10},{10,... | collective-permute-start | bytes 196616 | tf_op jit(solution)/shard_map/ppermute | solution.py:534
  17.2 8.5 %collective-permute-start.8 = (f32[1,112,128]{2,1,0:T(8,128)S(1)}, f32[1,112,128]{2,1,0:T(8,128)S(1)}, u32[]{:S(2)}, u32[]{:S(2)}) collective-permute-start(f32[1,112,128]{2,1,0:T(8,128)S(1)} %get-tuple-element.55), channel_id=1, source_target_pairs={{0,4},{1,5},{2,6},{3,7},{4,0},{5,1},{6,2},{7,3},{8,12},{9,13},{10,... | collective-permute-start | bytes 172040 | tf_op jit(solution)/shard_map/ppermute | solution.py:534
  18.5 7.6 %collective-permute-start.9 = (f32[1,112,128]{2,1,0:T(8,128)S(1)}, f32[1,112,128]{2,1,0:T(8,128)S(1)}, u32[]{:S(2)}, u32[]{:S(2)}) collective-permute-start(f32[1,112,128]{2,1,0:T(8,128)S(1)} %get-tuple-element.56), channel_id=1, source_target_pairs={{0,5},{1,4},{2,7},{3,6},{4,1},{5,0},{6,3},{7,2},{8,13},{9,12},{10,... | collective-permute-start | bytes 172040 | tf_op jit(solution)/shard_map/ppermute | solution.py:534
  20.6 5.7 %collective-permute-start.7 = (f32[1,112,128]{2,1,0:T(8,128)S(1)}, f32[1,112,128]{2,1,0:T(8,128)S(1)}, u32[]{:S(2)}, u32[]{:S(2)}) collective-permute-start(f32[1,112,128]{2,1,0:T(8,128)S(1)} %get-tuple-element.54), channel_id=1, source_target_pairs={{0,2},{1,3},{2,0},{3,1},{4,6},{5,7},{6,4},{7,5},{8,10},{9,11},{10,... | collective-permute-start | bytes 172040 | tf_op jit(solution)/shard_map/ppermute | solution.py:534
  22.1 6.0 %collective-permute-start.10 = (f32[1,112,128]{2,1,0:T(8,128)S(1)}, f32[1,112,128]{2,1,0:T(8,128)S(1)}, u32[]{:S(2)}, u32[]{:S(2)}) collective-permute-start(f32[1,112,128]{2,1,0:T(8,128)S(1)} %get-tuple-element.57), channel_id=1, source_target_pairs={{0,6},{1,7},{2,4},{3,5},{4,2},{5,3},{6,0},{7,1},{8,14},{9,15},{10,... | collective-permute-start | bytes 172040 | tf_op jit(solution)/shard_map/ppermute | solution.py:534

commit v6 on v5

--- a/solution.py
+++ b/solution.py
@@ -16,8 +16,8 @@
 ref_temp = 280.0
 LANES = 128
 PAD_ROWS = 8
-SENT = (7, 4, 5, 1, 3, 6, 2)
-AFTER = {6: (1,), 2: (7,)}
+SENT = (7, 6, 5, 1, 3, 4, 2)
+AFTER = {4: (1,), 2: (7,)}
 
 
 def gll_tables():
@@ -88,16 +88,24 @@
     return first[:, 0:size_y] + (first[:, size_y:] + dot(lo, mat[:, 0:size_y]))
 
 
-def fluxes(iso_ref, wind_ref, metric_ref, s, n, weight):
-    pitch = metric_ref.shape[0] + PAD_ROWS
+def scale_winds(wind_ref, metric_ref, scaled_ref, weight):
+    size_x = metric_ref.shape[0]
+    pitch = size_x + PAD_ROWS
     part = wind_ref.shape[0] // 2
     levels = part // pitch
-    jac = metric_ref[n : n + 1, :]
-    q = iso_ref[pl.ds(s * part + n, levels, stride=pitch), :]
-    fx = (jac * wind_ref[pl.ds(n, levels, stride=pitch), :]) * q
-    if weight is None:
-        return fx
-    return fx, ((jac * weight) * wind_ref[pl.ds(part + n, levels, stride=pitch), :]) * q
+    for n in range(size_x):
+        jac = metric_ref[n : n + 1, :]
+        first, second = (pl.ds((2 * n + k) * levels, levels) for k in range(2))
+        scaled_ref[first, :] = jac * wind_ref[pl.ds(n, levels, stride=pitch), :]
+        scaled_ref[second, :] = (jac * float(weight[n % 4])) * wind_ref[pl.ds(part + n, levels, stride=pitch), :]
+
+
+def fluxes(iso_ref, scaled_ref, size_x, s, n):
+    levels = scaled_ref.shape[0] // (2 * size_x)
+    pitch = size_x + PAD_ROWS
+    q = iso_ref[pl.ds(s * levels * pitch + n, levels, stride=pitch), :]
+    first, second = (scaled_ref[pl.ds((2 * n + k) * levels, levels), :] for k in range(2))
+    return first * q, second * q
 
 
 def weighted_derivative(coefs, fx):
@@ -128,6 +136,7 @@
     wind_ref,
     metric_ref,
     mat_ref,
+    scaled_ref,
     hi_ref,
     lo_ref,
     sems,
@@ -168,13 +177,14 @@
 
     for c in copies[1:3]:
         c.wait()
+    scale_winds(wind_ref, metric_ref, scaled_ref, weight)
     for s in range(3):
         copies[3 + s].wait()
         held = None
         for e in range(size_x // 4):
             fx, fy = [], []
             for j in range(4):
-                f, g = fluxes(iso_ref, wind_ref, metric_ref, s, 4 * e + j, float(weight[j]))
+                f, g = fluxes(iso_ref, scaled_ref, size_x, s, 4 * e + j)
                 fx.append(f)
                 fy.append(g)
             for i in range(4):
@@ -592,6 +602,7 @@
             pltpu.VMEM((2 * levels * (size_x + PAD_ROWS), size_y), jnp.float32),
             pltpu.VMEM((size_x, size_y), jnp.float32),
             pltpu.VMEM(matrix.shape, bf16),
+            pltpu.VMEM((2 * levels * size_x, size_y), jnp.float32),
         ]
         + [pltpu.VMEM((n_rows * chans, 2 * size_y), bf16)] * 2 + [pltpu.SemaphoreType.DMA((10,))],
         "transport",

time: 29.3 us -> 29.2 us (level)
  waiting for transfers between devices: 4.05 us -> 5.43 us
  starting transfers between devices: 16.4 us -> 15.1 us
    ppermute x7, waiting for transfers between devices: 2.75 us -> 4.15 us  [exchange(): got[k] = lax.ppermute(block, 'blk', [(j, j ^ k) for j in range(n_peers)])]
    ppermute x7, starting transfers between devices: 10.7 us -> 9.35 us  [exchange(): got[k] = lax.ppermute(block, 'blk', [(j, j ^ k) for j in range(n_peers)])]
  transfers between devices with their start and end apart: 11 -> 11, of which waited for: 6 -> 5; matrix products, arithmetic and copies ran while one was open for 0% -> 0% of each run, Pallas kernels for 13% -> 14%
where the time goes in v6:
time: 29.2 us; the launch traced here: 29 us
  starting transfers between devices  15.1 us (52%)
  Pallas kernels  7.81 us (27%)
  waiting for transfers between devices  5.43 us (19%)
  between operations  0.68 us (2%)
    ppermute x7, starting transfers between devices, exchange(): got[k] = lax.ppermute(block, 'blk', [(j, j ^ k) for j in range(n_peers)])  9.35 us
    pallas_call x6, Pallas kernels, call(): pl.pallas_call(kernel, out_shape=outs, **more, scratch_shapes=scratch, na...  7.81 us
    ppermute x7, waiting for transfers between devices, exchange(): got[k] = lax.ppermute(block, 'blk', [(j, j ^ k) for j in range(n_peers)])  4.15 us
    ppermute x1, starting transfers between devices, on_device(): lax.ppermute(right, ('face', 'blk'), [(i * n_blk + j, i_up * n_blk + j_up...  2.43 us
    ppermute x1, starting transfers between devices, on_device(): before = lax.ppermute(right, 'blk', blk_up)  1.55 us
    ppermute x1, starting transfers between devices, on_device(): from_low = lax.ppermute(high, 'face', face_up)  1.35 us
    ppermute x1, waiting for transfers between devices, on_device(): before = lax.ppermute(right, 'blk', blk_up)  1.04 us
  transfers between devices with their start and end apart: 11, of which 5 were waited for; matrix products, arithmetic and copies ran while one was open for 0% of the time, Pallas kernels for 14%

profile of v6, /device:TPU:0, one launch (start us, length us, event | category | flops | bytes accessed | tf_op | source)
XLA Modules:
  0.0 29.0 jit_solution(8824834608605636874)
XLA Ops:
  0.6 2.3 %transport.1 = (f32[2304,128]{1,0:T(8,128)S(1)}, f32[32,1152]{1,0:T(8,128)S(1)}, s32[1,1152]{1,0:T(1,128)S(1)}, s32[1,1152]{1,0:T(1,128)S(1)}, f32[1248,128]{1,0...) custom-call(f32[1536,128]{1,0:T(8,128)} %bitcast.5, ...), custom_call_target="tpu_custom_call" | custom-call | tf_op jit(solution)/shard_map/transport/pallas_call | solution.py:550
  2.9 2.4 %collective-permute-start = (f32[104,128]{1,0:T(8,128)S(1)}, f32[104,128]{1,0:T(8,128)S(1)}, u32[]{:S(2)}, u32[]{:S(2)}) collective-permute-start(f32[104,128]{1,0:T(8,128)S(1)} %get-tuple-element.33), channel_id=1, source_target_pairs={{0,9},{1,10},{2,11},{3,12},{4,13},{5,14},{6,15},{7,8},{8,17},{9,18... | collective-permute-start | bytes 159752 | tf_op jit(solution)/shard_map/ppermute | solution.py:614
  5.4 1.6 %collective-permute-start.1 = (f32[104,128]{1,0:T(8,128)S(1)}, f32[104,128]{1,0:T(8,128)S(1)}, u32[]{:S(2)}, u32[]{:S(2)}) collective-permute-start(f32[104,128]{1,0:T(8,128)S(1)} %get-tuple-element.33), channel_id=1, source_target_pairs={{0,1},{1,2},{2,3},{3,4},{4,5},{5,6},{6,7},{7,0},{8,9},{9,10},{10,1... | collective-permute-start | bytes 159752 | tf_op jit(solution)/shard_map/ppermute | solution.py:617
  6.9 1.3 %collective-permute-start.2 = (f32[104,128]{1,0:T(8,128)S(1)}, f32[104,128]{1,0:T(8,128)S(1)}, u32[]{:S(2)}, u32[]{:S(2)}) collective-permute-start(f32[104,128]{1,0:T(8,128)S(1)} %get-tuple-element.34), channel_id=1, source_target_pairs={{0,8},{8,16},{16,24},{24,0},{1,9},{9,17},{17,25},{25,1},{2,10},{10... | collective-permute-start | bytes 159752 | tf_op jit(solution)/shard_map/ppermute | solution.py:618
  8.3 0.4 %collective-permute-start.3 = (f32[104,128]{1,0:T(8,128)S(1)}, f32[104,128]{1,0:T(8,128)S(1)}, u32[]{:S(2)}, u32[]{:S(2)}) collective-permute-start(f32[104,128]{1,0:T(8,128)S(1)} %get-tuple-element.35), channel_id=1, source_target_pairs={{8,0},{16,8},{24,16},{0,24},{9,1},{17,9},{25,17},{1,25},{10,2},{18... | collective-permute-start | bytes 159752 | tf_op jit(solution)/shard_map/ppermute | solution.py:619
  8.7 0.8 %send_order.1 = (bf16[1408,1152]{1,0:T(8,128)(2,1)S(1)}, bf16[256,1152]{1,0:T(8,128)(2,1)S(1)}) custom-call(f32[16,128]{1,0:T(8,128)S(1)} %get-tuple-element.32.refs_0_.den_ref.refs_2_, s32[1,1152]{1,0:T(1,128)S(1)} %get-tuple-element.38.refs_1_), custom_call_target="tpu_custom_call" | custom-call | tf_op jit(solution)/shard_map/send_order/pallas_call | solution.py:550
  9.4 1.5 %inner_columns.1 = (f32[96,1152]{1,0:T(8,128)S(1)}, f32[96,128]{1,0:T(8,128)S(1)}, f32[104,128]{1,0:T(8,128)S(1)}, f32[416,128]{1,0:T(8,128)S(1)}, f32[104,128]{1,0:T(8,128)S(1)}) custom-call(f32[2304,128]{1,0:T(8,128)S(1)} %get-tuple-element.30.iso_ref.refs_0_, f32[1248,128]{1,0:T(8,128)S(1)} %get-tuple-element.31.sums_ref.refs_1_, ...), custom_call_target="tpu_custom_call" | custom-call | tf_op jit(solution)/shard_map/inner_columns/pallas_call | solution.py:550
  11.0 0.2 collective-permute-done.refs_9_.refs_3_
  11.2 1.0 %collective-permute-done.1.refs_10_.refs_4_ = f32[104,128]{1,0:T(8,128)S(1)} collective-permute-done((f32[104,128]{1,0:T(8,128)S(1)}, f32[104,128]{1,0:T(8,128)S(1)}, u32[]{:S(2)}, u32[]{:S(2)}) %collective-permute-start.1) | collective-permute-done | bytes 53280 | tf_op jit(solution)/shard_map/ppermute | solution.py:617
  12.2 0.0 collective-permute-done.2.refs_11_.refs_5_
  12.2 0.0 collective-permute-done.3.refs_12_.refs_6_
  12.2 0.5 %edge_columns.1 = (f32[1,112,128]{2,1,0:T(8,128)S(1)}, f32[1,128,128]{2,1,0:T(8,128)S(1)}, f32[1,112,128]{2,1,0:T(8,128)S(1)}, f32[1,128,128]{2,1,0:T(8,128)S(1)...) custom-call(f32[2304,128]{1,0:T(8,128)S(1)} %get-tuple-element.30.is, ...), custom_call_target="tpu_custom_call" | custom-call | tf_op jit(solution)/shard_map/edge_columns/pallas_call | solution.py:550
  12.8 2.0 %collective-permute-start.6 = (f32[1,128,128]{2,1,0:T(8,128)S(1)}, f32[1,128,128]{2,1,0:T(8,128)S(1)}, u32[]{:S(2)}, u32[]{:S(2)}) collective-permute-start(f32[1,128,128]{2,1,0:T(8,128)S(1)} %get-tuple-element.51), channel_id=1, source_target_pairs={{0,7},{1,6},{2,5},{3,4},{4,3},{5,2},{6,1},{7,0},{8,15},{9,14},{10,... | collective-permute-start | bytes 196616 | tf_op jit(solution)/shard_map/ppermute | solution.py:544
  14.7 1.3 %collective-permute-start.4 = (f32[1,128,128]{2,1,0:T(8,128)S(1)}, f32[1,128,128]{2,1,0:T(8,128)S(1)}, u32[]{:S(2)}, u32[]{:S(2)}) collective-permute-start(f32[1,128,128]{2,1,0:T(8,128)S(1)} %get-tuple-element.47), channel_id=1, source_target_pairs={{0,1},{1,0},{2,3},{3,2},{4,5},{5,4},{6,7},{7,6},{8,9},{9,8},{10,11... | collective-permute-start | bytes 196616 | tf_op jit(solution)/shard_map/ppermute | solution.py:544
  16.1 1.0 %collective-permute-start.5 = (f32[1,128,128]{2,1,0:T(8,128)S(1)}, f32[1,128,128]{2,1,0:T(8,128)S(1)}, u32[]{:S(2)}, u32[]{:S(2)}) collective-permute-start(f32[1,128,128]{2,1,0:T(8,128)S(1)} %get-tuple-element.49), channel_id=1, source_target_pairs={{0,3},{1,2},{2,1},{3,0},{4,7},{5,6},{6,5},{7,4},{8,11},{9,10},{10,... | collective-permute-start | bytes 196616 | tf_op jit(solution)/shard_map/ppermute | solution.py:544
  17.1 1.3 %collective-permute-start.10 = (f32[1,112,128]{2,1,0:T(8,128)S(1)}, f32[1,112,128]{2,1,0:T(8,128)S(1)}, u32[]{:S(2)}, u32[]{:S(2)}) collective-permute-start(f32[1,112,128]{2,1,0:T(8,128)S(1)} %get-tuple-element.57), channel_id=1, source_target_pairs={{0,6},{1,7},{2,4},{3,5},{4,2},{5,3},{6,0},{7,1},{8,14},{9,15},{10,... | collective-permute-start | bytes 172040 | tf_op jit(solution)/shard_map/ppermute | solution.py:544
  18.4 2.0 %collective-permute-start.9 = (f32[1,112,128]{2,1,0:T(8,128)S(1)}, f32[1,112,128]{2,1,0:T(8,128)S(1)}, u32[]{:S(2)}, u32[]{:S(2)}) collective-permute-start(f32[1,112,128]{2,1,0:T(8,128)S(1)} %get-tuple-element.56), channel_id=1, source_target_pairs={{0,5},{1,4},{2,7},{3,6},{4,1},{5,0},{6,3},{7,2},{8,13},{9,12},{10,... | collective-permute-start | bytes 172040 | tf_op jit(solution)/shard_map/ppermute | solution.py:544
  20.4 0.0 collective-permute-done.6.refs_9_.refs_7_
  20.4 1.0 %collective-permute-start.7 = (f32[1,112,128]{2,1,0:T(8,128)S(1)}, f32[1,112,128]{2,1,0:T(8,128)S(1)}, u32[]{:S(2)}, u32[]{:S(2)}) collective-permute-start(f32[1,112,128]{2,1,0:T(8,128)S(1)} %get-tuple-element.54), channel_id=1, source_target_pairs={{0,2},{1,3},{2,0},{3,1},{4,6},{5,7},{6,4},{7,5},{8,10},{9,11},{10,... | collective-permute-start | bytes 172040 | tf_op jit(solution)/shard_map/ppermute | solution.py:544
  21.5 0.9 %collective-permute-done.4.refs_7_.refs_1_ = f32[1,128,128]{2,1,0:T(8,128)S(1)} collective-permute-done((f32[1,128,128]{2,1,0:T(8,128)S(1)}, f32[1,128,128]{2,1,0:T(8,128)S(1)}, u32[]{:S(2)}, u32[]{:S(2)}) %collective-permute-start.4) | collective-permute-done | bytes 65568 | tf_op jit(solution)/shard_map/ppermute | solution.py:544
  22.4 0.7 %collective-permute-start.8 = (f32[1,112,128]{2,1,0:T(8,128)S(1)}, f32[1,112,128]{2,1,0:T(8,128)S(1)}, u32[]{:S(2)}, u32[]{:S(2)}) collective-permute-start(f32[1,112,128]{2,1,0:T(8,128)S(1)} %get-tuple-element.55), channel_id=1, source_target_pairs={{0,4},{1,5},{2,6},{3,7},{4,0},{5,1},{6,2},{7,3},{8,12},{9,13},{10,... | collective-permute-start | bytes 172040 | tf_op jit(solution)/shard_map/ppermute | solution.py:544
  23.0 0.0 collective-permute-done.5.refs_8_.refs_3_
  23.0 1.7 %advance.1 = f32[1536,128]{1,0:T(8,128)} custom-call(f32[2304,128]{1,0:T(8,128)S(1)} %get-tuple-element.30.iso_ref.refs_0_, f32[1248,128]{1,0:T(8,128)S(1)} %get-tuple-element.31.sums_ref.refs_1_, f32[16,128]{1,0:T(8,128)S(1)} %get-tuple-element.32.refs_0_.den_ref.refs_2_, f32[104,128]{1,0:T(8,128)S(1)} %collective-permute-done.refs_9_.refs_3_, ...), custom_call_target="tpu_custom_call" | custom-call | tf_op jit(solution)/shard_map/advance/pallas_call | solution.py:550
  24.7 0.0 collective-permute-done.10.refs_6_
  24.7 2.8 %collective-permute-done.9.refs_5_ = f32[1,112,128]{2,1,0:T(8,128)S(1)} collective-permute-done((f32[1,112,128]{2,1,0:T(8,128)S(1)}, f32[1,112,128]{2,1,0:T(8,128)S(1)}, u32[]{:S(2)}, u32[]{:S(2)}) %collective-permute-start.9) | collective-permute-done | bytes 57376 | tf_op jit(solution)/shard_map/ppermute | solution.py:544
  27.5 0.0 collective-permute-done.7.refs_2_
  27.6 0.4 %collective-permute-done.8.refs_4_ = f32[1,112,128]{2,1,0:T(8,128)S(1)} collective-permute-done((f32[1,112,128]{2,1,0:T(8,128)S(1)}, f32[1,112,128]{2,1,0:T(8,128)S(1)}, u32[]{:S(2)}, u32[]{:S(2)}) %collective-permute-start.8) | collective-permute-done | bytes 57376 | tf_op jit(solution)/shard_map/ppermute | solution.py:544
  28.0 1.0 %assemble.1 = f32[96,1152]{1,0:T(8,128)} custom-call(f32[1,112,128]{2,1,0:T(8,128)S(1)} %get-tuple-element.53.refs_0_, f32[1,128,128]{2,1,0:T(8,128)S(1)} %collective-permute-done.4.refs_7_.refs_1_, f32[1,112,128]{2,1,0:T(8,128)S(1)} %collective-permute-done.7.refs_2_, f32[1,128,128]{2,1,0:T(8,128)S(1)} %collective-permute-done.5.refs_8_.refs_3_, ...), custom_call_target="tpu_custom_call" | custom-call | tf_op jit(solution)/shard_map/assemble/pallas_call | solution.py:550
Async XLA Ops:
  2.9 8.2 %collective-permute-start = (f32[104,128]{1,0:T(8,128)S(1)}, f32[104,128]{1,0:T(8,128)S(1)}, u32[]{:S(2)}, u32[]{:S(2)}) collective-permute-start(f32[104,128]{1,0:T(8,128)S(1)} %get-tuple-element.33), channel_id=1, source_target_pairs={{0,9},{1,10},{2,11},{3,12},{4,13},{5,14},{6,15},{7,8},{8,17},{9,18... | collective-permute-start | bytes 159752 | tf_op jit(solution)/shard_map/ppermute | solution.py:614
  5.4 6.9 %collective-permute-start.1 = (f32[104,128]{1,0:T(8,128)S(1)}, f32[104,128]{1,0:T(8,128)S(1)}, u32[]{:S(2)}, u32[]{:S(2)}) collective-permute-start(f32[104,128]{1,0:T(8,128)S(1)} %get-tuple-element.33), channel_id=1, source_target_pairs={{0,1},{1,2},{2,3},{3,4},{4,5},{5,6},{6,7},{7,0},{8,9},{9,10},{10,1... | collective-permute-start | bytes 159752 | tf_op jit(solution)/shard_map/ppermute | solution.py:617
  6.9 5.3 %collective-permute-start.2 = (f32[104,128]{1,0:T(8,128)S(1)}, f32[104,128]{1,0:T(8,128)S(1)}, u32[]{:S(2)}, u32[]{:S(2)}) collective-permute-start(f32[104,128]{1,0:T(8,128)S(1)} %get-tuple-element.34), channel_id=1, source_target_pairs={{0,8},{8,16},{16,24},{24,0},{1,9},{9,17},{17,25},{25,1},{2,10},{10... | collective-permute-start | bytes 159752 | tf_op jit(solution)/shard_map/ppermute | solution.py:618
  8.3 4.0 %collective-permute-start.3 = (f32[104,128]{1,0:T(8,128)S(1)}, f32[104,128]{1,0:T(8,128)S(1)}, u32[]{:S(2)}, u32[]{:S(2)}) collective-permute-start(f32[104,128]{1,0:T(8,128)S(1)} %get-tuple-element.35), channel_id=1, source_target_pairs={{8,0},{16,8},{24,16},{0,24},{9,1},{17,9},{25,17},{1,25},{10,2},{18... | collective-permute-start | bytes 159752 | tf_op jit(solution)/shard_map/ppermute | solution.py:619
  12.8 7.7 %collective-permute-start.6 = (f32[1,128,128]{2,1,0:T(8,128)S(1)}, f32[1,128,128]{2,1,0:T(8,128)S(1)}, u32[]{:S(2)}, u32[]{:S(2)}) collective-permute-start(f32[1,128,128]{2,1,0:T(8,128)S(1)} %get-tuple-element.51), channel_id=1, source_target_pairs={{0,7},{1,6},{2,5},{3,4},{4,3},{5,2},{6,1},{7,0},{8,15},{9,14},{10,... | collective-permute-start | bytes 196616 | tf_op jit(solution)/shard_map/ppermute | solution.py:544
  14.7 7.6 %collective-permute-start.4 = (f32[1,128,128]{2,1,0:T(8,128)S(1)}, f32[1,128,128]{2,1,0:T(8,128)S(1)}, u32[]{:S(2)}, u32[]{:S(2)}) collective-permute-start(f32[1,128,128]{2,1,0:T(8,128)S(1)} %get-tuple-element.47), channel_id=1, source_target_pairs={{0,1},{1,0},{2,3},{3,2},{4,5},{5,4},{6,7},{7,6},{8,9},{9,8},{10,11... | collective-permute-start | bytes 196616 | tf_op jit(solution)/shard_map/ppermute | solution.py:544
  16.1 7.0 %collective-permute-start.5 = (f32[1,128,128]{2,1,0:T(8,128)S(1)}, f32[1,128,128]{2,1,0:T(8,128)S(1)}, u32[]{:S(2)}, u32[]{:S(2)}) collective-permute-start(f32[1,128,128]{2,1,0:T(8,128)S(1)} %get-tuple-element.49), channel_id=1, source_target_pairs={{0,3},{1,2},{2,1},{3,0},{4,7},{5,6},{6,5},{7,4},{8,11},{9,10},{10,... | collective-permute-start | bytes 196616 | tf_op jit(solution)/shard_map/ppermute | solution.py:544
  17.1 7.6 %collective-permute-start.10 = (f32[1,112,128]{2,1,0:T(8,128)S(1)}, f32[1,112,128]{2,1,0:T(8,128)S(1)}, u32[]{:S(2)}, u32[]{:S(2)}) collective-permute-start(f32[1,112,128]{2,1,0:T(8,128)S(1)} %get-tuple-element.57), channel_id=1, source_target_pairs={{0,6},{1,7},{2,4},{3,5},{4,2},{5,3},{6,0},{7,1},{8,14},{9,15},{10,... | collective-permute-start | bytes 172040 | tf_op jit(solution)/shard_map/ppermute | solution.py:544
  18.4 9.1 %collective-permute-start.9 = (f32[1,112,128]{2,1,0:T(8,128)S(1)}, f32[1,112,128]{2,1,0:T(8,128)S(1)}, u32[]{:S(2)}, u32[]{:S(2)}) collective-permute-start(f32[1,112,128]{2,1,0:T(8,128)S(1)} %get-tuple-element.56), channel_id=1, source_target_pairs={{0,5},{1,4},{2,7},{3,6},{4,1},{5,0},{6,3},{7,2},{8,13},{9,12},{10,... | collective-permute-start | bytes 172040 | tf_op jit(solution)/shard_map/ppermute | solution.py:544
  20.4 7.1 %collective-permute-start.7 = (f32[1,112,128]{2,1,0:T(8,128)S(1)}, f32[1,112,128]{2,1,0:T(8,128)S(1)}, u32[]{:S(2)}, u32[]{:S(2)}) collective-permute-start(f32[1,112,128]{2,1,0:T(8,128)S(1)} %get-tuple-element.54), channel_id=1, source_target_pairs={{0,2},{1,3},{2,0},{3,1},{4,6},{5,7},{6,4},{7,5},{8,10},{9,11},{10,... | collective-permute-start | bytes 172040 | tf_op jit(solution)/shard_map/ppermute | solution.py:544
  22.4 5.6 %collective-permute-start.8 = (f32[1,112,128]{2,1,0:T(8,128)S(1)}, f32[1,112,128]{2,1,0:T(8,128)S(1)}, u32[]{:S(2)}, u32[]{:S(2)}) collective-permute-start(f32[1,112,128]{2,1,0:T(8,128)S(1)} %get-tuple-element.55), channel_id=1, source_target_pairs={{0,4},{1,5},{2,6},{3,7},{4,0},{5,1},{6,2},{7,3},{8,12},{9,13},{10,... | collective-permute-start | bytes 172040 | tf_op jit(solution)/shard_map/ppermute | solution.py:544

commit v7 on v6

--- a/solution.py
+++ b/solution.py
@@ -17,7 +17,7 @@
 LANES = 128
 PAD_ROWS = 8
 SENT = (7, 6, 5, 1, 3, 4, 2)
-AFTER = {4: (1,), 2: (7,)}
+AFTER = {4: (1,), 2: (5,)}
 
 
 def gll_tables():

time: 29.2 us -> 29.8 us (1.021)
  starting transfers between devices: 15.1 us -> 16.9 us
  waiting for transfers between devices: 5.43 us -> 4.24 us
    ppermute x7, starting transfers between devices: 9.35 us -> 11.1 us  [exchange(): got[k] = lax.ppermute(block, 'blk', [(j, j ^ k) for j in range(n_peers)])]
    ppermute x7, waiting for transfers between devices: 4.15 us -> 2.96 us  [exchange(): got[k] = lax.ppermute(block, 'blk', [(j, j ^ k) for j in range(n_peers)])]
  transfers between devices with their start and end apart: 11 -> 11, of which waited for: 5 -> 6; matrix products, arithmetic and copies ran while one was open for 0% -> 0% of each run, Pallas kernels for 14% -> 13%
where the time goes in v7:
time: 29.8 us; the launch traced here: 29.6 us
  starting transfers between devices  16.9 us (57%)
  Pallas kernels  7.81 us (26%)
  waiting for transfers between devices  4.24 us (14%)
  between operations  0.68 us (2%)
    ppermute x7, starting transfers between devices, exchange(): got[k] = lax.ppermute(block, 'blk', [(j, j ^ k) for j in range(n_peers)])  11.1 us
    pallas_call x6, Pallas kernels, call(): pl.pallas_call(kernel, out_shape=outs, **more, scratch_shapes=scratch, na...  7.81 us
    ppermute x7, waiting for transfers between devices, exchange(): got[k] = lax.ppermute(block, 'blk', [(j, j ^ k) for j in range(n_peers)])  2.96 us
    ppermute x1, starting transfers between devices, on_device(): lax.ppermute(right, ('face', 'blk'), [(i * n_blk + j, i_up * n_blk + j_up...  2.43 us
    ppermute x1, starting transfers between devices, on_device(): before = lax.ppermute(right, 'blk', blk_up)  1.55 us
    ppermute x1, starting transfers between devices, on_device(): from_low = lax.ppermute(high, 'face', face_up)  1.35 us
    ppermute x1, waiting for transfers between devices, on_device(): before = lax.ppermute(right, 'blk', blk_up)  1.04 us
  transfers between devices with their start and end apart: 11, of which 6 were waited for; matrix products, arithmetic and copies ran while one was open for 0% of the time, Pallas kernels for 13%

profile of v7, /device:TPU:0, one launch (start us, length us, event | category | flops | bytes accessed | tf_op | source)
XLA Modules:
  0.0 29.6 jit_solution(3577694494814030513)
XLA Ops:
  0.6 2.3 %transport.1 = (f32[2304,128]{1,0:T(8,128)S(1)}, f32[32,1152]{1,0:T(8,128)S(1)}, s32[1,1152]{1,0:T(1,128)S(1)}, s32[1,1152]{1,0:T(1,128)S(1)}, f32[1248,128]{1,0...) custom-call(f32[1536,128]{1,0:T(8,128)} %bitcast.5, ...), custom_call_target="tpu_custom_call" | custom-call | tf_op jit(solution)/shard_map/transport/pallas_call | solution.py:550
  2.9 2.4 %collective-permute-start = (f32[104,128]{1,0:T(8,128)S(1)}, f32[104,128]{1,0:T(8,128)S(1)}, u32[]{:S(2)}, u32[]{:S(2)}) collective-permute-start(f32[104,128]{1,0:T(8,128)S(1)} %get-tuple-element.33), channel_id=1, source_target_pairs={{0,9},{1,10},{2,11},{3,12},{4,13},{5,14},{6,15},{7,8},{8,17},{9,18... | collective-permute-start | bytes 159752 | tf_op jit(solution)/shard_map/ppermute | solution.py:614
  5.4 1.6 %collective-permute-start.1 = (f32[104,128]{1,0:T(8,128)S(1)}, f32[104,128]{1,0:T(8,128)S(1)}, u32[]{:S(2)}, u32[]{:S(2)}) collective-permute-start(f32[104,128]{1,0:T(8,128)S(1)} %get-tuple-element.33), channel_id=1, source_target_pairs={{0,1},{1,2},{2,3},{3,4},{4,5},{5,6},{6,7},{7,0},{8,9},{9,10},{10,1... | collective-permute-start | bytes 159752 | tf_op jit(solution)/shard_map/ppermute | solution.py:617
  6.9 1.3 %collective-permute-start.2 = (f32[104,128]{1,0:T(8,128)S(1)}, f32[104,128]{1,0:T(8,128)S(1)}, u32[]{:S(2)}, u32[]{:S(2)}) collective-permute-start(f32[104,128]{1,0:T(8,128)S(1)} %get-tuple-element.34), channel_id=1, source_target_pairs={{0,8},{8,16},{16,24},{24,0},{1,9},{9,17},{17,25},{25,1},{2,10},{10... | collective-permute-start | bytes 159752 | tf_op jit(solution)/shard_map/ppermute | solution.py:618
  8.3 0.4 %collective-permute-start.3 = (f32[104,128]{1,0:T(8,128)S(1)}, f32[104,128]{1,0:T(8,128)S(1)}, u32[]{:S(2)}, u32[]{:S(2)}) collective-permute-start(f32[104,128]{1,0:T(8,128)S(1)} %get-tuple-element.35), channel_id=1, source_target_pairs={{8,0},{16,8},{24,16},{0,24},{9,1},{17,9},{25,17},{1,25},{10,2},{18... | collective-permute-start | bytes 159752 | tf_op jit(solution)/shard_map/ppermute | solution.py:619
  8.7 0.8 %send_order.1 = (bf16[1408,1152]{1,0:T(8,128)(2,1)S(1)}, bf16[256,1152]{1,0:T(8,128)(2,1)S(1)}) custom-call(f32[16,128]{1,0:T(8,128)S(1)} %get-tuple-element.32.refs_0_.den_ref.refs_2_, s32[1,1152]{1,0:T(1,128)S(1)} %get-tuple-element.38.refs_1_), custom_call_target="tpu_custom_call" | custom-call | tf_op jit(solution)/shard_map/send_order/pallas_call | solution.py:550
  9.4 1.5 %inner_columns.1 = (f32[96,1152]{1,0:T(8,128)S(1)}, f32[96,128]{1,0:T(8,128)S(1)}, f32[104,128]{1,0:T(8,128)S(1)}, f32[416,128]{1,0:T(8,128)S(1)}, f32[104,128]{1,0:T(8,128)S(1)}) custom-call(f32[2304,128]{1,0:T(8,128)S(1)} %get-tuple-element.30.iso_ref.refs_0_, f32[1248,128]{1,0:T(8,128)S(1)} %get-tuple-element.31.sums_ref.refs_1_, ...), custom_call_target="tpu_custom_call" | custom-call | tf_op jit(solution)/shard_map/inner_columns/pallas_call | solution.py:550
  11.0 0.2 collective-permute-done.refs_9_.refs_3_
  11.2 1.0 %collective-permute-done.1.refs_10_.refs_4_ = f32[104,128]{1,0:T(8,128)S(1)} collective-permute-done((f32[104,128]{1,0:T(8,128)S(1)}, f32[104,128]{1,0:T(8,128)S(1)}, u32[]{:S(2)}, u32[]{:S(2)}) %collective-permute-start.1) | collective-permute-done | bytes 53280 | tf_op jit(solution)/shard_map/ppermute | solution.py:617
  12.2 0.0 collective-permute-done.2.refs_11_.refs_5_
  12.2 0.0 collective-permute-done.3.refs_12_.refs_6_
  12.2 0.5 %edge_columns.1 = (f32[1,112,128]{2,1,0:T(8,128)S(1)}, f32[1,128,128]{2,1,0:T(8,128)S(1)}, f32[1,112,128]{2,1,0:T(8,128)S(1)}, f32[1,128,128]{2,1,0:T(8,128)S(1)...) custom-call(f32[2304,128]{1,0:T(8,128)S(1)} %get-tuple-element.30.is, ...), custom_call_target="tpu_custom_call" | custom-call | tf_op jit(solution)/shard_map/edge_columns/pallas_call | solution.py:550
  12.8 0.3 collective-permute-start.4
  13.0 2.6 %collective-permute-start.7 = (f32[1,112,128]{2,1,0:T(8,128)S(1)}, f32[1,112,128]{2,1,0:T(8,128)S(1)}, u32[]{:S(2)}, u32[]{:S(2)}) collective-permute-start(f32[1,112,128]{2,1,0:T(8,128)S(1)} %get-tuple-element.53), channel_id=1, source_target_pairs={{0,5},{1,4},{2,7},{3,6},{4,1},{5,0},{6,3},{7,2},{8,13},{9,12},{10,... | collective-permute-start | bytes 172040 | tf_op jit(solution)/shard_map/ppermute | solution.py:544
  15.6 1.1 %collective-permute-start.5 = (f32[1,128,128]{2,1,0:T(8,128)S(1)}, f32[1,128,128]{2,1,0:T(8,128)S(1)}, u32[]{:S(2)}, u32[]{:S(2)}) collective-permute-start(f32[1,128,128]{2,1,0:T(8,128)S(1)} %get-tuple-element.49), channel_id=1, source_target_pairs={{0,3},{1,2},{2,1},{3,0},{4,7},{5,6},{6,5},{7,4},{8,11},{9,10},{10,... | collective-permute-start | bytes 196616 | tf_op jit(solution)/shard_map/ppermute | solution.py:544
  16.8 2.8 %collective-permute-start.6 = (f32[1,128,128]{2,1,0:T(8,128)S(1)}, f32[1,128,128]{2,1,0:T(8,128)S(1)}, u32[]{:S(2)}, u32[]{:S(2)}) collective-permute-start(f32[1,128,128]{2,1,0:T(8,128)S(1)} %get-tuple-element.50), channel_id=1, source_target_pairs={{0,7},{1,6},{2,5},{3,4},{4,3},{5,2},{6,1},{7,0},{8,15},{9,14},{10,... | collective-permute-start | bytes 196616 | tf_op jit(solution)/shard_map/ppermute | solution.py:544
  19.5 1.8 %collective-permute-start.10 = (f32[1,112,128]{2,1,0:T(8,128)S(1)}, f32[1,112,128]{2,1,0:T(8,128)S(1)}, u32[]{:S(2)}, u32[]{:S(2)}) collective-permute-start(f32[1,112,128]{2,1,0:T(8,128)S(1)} %get-tuple-element.57), channel_id=1, source_target_pairs={{0,6},{1,7},{2,4},{3,5},{4,2},{5,3},{6,0},{7,1},{8,14},{9,15},{10,... | collective-permute-start | bytes 172040 | tf_op jit(solution)/shard_map/ppermute | solution.py:544
  21.3 0.0 collective-permute-done.7.refs_5_
  21.3 0.0 collective-permute-start.8
  21.4 0.0 collective-permute-done.4.refs_7_.refs_1_
  21.4 2.6 %collective-permute-start.9 = (f32[1,112,128]{2,1,0:T(8,128)S(1)}, f32[1,112,128]{2,1,0:T(8,128)S(1)}, u32[]{:S(2)}, u32[]{:S(2)}) collective-permute-start(f32[1,112,128]{2,1,0:T(8,128)S(1)} %get-tuple-element.55), channel_id=1, source_target_pairs={{0,4},{1,5},{2,6},{3,7},{4,0},{5,1},{6,2},{7,3},{8,12},{9,13},{10,... | collective-permute-start | bytes 172040 | tf_op jit(solution)/shard_map/ppermute | solution.py:544
  23.9 0.0 collective-permute-done.5.refs_8_.refs_3_
  23.9 0.2 collective-permute-done.6.refs_9_.refs_7_
  24.1 1.7 %advance.1 = f32[1536,128]{1,0:T(8,128)} custom-call(f32[2304,128]{1,0:T(8,128)S(1)} %get-tuple-element.30.iso_ref.refs_0_, f32[1248,128]{1,0:T(8,128)S(1)} %get-tuple-element.31.sums_ref.refs_1_, f32[16,128]{1,0:T(8,128)S(1)} %get-tuple-element.32.refs_0_.den_ref.refs_2_, f32[104,128]{1,0:T(8,128)S(1)} %collective-permute-done.refs_9_.refs_3_, ...), custom_call_target="tpu_custom_call" | custom-call | tf_op jit(solution)/shard_map/advance/pallas_call | solution.py:550
  25.8 0.4 %collective-permute-done.10.refs_6_ = f32[1,112,128]{2,1,0:T(8,128)S(1)} collective-permute-done((f32[1,112,128]{2,1,0:T(8,128)S(1)}, f32[1,112,128]{2,1,0:T(8,128)S(1)}, u32[]{:S(2)}, u32[]{:S(2)}) %collective-permute-start.10) | collective-permute-done | bytes 57376 | tf_op jit(solution)/shard_map/ppermute | solution.py:544
  26.2 0.1 collective-permute-done.8.refs_2_
  26.4 2.2 %collective-permute-done.9.refs_4_ = f32[1,112,128]{2,1,0:T(8,128)S(1)} collective-permute-done((f32[1,112,128]{2,1,0:T(8,128)S(1)}, f32[1,112,128]{2,1,0:T(8,128)S(1)}, u32[]{:S(2)}, u32[]{:S(2)}) %collective-permute-start.9) | collective-permute-done | bytes 57376 | tf_op jit(solution)/shard_map/ppermute | solution.py:544
  28.6 1.0 %assemble.1 = f32[96,1152]{1,0:T(8,128)} custom-call(f32[1,112,128]{2,1,0:T(8,128)S(1)} %get-tuple-element.51.refs_0_, f32[1,128,128]{2,1,0:T(8,128)S(1)} %collective-permute-done.4.refs_7_.refs_1_, f32[1,112,128]{2,1,0:T(8,128)S(1)} %collective-permute-done.8.refs_2_, f32[1,128,128]{2,1,0:T(8,128)S(1)} %collective-permute-done.5.refs_8_.refs_3_, ...), custom_call_target="tpu_custom_call" | custom-call | tf_op jit(solution)/shard_map/assemble/pallas_call | solution.py:550
Async XLA Ops:
  2.9 8.2 %collective-permute-start = (f32[104,128]{1,0:T(8,128)S(1)}, f32[104,128]{1,0:T(8,128)S(1)}, u32[]{:S(2)}, u32[]{:S(2)}) collective-permute-start(f32[104,128]{1,0:T(8,128)S(1)} %get-tuple-element.33), channel_id=1, source_target_pairs={{0,9},{1,10},{2,11},{3,12},{4,13},{5,14},{6,15},{7,8},{8,17},{9,18... | collective-permute-start | bytes 159752 | tf_op jit(solution)/shard_map/ppermute | solution.py:614
  5.4 6.9 %collective-permute-start.1 = (f32[104,128]{1,0:T(8,128)S(1)}, f32[104,128]{1,0:T(8,128)S(1)}, u32[]{:S(2)}, u32[]{:S(2)}) collective-permute-start(f32[104,128]{1,0:T(8,128)S(1)} %get-tuple-element.33), channel_id=1, source_target_pairs={{0,1},{1,2},{2,3},{3,4},{4,5},{5,6},{6,7},{7,0},{8,9},{9,10},{10,1... | collective-permute-start | bytes 159752 | tf_op jit(solution)/shard_map/ppermute | solution.py:617
  6.9 5.3 %collective-permute-start.2 = (f32[104,128]{1,0:T(8,128)S(1)}, f32[104,128]{1,0:T(8,128)S(1)}, u32[]{:S(2)}, u32[]{:S(2)}) collective-permute-start(f32[104,128]{1,0:T(8,128)S(1)} %get-tuple-element.34), channel_id=1, source_target_pairs={{0,8},{8,16},{16,24},{24,0},{1,9},{9,17},{17,25},{25,1},{2,10},{10... | collective-permute-start | bytes 159752 | tf_op jit(solution)/shard_map/ppermute | solution.py:618
  8.3 4.0 %collective-permute-start.3 = (f32[104,128]{1,0:T(8,128)S(1)}, f32[104,128]{1,0:T(8,128)S(1)}, u32[]{:S(2)}, u32[]{:S(2)}) collective-permute-start(f32[104,128]{1,0:T(8,128)S(1)} %get-tuple-element.35), channel_id=1, source_target_pairs={{8,0},{16,8},{24,16},{0,24},{9,1},{17,9},{25,17},{1,25},{10,2},{18... | collective-permute-start | bytes 159752 | tf_op jit(solution)/shard_map/ppermute | solution.py:619
  12.8 8.6 %collective-permute-start.4 = (f32[1,128,128]{2,1,0:T(8,128)S(1)}, f32[1,128,128]{2,1,0:T(8,128)S(1)}, u32[]{:S(2)}, u32[]{:S(2)}) collective-permute-start(f32[1,128,128]{2,1,0:T(8,128)S(1)} %get-tuple-element.47), channel_id=1, source_target_pairs={{0,1},{1,0},{2,3},{3,2},{4,5},{5,4},{6,7},{7,6},{8,9},{9,8},{10,11... | collective-permute-start | bytes 196616 | tf_op jit(solution)/shard_map/ppermute | solution.py:544
  13.0 8.3 %collective-permute-start.7 = (f32[1,112,128]{2,1,0:T(8,128)S(1)}, f32[1,112,128]{2,1,0:T(8,128)S(1)}, u32[]{:S(2)}, u32[]{:S(2)}) collective-permute-start(f32[1,112,128]{2,1,0:T(8,128)S(1)} %get-tuple-element.53), channel_id=1, source_target_pairs={{0,5},{1,4},{2,7},{3,6},{4,1},{5,0},{6,3},{7,2},{8,13},{9,12},{10,... | collective-permute-start | bytes 172040 | tf_op jit(solution)/shard_map/ppermute | solution.py:544
  15.6 8.3 %collective-permute-start.5 = (f32[1,128,128]{2,1,0:T(8,128)S(1)}, f32[1,128,128]{2,1,0:T(8,128)S(1)}, u32[]{:S(2)}, u32[]{:S(2)}) collective-permute-start(f32[1,128,128]{2,1,0:T(8,128)S(1)} %get-tuple-element.49), channel_id=1, source_target_pairs={{0,3},{1,2},{2,1},{3,0},{4,7},{5,6},{6,5},{7,4},{8,11},{9,10},{10,... | collective-permute-start | bytes 196616 | tf_op jit(solution)/shard_map/ppermute | solution.py:544
  16.8 7.4 %collective-permute-start.6 = (f32[1,128,128]{2,1,0:T(8,128)S(1)}, f32[1,128,128]{2,1,0:T(8,128)S(1)}, u32[]{:S(2)}, u32[]{:S(2)}) collective-permute-start(f32[1,128,128]{2,1,0:T(8,128)S(1)} %get-tuple-element.50), channel_id=1, source_target_pairs={{0,7},{1,6},{2,5},{3,4},{4,3},{5,2},{6,1},{7,0},{8,15},{9,14},{10,... | collective-permute-start | bytes 196616 | tf_op jit(solution)/shard_map/ppermute | solution.py:544
  19.5 6.7 %collective-permute-start.10 = (f32[1,112,128]{2,1,0:T(8,128)S(1)}, f32[1,112,128]{2,1,0:T(8,128)S(1)}, u32[]{:S(2)}, u32[]{:S(2)}) collective-permute-start(f32[1,112,128]{2,1,0:T(8,128)S(1)} %get-tuple-element.57), channel_id=1, source_target_pairs={{0,6},{1,7},{2,4},{3,5},{4,2},{5,3},{6,0},{7,1},{8,14},{9,15},{10,... | collective-permute-start | bytes 172040 | tf_op jit(solution)/shard_map/ppermute | solution.py:544
  21.3 5.0 %collective-permute-start.8 = (f32[1,112,128]{2,1,0:T(8,128)S(1)}, f32[1,112,128]{2,1,0:T(8,128)S(1)}, u32[]{:S(2)}, u32[]{:S(2)}) collective-permute-start(f32[1,112,128]{2,1,0:T(8,128)S(1)} %get-tuple-element.54), channel_id=1, source_target_pairs={{0,2},{1,3},{2,0},{3,1},{4,6},{5,7},{6,4},{7,5},{8,10},{9,11},{10,... | collective-permute-start | bytes 172040 | tf_op jit(solution)/shard_map/ppermute | solution.py:544
  21.4 7.2 %collective-permute-start.9 = (f32[1,112,128]{2,1,0:T(8,128)S(1)}, f32[1,112,128]{2,1,0:T(8,128)S(1)}, u32[]{:S(2)}, u32[]{:S(2)}) collective-permute-start(f32[1,112,128]{2,1,0:T(8,128)S(1)} %get-tuple-element.55), channel_id=1, source_target_pairs={{0,4},{1,5},{2,6},{3,7},{4,0},{5,1},{6,2},{7,3},{8,12},{9,13},{10,... | collective-permute-start | bytes 172040 | tf_op jit(solution)/shard_map/ppermute | solution.py:544
